TPU v7x, 32 devices: a whole 2x2x4 slice. The times are simulated.
32 devices in a mesh: grp: 4 (over x, core), seq: 8 (over z, y).
Axes of the slice: x: 2, y: 2, z: 4, core: 2. Of those that a mesh axis runs over, the one named last changes fastest.
Arguments:
- hidden: bfloat16 [4096, 1536], P(('grp', 'seq')), may hold values from -6 to 6
- latent_shape: int32 [4, 3, 2], P('grp'), may hold values from 2 to 64, as said below
- cond_r: float32 [12, 64], P('grp'), may hold values from -6 to 6
- clip: bfloat16 [12, 77, 1280], P('grp'), may hold values from -6 to 6
- cotangent: bfloat16 [4096, 1536], P(('grp', 'seq')), may hold values from -6 to 6
- conv_weight: bfloat16 [9, 1536], P(None, 'seq'), may hold values from -2 to 2
- conv_bias: bfloat16 [1536], P('seq'), may hold values from -3 to 3
- fc1_weight: bfloat16 [1536, 6144], P(None, 'seq'), may hold values from -0.15625 to 0.15625
- fc1_bias: bfloat16 [6144], P('seq'), may hold values from -2 to 2
- grn_gamma: bfloat16 [6144], P('seq'), may hold values from -3 to 3
- grn_beta: bfloat16 [6144], P('seq'), may hold values from -2 to 2
- fc2_weight: bfloat16 [6144, 1536], P(None, 'seq'), may hold values from -0.078125 to 0.078125
- fc2_bias: bfloat16 [1536], P('seq'), may hold values from -2 to 2
- time_weight: bfloat16 [64, 3072], P(None, 'seq'), may hold values from -0.25 to 0.25
- time_bias: bfloat16 [3072], P('seq'), may hold values from -1.5 to 1.5
- map_weight: bfloat16 [1280, 1536], P(None, 'seq'), may hold values from -0.15625 to 0.15625
- map_bias: bfloat16 [1536], P('seq'), may hold values from -2 to 2
- query_weight: bfloat16 [1536, 1536], P(None, 'seq'), may hold values from -0.15625 to 0.15625
- query_bias: bfloat16 [1536], P('seq'), may hold values from -2 to 2
- key_weight: bfloat16 [1536, 1536], P(None, 'seq'), may hold values from -0.15625 to 0.15625
- value_weight: bfloat16 [1536, 1536], P(None, 'seq'), may hold values from -0.15625 to 0.15625
- value_bias: bfloat16 [1536], P('seq'), may hold values from -2 to 2
- out_weight: bfloat16 [1536, 1536], P(None, 'seq'), may hold values from -3 to 3
- out_bias: bfloat16 [1536], P('seq'), may hold values from -2 to 2
Outputs:
- activations: bfloat16 [4096, 1536], P(('grp', 'seq'))
- input_grad: float32 [4096, 1536], P(('grp', 'seq'))
- conv_weight_grad: float32 [9, 1536], P(None, 'seq')
- conv_bias_grad: float32 [1536], P('seq')
- fc1_weight_grad: float32 [1536, 6144], P(None, 'seq')
- fc1_bias_grad: float32 [6144], P('seq')
- grn_gamma_grad: float32 [6144], P('seq')
- grn_beta_grad: float32 [6144], P('seq')
- fc2_weight_grad: float32 [6144, 1536], P(None, 'seq')
- fc2_bias_grad: float32 [1536], P('seq')
- time_weight_grad: float32 [64, 3072], P(None, 'seq')
- time_bias_grad: float32 [3072], P('seq')
- map_weight_grad: float32 [1280, 1536], P(None, 'seq')
- map_bias_grad: float32 [1536], P('seq')
- query_weight_grad: float32 [1536, 1536], P(None, 'seq')
- query_bias_grad: float32 [1536], P('seq')
- key_weight_grad: float32 [1536, 1536], P(None, 'seq')
- value_weight_grad: float32 [1536, 1536], P(None, 'seq')
- value_bias_grad: float32 [1536], P('seq')
- out_weight_grad: float32 [1536, 1536], P(None, 'seq')
- out_bias_grad: float32 [1536], P('seq')
Inputs may be any that keep to these rules, and one draw needn't show every extreme that they name: `latent_shape`: each group packs its three latents without gaps into its 1024 pixels, all 64 pixels wide; the middle latent has 10 rows, the first and last latents share the remaining rows, each with 2 rows or more; in some group the first latent has exactly that many.
All inputs are finite; a program needn't handle non-finite values.
Results may differ from a plain program's by a relative error of at most 0.018.
Values may be sent and summed in bfloat16 or wider, within the bound.
A program may use at most 384 MiB of HBM per device.

v0:
```python
import math

import jax
import jax.numpy as jnp
from jax import lax
from jax.sharding import PartitionSpec as P

C = 1536
HEADS = 24
HEAD_DIM = 64
FF = 6144
CLIP = 1280
NCTX = 77
NLAT = 3
WMAX = 64


EPS_NORM = 1e-06
SCORE_SCALE = 0.125
MASKED = -1e30
HIGHEST_PRECISION = lax.Precision.HIGHEST


def padded_2(block, sides, width):
    for axis, dim in sides:
        count = lax.axis_size(axis)
        forward = [(i, i + 1) for i in range(count - 1)]
        backward = [(target, source) for source, target in forward]
        low = lax.ppermute(
            lax.slice_in_dim(block, block.shape[dim] - width, None, axis=dim), axis, forward
        )
        high = lax.ppermute(lax.slice_in_dim(block, 0, width, axis=dim), axis, backward)
        block = jnp.concatenate([low, block, high], axis=dim)
    return block


def latent_grid(positions, shape_row):
    latent_count = shape_row.shape[0]
    heights = shape_row[:, 0]
    latent_width = shape_row[0, 1]
    pixel_counts = heights * latent_width
    end_points = jnp.cumsum(pixel_counts)
    start_points = end_points - pixel_counts
    segment = jnp.sum((positions[:, None] >= end_points[None, :]).astype(jnp.int32), axis=1)
    segment = jnp.minimum(segment, latent_count - 1)
    picked = (segment[:, None] == jnp.arange(latent_count, dtype=jnp.int32)[None, :]).astype(
        jnp.int32
    )
    first_pixel = jnp.sum(picked * start_points[None, :], axis=1)
    height = jnp.sum(picked * heights[None, :], axis=1)
    offset_in = positions - first_pixel
    row_index = jnp.floor_divide(offset_in, latent_width)
    column = offset_in - row_index * latent_width
    return (segment, row_index, column, height, latent_width)


def valid_tap(row_index, column, height, latent_width, down_step, side_step):
    upright = (row_index + down_step >= 0) & (row_index + down_step < height)
    across = (column + side_step >= 0) & (column + side_step < latent_width)
    return (upright & across).astype(jnp.float32)


def layer_stats(values_in):
    average = jnp.mean(values_in, axis=-1, keepdims=True)
    centred = values_in - average
    variance = jnp.mean(centred * centred, axis=-1, keepdims=True)
    inverse = lax.rsqrt(variance + EPS_NORM)
    return (centred * inverse, inverse)


def layer_back(gradient, normed, inverse):
    mean_grad = jnp.mean(gradient, axis=-1, keepdims=True)
    mean_mixed = jnp.mean(gradient * normed, axis=-1, keepdims=True)
    return inverse * (gradient - mean_grad - normed * mean_mixed)


def against(values_low, weight_low):
    return lax.dot_general(
        values_low, weight_low, (((1,), (1,)), ((), ())), preferred_element_type=jnp.float32
    )


def against_exact(values_in, weight_in):
    return lax.dot_general(
        values_in,
        weight_in,
        (((1,), (1,)), ((), ())),
        precision=HIGHEST_PRECISION,
        preferred_element_type=jnp.float32,
    )


def outer_sum(left_low, right_low):
    return lax.dot_general(
        left_low, right_low, (((0,), (0,)), ((), ())), preferred_element_type=jnp.float32
    )


def column_sum(picked, values_in):
    return lax.dot_general(
        picked,
        values_in,
        (((0,), (0,)), ((), ())),
        precision=HIGHEST_PRECISION,
        preferred_element_type=jnp.float32,
    )


def exact_gelu(values_in):
    return jax.nn.gelu(values_in, approximate=False)


def block_size(row_count, shard_rows):
    shard_total = row_count // shard_rows
    return math.gcd(shard_total, max(1, 1024 // shard_rows)) * shard_rows


def on_device(
    hidden,
    latent_shape,
    cond_r,
    clip,
    cotangent,
    conv_weight,
    conv_bias,
    fc1_weight,
    fc1_bias,
    grn_gamma,
    grn_beta,
    fc2_weight,
    fc2_bias,
    time_weight,
    time_bias,
    map_weight,
    map_bias,
    query_weight,
    query_bias,
    key_weight,
    value_weight,
    value_bias,
    out_weight,
    out_bias,
):
    tok_rows = hidden.shape[0]
    positions = lax.axis_index("seq") * tok_rows + jnp.arange(tok_rows, dtype=jnp.int32)
    shape_row = latent_shape[0]
    segment, row_index, column, height, latent_width = latent_grid(positions, shape_row)
    margin = WMAX + 1
    gathered = (
        lax.all_gather(conv_weight, "seq", axis=1, tiled=True),
        lax.all_gather(conv_bias, "seq", axis=0, tiled=True),
        lax.all_gather(fc1_weight, "seq", axis=1, tiled=True),
        lax.all_gather(fc1_bias, "seq", axis=0, tiled=True),
        lax.all_gather(grn_gamma, "seq", axis=0, tiled=True),
        lax.all_gather(grn_beta, "seq", axis=0, tiled=True),
        lax.all_gather(fc2_weight, "seq", axis=1, tiled=True),
        lax.all_gather(fc2_bias, "seq", axis=0, tiled=True),
        lax.all_gather(time_weight, "seq", axis=1, tiled=True),
        lax.all_gather(time_bias, "seq", axis=0, tiled=True),
        lax.all_gather(map_weight, "seq", axis=1, tiled=True),
        lax.all_gather(map_bias, "seq", axis=0, tiled=True),
        lax.all_gather(query_weight, "seq", axis=1, tiled=True),
        lax.all_gather(query_bias, "seq", axis=0, tiled=True),
        lax.all_gather(key_weight, "seq", axis=1, tiled=True),
        lax.all_gather(value_weight, "seq", axis=1, tiled=True),
        lax.all_gather(value_bias, "seq", axis=0, tiled=True),
        lax.all_gather(out_weight, "seq", axis=1, tiled=True),
        lax.all_gather(out_bias, "seq", axis=0, tiled=True),
    )
    (
        kernel_full,
        kernel_bias,
        expand_full,
        expand_bias,
        gamma_full,
        beta_full,
        shrink_full,
        shrink_bias,
        time_full,
        time_bias_full,
        mapper_full,
        mapper_bias,
        query_full,
        query_bias_full,
        key_full,
        value_full,
        value_bias_full,
        output_full,
        output_bias_full,
    ) = gathered
    padded = padded_2(hidden, (("seq", 0),), margin)
    conv_out = jnp.broadcast_to(kernel_bias.astype(jnp.float32)[None, :], (tok_rows, C))
    tap_list = []
    for down_step in (-1, 0, 1):
        for side_step in (-1, 0, 1):
            tap_number = 3 * (down_step + 1) + (side_step + 1)
            valid = valid_tap(row_index, column, height, latent_width, down_step, side_step)
            offset_rows = down_step * latent_width + side_step
            nearby = lax.dynamic_slice_in_dim(padded, margin + offset_rows, tok_rows, 0).astype(
                jnp.float32
            )
            conv_out = (
                conv_out
                + kernel_full[tap_number].astype(jnp.float32)[None, :] * nearby * valid[:, None]
            )
            tap_list.append((tap_number, down_step, side_step, offset_rows, valid))
    normed_one, inverse_one = layer_stats(conv_out)
    normed_low = normed_one.astype(jnp.bfloat16)
    pre_act = jnp.dot(
        normed_low, expand_full, preferred_element_type=jnp.float32
    ) + expand_bias.astype(jnp.float32)
    activated, gelu_pull = jax.vjp(exact_gelu, pre_act)
    picked = (segment[:, None] == jnp.arange(NLAT, dtype=jnp.int32)[None, :]).astype(jnp.float32)
    energy = lax.psum(column_sum(picked, activated * activated), "seq")
    root = jnp.sqrt(energy + 1.0)
    denom = jnp.mean(root, axis=-1, keepdims=True) + EPS_NORM
    ratio = root / denom
    ratio_rows = jnp.dot(picked, ratio, precision=HIGHEST_PRECISION)
    gamma_value = gamma_full.astype(jnp.float32)
    response = gamma_value * (activated * ratio_rows) + beta_full.astype(jnp.float32) + activated
    response_low = response.astype(jnp.bfloat16)
    branch = jnp.dot(
        response_low, shrink_full, preferred_element_type=jnp.float32
    ) + shrink_bias.astype(jnp.float32)
    first_sum = hidden.astype(jnp.float32) + branch
    modulation = jnp.dot(
        cond_r, time_full.astype(jnp.float32), precision=HIGHEST_PRECISION
    ) + time_bias_full.astype(jnp.float32)
    mod_rows = jnp.dot(picked, modulation, precision=HIGHEST_PRECISION)
    scale_rows = 1.0 + mod_rows[:, :C]
    second_sum = first_sum * scale_rows + mod_rows[:, C:]
    normed_two, inverse_two = layer_stats(second_sum)
    attn_in = normed_two.astype(jnp.bfloat16)
    context_in = jax.nn.silu(clip.reshape(NLAT * NCTX, CLIP).astype(jnp.float32)).astype(
        jnp.bfloat16
    )
    context = (
        jnp.dot(context_in, mapper_full, preferred_element_type=jnp.float32)
        + mapper_bias.astype(jnp.float32)
    ).astype(jnp.bfloat16)
    queries = (
        jnp.dot(attn_in, query_full, preferred_element_type=jnp.float32)
        + query_bias_full.astype(jnp.float32)
    ).astype(jnp.bfloat16)
    keys_low = jnp.dot(attn_in, key_full, preferred_element_type=jnp.float32).astype(jnp.bfloat16)
    values_low = (
        jnp.dot(attn_in, value_full, preferred_element_type=jnp.float32)
        + value_bias_full.astype(jnp.float32)
    ).astype(jnp.bfloat16)
    context_keys = jnp.dot(context, key_full, preferred_element_type=jnp.float32).astype(
        jnp.bfloat16
    )
    context_values = (
        jnp.dot(context, value_full, preferred_element_type=jnp.float32)
        + value_bias_full.astype(jnp.float32)
    ).astype(jnp.bfloat16)
    query_heads = queries.reshape(tok_rows, HEADS, HEAD_DIM)
    key_heads = keys_low.reshape(tok_rows, HEADS, HEAD_DIM)
    value_heads = values_low.reshape(tok_rows, HEADS, HEAD_DIM)
    ctx_key_heads = context_keys.reshape(NLAT * NCTX, HEADS, HEAD_DIM)
    ctx_value_heads = context_values.reshape(NLAT * NCTX, HEADS, HEAD_DIM)
    context_segment = jnp.arange(NLAT * NCTX, dtype=jnp.int32) // NCTX
    ctx_admit = segment[:, None] == context_segment[None, :]

    def segments_at(first_row, length):
        return latent_grid(first_row + jnp.arange(length, dtype=jnp.int32), shape_row)[0]

    ctx_scores = (
        jnp.einsum("qhd,khd->hqk", query_heads, ctx_key_heads, preferred_element_type=jnp.float32)
        * SCORE_SCALE
    )
    ctx_scores = jnp.where(ctx_admit[None], ctx_scores, MASKED)
    start_max = jnp.max(ctx_scores, axis=-1)
    ctx_expo = jnp.exp(ctx_scores - start_max[..., None])
    start_total = jnp.sum(ctx_expo, axis=-1)
    start_accum = jnp.einsum(
        "hqk,khd->qhd",
        ctx_expo.astype(jnp.bfloat16),
        ctx_value_heads,
        preferred_element_type=jnp.float32,
    )
    key_part = lax.all_gather(keys_low, "seq", axis=0, tiled=True)
    value_part = lax.all_gather(values_low, "seq", axis=0, tiled=True)
    block_rows = block_size(key_part.shape[0], tok_rows)
    block_count = key_part.shape[0] // block_rows
    key_stack = key_part.reshape(block_count, block_rows, HEADS, HEAD_DIM)
    value_stack = value_part.reshape(block_count, block_rows, HEADS, HEAD_DIM)

    def attend_visit(state_now, element):
        key_block, value_block, block_index = element
        key_segment = segments_at(block_index * block_rows, block_rows)
        admitted = segment[:, None] == key_segment[None, :]
        scores = (
            jnp.einsum("qhd,khd->hqk", query_heads, key_block, preferred_element_type=jnp.float32)
            * SCORE_SCALE
        )
        scores = jnp.where(admitted[None], scores, MASKED)
        old_max, old_total, old_accum = state_now
        new_max = jnp.maximum(old_max, jnp.max(scores, axis=-1))
        factor = jnp.exp(old_max - new_max)
        expo_block = jnp.exp(scores - new_max[..., None])
        new_total = old_total * factor + jnp.sum(expo_block, axis=-1)
        new_accum = old_accum * factor.T[:, :, None] + jnp.einsum(
            "hqk,khd->qhd",
            expo_block.astype(jnp.bfloat16),
            value_block,
            preferred_element_type=jnp.float32,
        )
        return ((new_max, new_total, new_accum), None)

    state_end, ignored = lax.scan(
        attend_visit,
        (start_max, start_total, start_accum),
        (key_stack, value_stack, jnp.arange(block_count, dtype=jnp.int32)),
    )
    run_max, run_total, accum = state_end
    mixed = accum / run_total.T[:, :, None]
    log_total = run_max + jnp.log(run_total)
    mixed_low = mixed.reshape(tok_rows, C).astype(jnp.bfloat16)
    activations = (
        second_sum
        + jnp.dot(mixed_low, output_full, preferred_element_type=jnp.float32)
        + output_bias_full.astype(jnp.float32)
    ).astype(jnp.bfloat16)
    cot_value = cotangent.astype(jnp.float32)
    grad_out_w = outer_sum(mixed_low, cotangent)
    grad_out_b = jnp.sum(cot_value, axis=0)
    d_mixed_low = against(cotangent, output_full).astype(jnp.bfloat16)
    dmix_heads = d_mixed_low.reshape(tok_rows, HEADS, HEAD_DIM)
    delta = jnp.sum(dmix_heads.astype(jnp.float32) * mixed, axis=-1).T
    ctx_probs = jnp.exp(ctx_scores - log_total[..., None])
    ctx_dprob = jnp.einsum(
        "qhd,khd->hqk", dmix_heads, ctx_value_heads, preferred_element_type=jnp.float32
    )
    ctx_dscore = (ctx_probs * (ctx_dprob - delta[..., None])).astype(jnp.bfloat16)
    dquery_start = (
        jnp.einsum("hqk,khd->qhd", ctx_dscore, ctx_key_heads, preferred_element_type=jnp.float32)
        * SCORE_SCALE
    )
    ctx_dkey_part = (
        jnp.einsum("hqk,qhd->khd", ctx_dscore, query_heads, preferred_element_type=jnp.float32)
        * SCORE_SCALE
    )
    ctx_dvalue_part = jnp.einsum(
        "hqk,qhd->khd",
        ctx_probs.astype(jnp.bfloat16),
        dmix_heads,
        preferred_element_type=jnp.float32,
    )
    key_part = lax.all_gather(keys_low, "seq", axis=0, tiled=True)
    value_part = lax.all_gather(values_low, "seq", axis=0, tiled=True)
    query_block_rows = block_size(key_part.shape[0], tok_rows)
    block_count = key_part.shape[0] // query_block_rows
    key_stack = key_part.reshape(block_count, query_block_rows, HEADS, HEAD_DIM)
    value_stack = value_part.reshape(block_count, query_block_rows, HEADS, HEAD_DIM)

    def query_visit(state_now, element):
        key_block, value_block, block_index = element
        key_segment = segments_at(block_index * query_block_rows, query_block_rows)
        admitted = segment[:, None] == key_segment[None, :]
        scores = (
            jnp.einsum("qhd,khd->hqk", query_heads, key_block, preferred_element_type=jnp.float32)
            * SCORE_SCALE
        )
        scores = jnp.where(admitted[None], scores, MASKED)
        probs = jnp.exp(scores - log_total[..., None])
        dprob = jnp.einsum(
            "qhd,khd->hqk", dmix_heads, value_block, preferred_element_type=jnp.float32
        )
        dscore = (probs * (dprob - delta[..., None])).astype(jnp.bfloat16)
        added = (
            jnp.einsum("hqk,khd->qhd", dscore, key_block, preferred_element_type=jnp.float32)
            * SCORE_SCALE
        )
        return (state_now + added, None)

    state_end, ignored = lax.scan(
        query_visit,
        dquery_start,
        (key_stack, value_stack, jnp.arange(block_count, dtype=jnp.int32)),
    )
    dquery = state_end
    lse_all, delta_all = (
        lax.all_gather(log_total.T, "seq", axis=0, tiled=True),
        lax.all_gather(delta.T, "seq", axis=0, tiled=True),
    )
    zero_heads = jnp.zeros((tok_rows, HEADS, HEAD_DIM), jnp.float32)
    query_part = lax.all_gather(queries, "seq", axis=0, tiled=True)
    dmix_part = lax.all_gather(d_mixed_low, "seq", axis=0, tiled=True)
    row_count = query_part.shape[0]
    key_block_rows = block_size(row_count, tok_rows)
    block_count = row_count // key_block_rows
    query_stack = query_part.reshape(block_count, key_block_rows, HEADS, HEAD_DIM)
    dmix_stack = dmix_part.reshape(block_count, key_block_rows, HEADS, HEAD_DIM)
    lse_stack = lse_all.reshape(block_count, key_block_rows, HEADS)
    delta_stack = delta_all.reshape(block_count, key_block_rows, HEADS)

    def key_visit(state_now, element):
        query_block, dmix_block, lse_block, delta_block, block_index = element
        query_segment = segments_at(block_index * key_block_rows, key_block_rows)
        admitted = segment[:, None] == query_segment[None, :]
        scores = (
            jnp.einsum("khd,qhd->hkq", key_heads, query_block, preferred_element_type=jnp.float32)
            * SCORE_SCALE
        )
        scores = jnp.where(admitted[None], scores, MASKED)
        probs = jnp.exp(scores - lse_block.T[:, None, :])
        dkey_now, dvalue_now = state_now
        dvalue_now = dvalue_now + jnp.einsum(
            "hkq,qhd->khd",
            probs.astype(jnp.bfloat16),
            dmix_block,
            preferred_element_type=jnp.float32,
        )
        dprob = jnp.einsum(
            "khd,qhd->hkq", value_heads, dmix_block, preferred_element_type=jnp.float32
        )
        dscore = (probs * (dprob - delta_block.T[:, None, :])).astype(jnp.bfloat16)
        dkey_now = (
            dkey_now
            + jnp.einsum("hkq,qhd->khd", dscore, query_block, preferred_element_type=jnp.float32)
            * SCORE_SCALE
        )
        return ((dkey_now, dvalue_now), None)

    state_end, ignored = lax.scan(
        key_visit,
        (zero_heads, zero_heads),
        (query_stack, dmix_stack, lse_stack, delta_stack, jnp.arange(block_count, dtype=jnp.int32)),
    )
    dkey, dvalue = state_end
    dquery_low = dquery.reshape(tok_rows, C).astype(jnp.bfloat16)
    dkey_low = dkey.reshape(tok_rows, C).astype(jnp.bfloat16)
    dvalue_low = dvalue.reshape(tok_rows, C).astype(jnp.bfloat16)
    ctx_dkey_flat = ctx_dkey_part.reshape(NLAT * NCTX, C)
    ctx_dvalue_flat = ctx_dvalue_part.reshape(NLAT * NCTX, C)
    context_value = context.astype(jnp.float32)
    d_attn_in = (
        against(dquery_low, query_full)
        + against(dkey_low, key_full)
        + against(dvalue_low, value_full)
    )
    grad_query_w = outer_sum(attn_in, dquery_low)
    grad_query_b = jnp.sum(dquery_low.astype(jnp.float32), axis=0)
    grad_key_w = outer_sum(attn_in, dkey_low) + column_sum(context_value, ctx_dkey_flat)
    grad_value_w = outer_sum(attn_in, dvalue_low) + column_sum(context_value, ctx_dvalue_flat)
    grad_value_b = jnp.sum(dvalue_low.astype(jnp.float32), axis=0) + jnp.sum(
        ctx_dvalue_flat, axis=0
    )
    d_context = against_exact(ctx_dkey_flat, key_full.astype(jnp.float32)) + against_exact(
        ctx_dvalue_flat, value_full.astype(jnp.float32)
    )
    grad_map_w = column_sum(context_in.astype(jnp.float32), d_context)
    grad_map_b = jnp.sum(d_context, axis=0)
    d_second = cot_value + layer_back(d_attn_in, normed_two, inverse_two)
    d_first = d_second * scale_rows
    d_mod_rows = jnp.concatenate([d_second * first_sum, d_second], axis=1)
    d_modulation = column_sum(picked, d_mod_rows)
    grad_time_w = lax.dot_general(
        cond_r,
        d_modulation,
        (((0,), (0,)), ((), ())),
        precision=HIGHEST_PRECISION,
        preferred_element_type=jnp.float32,
    )
    grad_time_b = jnp.sum(d_modulation, axis=0)
    d_branch_low = d_first.astype(jnp.bfloat16)
    grad_shrink_w = outer_sum(response_low, d_branch_low)
    grad_shrink_b = jnp.sum(d_branch_low.astype(jnp.float32), axis=0)
    d_response = against(d_branch_low, shrink_full)
    grad_gamma = jnp.sum(d_response * activated * ratio_rows, axis=0)
    grad_beta = jnp.sum(d_response, axis=0)
    d_ratio = lax.psum(column_sum(picked, d_response * gamma_value * activated), "seq")
    d_root = d_ratio / denom - jnp.sum(d_ratio * root, axis=-1, keepdims=True) / (
        FF * denom * denom
    )
    d_act = d_response * (gamma_value * ratio_rows + 1.0) + activated * jnp.dot(
        picked, d_root / root, precision=HIGHEST_PRECISION
    )
    d_pre_low = gelu_pull(d_act)[0].astype(jnp.bfloat16)
    grad_expand_w = outer_sum(normed_low, d_pre_low)
    grad_expand_b = jnp.sum(d_pre_low.astype(jnp.float32), axis=0)
    d_normed = against(d_pre_low, expand_full)
    d_conv_low = layer_back(d_normed, normed_one, inverse_one).astype(jnp.bfloat16)
    d_conv = d_conv_low.astype(jnp.float32)
    grad_kernel_b = jnp.sum(d_conv, axis=0)
    d_padded = padded_2(d_conv_low, (("seq", 0),), margin)
    kernel_rows = []
    input_grad = d_first
    for tap_number, down_step, side_step, offset_rows, valid in tap_list:
        nearby = lax.dynamic_slice_in_dim(padded, margin + offset_rows, tok_rows, 0).astype(
            jnp.float32
        )
        kernel_rows.append(jnp.sum(d_conv * nearby * valid[:, None], axis=0))
        source = positions - offset_rows
        src_segment, src_row, src_column, src_height, src_width = latent_grid(source, shape_row)
        src_valid = valid_tap(src_row, src_column, src_height, src_width, down_step, side_step)
        behind = lax.dynamic_slice_in_dim(d_padded, margin - offset_rows, tok_rows, 0).astype(
            jnp.float32
        )
        input_grad = (
            input_grad
            + kernel_full[tap_number].astype(jnp.float32)[None, :] * behind * src_valid[:, None]
        )
    grad_kernel_w = jnp.stack(kernel_rows, axis=0)
    gradients = (
        grad_kernel_w,
        grad_kernel_b,
        grad_expand_w,
        grad_expand_b,
        grad_gamma,
        grad_beta,
        grad_shrink_w,
        grad_shrink_b,
        grad_time_w,
        grad_time_b,
        grad_map_w,
        grad_map_b,
        grad_query_w,
        grad_query_b,
        grad_key_w,
        grad_value_w,
        grad_value_b,
        grad_out_w,
        grad_out_b,
    )
    shares = (
        lax.psum_scatter(gradients[0], "seq", scatter_dimension=1, tiled=True),
        lax.psum_scatter(gradients[1], "seq", scatter_dimension=0, tiled=True),
        lax.psum_scatter(gradients[2], "seq", scatter_dimension=1, tiled=True),
        lax.psum_scatter(gradients[3], "seq", scatter_dimension=0, tiled=True),
        lax.psum_scatter(gradients[4], "seq", scatter_dimension=0, tiled=True),
        lax.psum_scatter(gradients[5], "seq", scatter_dimension=0, tiled=True),
        lax.psum_scatter(gradients[6], "seq", scatter_dimension=1, tiled=True),
        lax.psum_scatter(gradients[7], "seq", scatter_dimension=0, tiled=True),
        lax.psum_scatter(gradients[8], "seq", scatter_dimension=1, tiled=True),
        lax.psum_scatter(gradients[9], "seq", scatter_dimension=0, tiled=True),
        lax.psum_scatter(gradients[10], "seq", scatter_dimension=1, tiled=True),
        lax.psum_scatter(gradients[11], "seq", scatter_dimension=0, tiled=True),
        lax.psum_scatter(gradients[12], "seq", scatter_dimension=1, tiled=True),
        lax.psum_scatter(gradients[13], "seq", scatter_dimension=0, tiled=True),
        lax.psum_scatter(gradients[14], "seq", scatter_dimension=1, tiled=True),
        lax.psum_scatter(gradients[15], "seq", scatter_dimension=1, tiled=True),
        lax.psum_scatter(gradients[16], "seq", scatter_dimension=0, tiled=True),
        lax.psum_scatter(gradients[17], "seq", scatter_dimension=1, tiled=True),
        lax.psum_scatter(gradients[18], "seq", scatter_dimension=0, tiled=True),
    )
    summed = (
        lax.psum(shares[0].astype(jnp.bfloat16), "grp").astype(jnp.float32),
        lax.psum(shares[1].astype(jnp.bfloat16), "grp").astype(jnp.float32),
        lax.psum(shares[2].astype(jnp.bfloat16), "grp").astype(jnp.float32),
        lax.psum(shares[3].astype(jnp.bfloat16), "grp").astype(jnp.float32),
        lax.psum(shares[4].astype(jnp.bfloat16), "grp").astype(jnp.float32),
        lax.psum(shares[5].astype(jnp.bfloat16), "grp").astype(jnp.float32),
        lax.psum(shares[6].astype(jnp.bfloat16), "grp").astype(jnp.float32),
        lax.psum(shares[7].astype(jnp.bfloat16), "grp").astype(jnp.float32),
        lax.psum(shares[8].astype(jnp.bfloat16), "grp").astype(jnp.float32),
        lax.psum(shares[9].astype(jnp.bfloat16), "grp").astype(jnp.float32),
        lax.psum(shares[10].astype(jnp.bfloat16), "grp").astype(jnp.float32),
        lax.psum(shares[11].astype(jnp.bfloat16), "grp").astype(jnp.float32),
        lax.psum(shares[12].astype(jnp.bfloat16), "grp").astype(jnp.float32),
        lax.psum(shares[13].astype(jnp.bfloat16), "grp").astype(jnp.float32),
        lax.psum(shares[14].astype(jnp.bfloat16), "grp").astype(jnp.float32),
        lax.psum(shares[15].astype(jnp.bfloat16), "grp").astype(jnp.float32),
        lax.psum(shares[16].astype(jnp.bfloat16), "grp").astype(jnp.float32),
        lax.psum(shares[17].astype(jnp.bfloat16), "grp").astype(jnp.float32),
        lax.psum(shares[18].astype(jnp.bfloat16), "grp").astype(jnp.float32),
    )
    return (
        activations,
        input_grad,
        summed[0],
        summed[1],
        summed[2],
        summed[3],
        summed[4],
        summed[5],
        summed[6],
        summed[7],
        summed[8],
        summed[9],
        summed[10],
        summed[11],
        summed[12],
        summed[13],
        summed[14],
        summed[15],
        summed[16],
        summed[17],
        summed[18],
    )


def solution(mesh):
    in_specs = (
        P(("grp", "seq"), None),
        P("grp", None, None),
        P("grp", None),
        P("grp", None, None),
        P(("grp", "seq"), None),
        P(None, "seq"),
        P("seq"),
        P(None, "seq"),
        P("seq"),
        P("seq"),
        P("seq"),
        P(None, "seq"),
        P("seq"),
        P(None, "seq"),
        P("seq"),
        P(None, "seq"),
        P("seq"),
        P(None, "seq"),
        P("seq"),
        P(None, "seq"),
        P(None, "seq"),
        P("seq"),
        P(None, "seq"),
        P("seq"),
    )
    out_specs = (
        P(("grp", "seq"), None),
        P(("grp", "seq"), None),
        P(None, "seq"),
        P("seq"),
        P(None, "seq"),
        P("seq"),
        P("seq"),
        P("seq"),
        P(None, "seq"),
        P("seq"),
        P(None, "seq"),
        P("seq"),
        P(None, "seq"),
        P("seq"),
        P(None, "seq"),
        P("seq"),
        P(None, "seq"),
        P(None, "seq"),
        P("seq"),
        P(None, "seq"),
        P("seq"),
    )
    return jax.shard_map(
        on_device, mesh=mesh, in_specs=in_specs, out_specs=out_specs, check_vma=False
    )
```

profile of v0, /device:TPU:9, one launch (start us, length us, event | category | flops | bytes accessed | tf_op | source)
XLA Modules:
  0.0 3953.4 jit_solution(15882219262859450209)
XLA Ops:
  23.0 69.1 %all-gather.2 = bf16[8,1,768]{2,1,0:T(2,128)(2,1)S(1)} all-gather(bf16[1,1,768]{2,1,0:T(2,128)(2,1)S(1)} %reshape.697), channel_id=1, replica_groups=mesh['grp'=4,'seq'=8] {'seq'}, dimensions={0}, use_global_device_ids=true | all-gather | bytes 13824 | tf_op jit(solution)/shard_map/all_gather | solution.py:153
  92.9 50.9 %all-gather.1 = bf16[8,192,9]{1,2,0:T(8,128)(2,1)S(1)} all-gather(bf16[1,192,9]{1,2,0:T(8,128)(2,1)S(1)} %bitcast.211), channel_id=1, replica_groups=mesh['grp'=4,'seq'=8] {'seq'}, dimensions={0}, use_global_device_ids=true | all-gather | bytes 31104 | tf_op jit(solution)/shard_map/all_gather | solution.py:150
  146.8 50.2 %all-reduce.17 = (bf16[1536]{0:T(1024)(128)(2,1)S(1)}, bf16[1536]{0:T(1024)(128)(2,1)}, bf16[1536]{0:T(1024)(128)(2,1)}, bf16[1536]{0:T(1024)(128)(2,1)}, bf16[1...) all-reduce(bf16[1536]{0:T(1024)(128)(2,1)S(1)} %dynamic-update-slice, ...), channel_id=1, replica_groups=mesh['grp'=4,'seq'=8] {'seq'}, use_global_device_ids=true, to_apply=%add | all-reduce | flops 9216 | bytes 36864
  205.2 175.5 %all-gather.17.cloned.1.call-done = bf16[1536,6144]{1,0:T(8,128)(2,1)} async-done(((bf16[1536,768]{1,0:T(8,128)(2,1)}), bf16[1536,6144]{1,0:T(8,128)(2,1)}) %all-gather.17.cloned.1.call-update) | async-done | bytes 18874384 | tf_op jit(solution)/shard_map/all_gather | solution.py:152
  400.0 61.6 %all-gather.33.cloned.1.call-done = bf16[1536,1536]{0,1:T(8,128)(2,1)} async-done(((bf16[1536,192]{0,1:T(8,128)(2,1)}), bf16[1536,1536]{0,1:T(8,128)(2,1)}) %all-gather.33.cloned.1.call-update) | async-done | bytes 4718608 | tf_op jit(solution)/shard_map/all_gather | solution.py:167
  466.5 20.6 all-gather.4
  488.5 23.1 all-gather.3
  512.9 24.0 all-gather
  537.5 53.4 %all_gather.85 = bf16[64,3072]{1,0:T(8,128)(2,1)S(1)} all-gather(bf16[64,384]{1,0:T(8,128)(2,1)} %param.37), channel_id=1, replica_groups=mesh['grp'=4,'seq'=8] {'seq'}, dimensions={1}, use_global_device_ids=true | all-gather | bytes 442368 | tf_op jit(solution)/shard_map/all_gather | solution.py:158
  601.7 303.6 %all-gather.19.cloned.1.call-done = bf16[6144,1536]{0,1:T(8,128)(2,1)} async-done(((bf16[6144,192]{0,1:T(8,128)(2,1)}), bf16[6144,1536]{0,1:T(8,128)(2,1)}) %all-gather.19.cloned.1.call-update) | async-done | bytes 18874384 | tf_op jit(solution)/shard_map/all_gather | solution.py:156
  905.2 15.4 fusion.167
  924.4 60.7 %all-gather.27.cloned.1.call-done = bf16[1536,1536]{0,1:T(8,128)(2,1)} async-done(((bf16[1536,192]{0,1:T(8,128)(2,1)}), bf16[1536,1536]{0,1:T(8,128)(2,1)}) %all-gather.27.cloned.1.call-update) | async-done | bytes 4718608 | tf_op jit(solution)/shard_map/all_gather | solution.py:164
  990.7 74.6 %all-gather.23.cloned.1.call-done = bf16[1536,1536]{0,1:T(8,128)(2,1)} async-done(((bf16[1536,192]{0,1:T(8,128)(2,1)}), bf16[1536,1536]{0,1:T(8,128)(2,1)}) %all-gather.23.cloned.1.call-update) | async-done | bytes 4718608 | tf_op jit(solution)/shard_map/all_gather | solution.py:165
  1087.5 48.4 %all-gather.21.cloned.1.call-done = bf16[1280,1536]{0,1:T(8,128)(2,1)} async-done(((bf16[1280,192]{0,1:T(8,128)(2,1)}), bf16[1280,1536]{0,1:T(8,128)(2,1)}) %all-gather.21.cloned.1.call-update) | async-done | bytes 3932176 | tf_op jit(solution)/shard_map/all_gather | solution.py:160
  1156.6 41.4 %all-gather.37.cloned.1.call-done = bf16[1024,1536]{1,0:T(8,128)(2,1)} async-done(((bf16[128,1536]{1,0:T(8,128)(2,1)}), bf16[1024,1536]{1,0:T(8,128)(2,1)}) %all-gather.37.cloned.1.call-update) | async-done | bytes 3145744 | tf_op jit(solution)/shard_map/all_gather | solution.py:389
  1206.6 71.5 %all-gather.25.cloned.1.call-done = bf16[1536,1536]{0,1:T(8,128)(2,1)} async-done(((bf16[1536,192]{0,1:T(8,128)(2,1)}), bf16[1536,1536]{0,1:T(8,128)(2,1)}) %all-gather.25.cloned.1.call-update) | async-done | bytes 4718608 | tf_op jit(solution)/shard_map/all_gather | solution.py:162
  1289.7 49.7 %all-gather.29.cloned.1.call-done = bf16[1024,1536]{1,0:T(8,128)(2,1)} async-done(((bf16[128,1536]{1,0:T(8,128)(2,1)}), bf16[1024,1536]{1,0:T(8,128)(2,1)}) %all-gather.29.cloned.1.call-update) | async-done | bytes 3145744 | tf_op jit(solution)/shard_map/all_gather | solution.py:282
  1354.0 46.7 %all-gather.31.cloned.1.call-done = bf16[1024,1536]{1,0:T(8,128)(2,1)} async-done(((bf16[128,1536]{1,0:T(8,128)(2,1)}), bf16[1024,1536]{1,0:T(8,128)(2,1)}) %all-gather.31.cloned.1.call-update) | async-done | bytes 3145744 | tf_op jit(solution)/shard_map/all_gather | solution.py:283
  1423.1 25.2 all_gather.101
  1448.4 25.7 all_gather.99
  1605.2 16.2 fusion.178
  1641.9 15.1 fusion.157
  1681.9 93.8 %reduce-scatter.18.cloned.1.call-done = f32[1280,192]{0,1:T(8,128)} async-done(((f32[1280,1536]{0,1:T(8,128)}), f32[1280,192]{0,1:T(8,128)}) %reduce-scatter.18.cloned.1.call-update) | async-done | bytes 983056 | tf_op jit(solution)/shard_map/reduce_scatter | solution.py:538
  1777.7 163.6 %reduce-scatter.20.cloned.1.call-done = f32[1536,192]{0,1:T(8,128)} async-done(((f32[1536,1536]{0,1:T(8,128)}), f32[1536,192]{0,1:T(8,128)}) %reduce-scatter.20.cloned.1.call-update) | async-done | bytes 1179664 | tf_op jit(solution)/shard_map/reduce_scatter | solution.py:540
  1943.5 163.9 %reduce-scatter.22.cloned.1.call-done = f32[1536,192]{0,1:T(8,128)} async-done(((f32[1536,1536]{0,1:T(8,128)}), f32[1536,192]{0,1:T(8,128)}) %reduce-scatter.22.cloned.1.call-update) | async-done | bytes 1179664 | tf_op jit(solution)/shard_map/reduce_scatter | solution.py:542
  2109.5 163.9 %reduce-scatter.24.cloned.1.call-done = f32[1536,192]{0,1:T(8,128)} async-done(((f32[1536,1536]{0,1:T(8,128)}), f32[1536,192]{0,1:T(8,128)}) %reduce-scatter.24.cloned.1.call-update) | async-done | bytes 1179664 | tf_op jit(solution)/shard_map/reduce_scatter | solution.py:543
  2275.5 163.9 %reduce-scatter.26.cloned.1.call-done = f32[1536,192]{0,1:T(8,128)} async-done(((f32[1536,1536]{0,1:T(8,128)}), f32[1536,192]{0,1:T(8,128)}) %reduce-scatter.26.cloned.1.call-update) | async-done | bytes 1179664 | tf_op jit(solution)/shard_map/reduce_scatter | solution.py:545
  2441.6 606.4 %reduce-scatter.14.cloned.1.call-done = f32[6144,192]{0,1:T(8,128)} async-done(((f32[6144,1536]{0,1:T(8,128)}), f32[6144,192]{0,1:T(8,128)}) %reduce-scatter.14.cloned.1.call-update) | async-done | bytes 4718608 | tf_op jit(solution)/shard_map/reduce_scatter | solution.py:534
  3052.0 603.4 %reduce-scatter.12.cloned.1.call-done = f32[1536,768]{1,0:T(8,128)} async-done(((f32[1536,6144]{1,0:T(8,128)}), f32[1536,768]{1,0:T(8,128)}) %reduce-scatter.12.cloned.1.call-update) | async-done | bytes 4718608 | tf_op jit(solution)/shard_map/reduce_scatter | solution.py:530
  3678.9 28.3 all-reduce.16
  3726.5 60.7 %reduce-scatter.16.cloned.1.call-done = f32[64,384]{1,0:T(8,128)} async-done(((f32[64,3072]{1,0:T(8,128)}), f32[64,384]{1,0:T(8,128)}) %reduce-scatter.16.cloned.1.call-update) | async-done | bytes 98320 | tf_op jit(solution)/shard_map/reduce_scatter | solution.py:536
  3808.6 125.3 %all-reduce.28.cloned.1.call-done = (bf16[1536,768]{1,0:T(8,128)(2,1)}, bf16[6144,192]{0,1:T(8,128)(2,1)}, bf16[1280,192]{0,1:T(8,128)(2,1)}, bf16[1536,192]{0,1...) async-done(((bf16[1536,768]{1,0:T(8,128)(2,1)}, bf16[6144,192]{0,1:T(8,128)(2,1)}, bf16[1280,192]{0,1:T(8,128)(2,1)}, ...) | async-done | bytes 7569424 | tf_op jit(solution)/shard_map/psum | solution.py:551
  (563 shorter events, 430.7 us)
Async XLA Ops:
  7.2 583.7 %copy-start = (f32[3,64]{1,0:T(4,128)S(1)}, f32[3,64]{1,0:T(4,128)}, u32[]{:S(2)}) copy-start(f32[3,64]{1,0:T(4,128)} %param.26) | copy-start | bytes 2308
  7.2 194.5 %copy-start.21 = (bf16[128,1536]{1,0:T(8,128)(2,1)S(1)}, bf16[128,1536]{1,0:T(8,128)(2,1)}, u32[]{:S(2)}) copy-start(bf16[128,1536]{1,0:T(8,128)(2,1)} %param.24) | copy-start | bytes 1179652
  7.3 373.3 %all-gather.17.cloned.1.call-start = ((), (), s32[]{:S(2)}) async-start(), calls=%async_computation.9 | async-start | bytes 21233664 | tf_op jit(solution)/shard_map/all_gather | solution.py:152
  8.1 453.6 %all-gather.33.cloned.1.call-start = ((), (), s32[]{:S(2)}) async-start(), calls=%async_computation.18 | async-start | bytes 5308416 | tf_op jit(solution)/shard_map/all_gather | solution.py:167
  9.2 192.5 %collective-permute-start.1 = (bf16[65,1536]{1,0:T(8,128)(2,1)S(1)}, bf16[65,1536]{1,0:T(8,128)(2,1)S(1)}, u32[]{:S(2)}, u32[]{:S(2)}) collective-permute-start(bf16[65,1536]{1,0:T(8,128)(2,1)S(1)} %get-tuple-element.225), channel_id=1, source_target_pairs={{1,0},{2,1},{3,2},{4,3},{5,4},{6,5},{7,6},{9,8},{10,9},{11,10},{12... | collective-permute-start | bytes 599048 | tf_op jit(solution)/shard_map/ppermute | solution.py:32
  12.2 189.5 %collective-permute-start = (bf16[65,1536]{1,0:T(8,128)(2,1)S(1)}, bf16[65,1536]{1,0:T(8,128)(2,1)S(1)}, u32[]{:S(2)}, u32[]{:S(2)}) collective-permute-start(bf16[65,1536]{1,0:T(8,128)(2,1)S(1)} %get-tuple-element.224), channel_id=1, source_target_pairs={{0,1},{1,2},{2,3},{3,4},{4,5},{5,6},{6,7},{8,9},{9,10},{10,11},{11... | collective-permute-start | bytes 599048 | tf_op jit(solution)/shard_map/ppermute | solution.py:29
  14.5 578.7 %all-reduce.24.cloned.1.call-start = ((), (), s32[]{:S(2)}) async-start(), calls=%async_computation.10 | async-start | bytes 196608 | tf_op jit(solution)/shard_map/psum | solution.py:214
  197.1 889.6 %copy-start.86 = (s32[128]{0:T(128)}, s32[128]{0:T(128)S(1)}, u32[]{:S(2)}) copy-start(s32[128]{0:T(128)S(1)} %broadcast_minimum_fusion.9) | copy-start | bytes 1540
  204.8 188.7 %copy-start.93 = (f32[128]{0:T(128)}, f32[128]{0:T(128)S(1)}, u32[]{:S(2)}) copy-start(f32[128]{0:T(128)S(1)} %broadcast_multiply_fusion.5) | copy-start | bytes 1540
  205.2 188.3 %copy-start.96 = (f32[128]{0:T(128)}, f32[128]{0:T(128)S(1)}, u32[]{:S(2)}) copy-start(f32[128]{0:T(128)S(1)} %add_rsqrt_fusion.1) | copy-start | bytes 1540
  397.2 508.0 %all-gather.19.cloned.1.call-start = ((), (), s32[]{:S(2)}) async-start(), calls=%async_computation.11 | async-start | bytes 21233664 | tf_op jit(solution)/shard_map/all_gather | solution.py:156
  397.8 587.4 %all-gather.27.cloned.1.call-start = ((), (), s32[]{:S(2)}) async-start(), calls=%async_computation.15 | async-start | bytes 5308416 | tf_op jit(solution)/shard_map/all_gather | solution.py:164
  398.4 666.9 %all-gather.23.cloned.1.call-start = ((), (), s32[]{:S(2)}) async-start(), calls=%async_computation.13 | async-start | bytes 5308416 | tf_op jit(solution)/shard_map/all_gather | solution.py:165
  399.0 737.0 %all-gather.21.cloned.1.call-start = ((), (), s32[]{:S(2)}) async-start(), calls=%async_computation.12 | async-start | bytes 4423680 | tf_op jit(solution)/shard_map/all_gather | solution.py:160
  399.7 798.3 %all-gather.37.cloned.1.call-start = ((), (), s32[]{:S(2)}) async-start(), calls=%async_computation.20 | async-start | bytes 3538944 | tf_op jit(solution)/shard_map/all_gather | solution.py:389
  465.7 812.4 %all-gather.25.cloned.1.call-start = ((), (), s32[]{:S(2)}) async-start(), calls=%async_computation.14 | async-start | bytes 5308416 | tf_op jit(solution)/shard_map/all_gather | solution.py:162
  466.4 873.0 %all-gather.29.cloned.1.call-start = ((), (), s32[]{:S(2)}) async-start(), calls=%async_computation.16 | async-start | bytes 3538944 | tf_op jit(solution)/shard_map/all_gather | solution.py:282
  990.0 410.8 %all-gather.31.cloned.1.call-start = ((), (), s32[]{:S(2)}) async-start(), calls=%async_computation.17 | async-start | bytes 3538944 | tf_op jit(solution)/shard_map/all_gather | solution.py:283
  1070.0 425.8 %all-gather.35.cloned.1.call-start = ((), (), s32[]{:S(2)}) async-start(), calls=%async_computation.19 | async-start | bytes 3538944 | tf_op jit(solution)/shard_map/all_gather | solution.py:388
  1284.7 347.0 %all-reduce.26.cloned.1.call-start = ((), (), s32[]{:S(2)}) async-start(), calls=%async_computation.21 | async-start | bytes 196608 | tf_op jit(solution)/shard_map/psum | solution.py:473
  1550.4 225.3 %reduce-scatter.18.cloned.1.call-start = ((), (), s32[]{:S(2)}) async-start(), calls=%async_computation.25 | async-start | bytes 8847360 | tf_op jit(solution)/shard_map/reduce_scatter | solution.py:538
  1569.8 371.6 %reduce-scatter.20.cloned.1.call-start = ((), (), s32[]{:S(2)}) async-start(), calls=%async_computation.26 | async-start | bytes 10616832 | tf_op jit(solution)/shard_map/reduce_scatter | solution.py:540
  1575.8 531.5 %reduce-scatter.22.cloned.1.call-start = ((), (), s32[]{:S(2)}) async-start(), calls=%async_computation.27 | async-start | bytes 10616832 | tf_op jit(solution)/shard_map/reduce_scatter | solution.py:542
  1586.6 686.8 %reduce-scatter.24.cloned.1.call-start = ((), (), s32[]{:S(2)}) async-start(), calls=%async_computation.28 | async-start | bytes 10616832 | tf_op jit(solution)/shard_map/reduce_scatter | solution.py:543
  1597.2 842.2 %reduce-scatter.26.cloned.1.call-start = ((), (), s32[]{:S(2)}) async-start(), calls=%async_computation.29 | async-start | bytes 10616832 | tf_op jit(solution)/shard_map/reduce_scatter | solution.py:545
  1604.2 1443.7 %reduce-scatter.14.cloned.1.call-start = ((), (), s32[]{:S(2)}) async-start(), calls=%async_computation.23 | async-start | bytes 42467328 | tf_op jit(solution)/shard_map/reduce_scatter | solution.py:534
  1621.4 2034.0 %reduce-scatter.12.cloned.1.call-start = ((), (), s32[]{:S(2)}) async-start(), calls=%async_computation.22 | async-start | bytes 42467328 | tf_op jit(solution)/shard_map/reduce_scatter | solution.py:530
  1657.0 2064.3 %reduce-scatter.28.cloned.1.call-start = ((), (), s32[]{:S(2)}) async-start(), calls=%async_computation.30 | async-start | bytes 884736
  1680.1 2107.1 %reduce-scatter.16.cloned.1.call-start = ((), (), s32[]{:S(2)}) async-start(), calls=%async_computation.24 | async-start | bytes 884736 | tf_op jit(solution)/shard_map/reduce_scatter | solution.py:536
  1681.9 2252.1 %all-reduce.28.cloned.1.call-start = ((), (), s32[]{:S(2)}) async-start(), calls=%async_computation.31 | async-start | bytes 15138816 | tf_op jit(solution)/shard_map/psum | solution.py:551
  3667.0 55.2 %collective-permute-start.2 = (bf16[65,1536]{1,0:T(8,128)(2,1)}, bf16[65,1536]{1,0:T(8,128)(2,1)S(1)}, u32[]{:S(2)}, u32[]{:S(2)}) collective-permute-start(bf16[65,1536]{1,0:T(8,128)(2,1)} %get-tuple-element.223), channel_id=1, source_target_pairs={{0,1},{1,2},{2,3},{3,4},{4,5},{5,6},{6,7},{8,9},{9,10},{10,11},{11... | collective-permute-start | bytes 599048 | tf_op jit(solution)/shard_map/ppermute | solution.py:29
  3670.3 51.9 %collective-permute-start.3 = (bf16[65,1536]{1,0:T(8,128)(2,1)S(1)}, bf16[65,1536]{1,0:T(8,128)(2,1)S(1)}, u32[]{:S(2)}, u32[]{:S(2)}) collective-permute-start(bf16[65,1536]{1,0:T(8,128)(2,1)S(1)} %get-tuple-element.222), channel_id=1, source_target_pairs={{1,0},{2,1},{3,2},{4,3},{5,4},{6,5},{7,6},{9,8},{10,9},{11,10},{12... | collective-permute-start | bytes 599048 | tf_op jit(solution)/shard_map/ppermute | solution.py:32
  (146 other events, 2994.0 us)
Sparse Core Ops, SparseCore 0:
  9.7 370.9 all-gather.16
  382.8 78.7 all-gather.32
  465.6 66.8 all-reduce.23
  533.8 371.3 all-gather.18
  907.3 77.8 all-gather.26
  987.2 78.0 all-gather.22
  1067.5 68.4 all-gather.20
  1138.7 59.3 all-gather.36
  1200.2 77.7 all-gather.24
  1280.1 59.3 all-gather.28
  1341.6 59.0 all-gather.30
  1403.3 60.3 all-gather.34
  1550.5 81.1 all-reduce.25
  1635.2 140.4 reduce-scatter.17
  1779.1 162.1 reduce-scatter.19
  1944.8 162.5 reduce-scatter.21
  2110.8 162.5 reduce-scatter.23
  2276.8 162.5 reduce-scatter.25
  2443.3 604.6 reduce-scatter.13
  3052.2 603.1 reduce-scatter.11
  3659.3 61.9 reduce-scatter.27
  3725.5 61.6 reduce-scatter.15
  3791.8 142.1 all-reduce.27
where the time goes:
time: 3970 us; the launch traced here: 3950 us
  waiting for transfers between devices  3110 us (78%)
  blocking collectives  384 us (10%)
  matrix products  269 us (7%)
  other arithmetic  86.6 us (2%)
  local copies, waits for them, and re-layouts  56.7 us (1%)
    reduce_scatter x1, waiting for transfers between devices, on_device(): lax.psum_scatter(gradients[6], 'seq', scatter_dimension=1, tiled=True)  606 us
    reduce_scatter x1, waiting for transfers between devices, on_device(): lax.psum_scatter(gradients[2], 'seq', scatter_dimension=1, tiled=True)  603 us
    all_gather x1, waiting for transfers between devices, on_device(): lax.all_gather(fc2_weight, 'seq', axis=1, tiled=True)  304 us
    all_gather x1, waiting for transfers between devices, on_device(): lax.all_gather(fc1_weight, 'seq', axis=1, tiled=True)  175 us
    reduce_scatter x1, waiting for transfers between devices, on_device(): lax.psum_scatter(gradients[15], 'seq', scatter_dimension=1, tiled=True)  164 us
    reduce_scatter x1, waiting for transfers between devices, on_device(): lax.psum_scatter(gradients[17], 'seq', scatter_dimension=1, tiled=True)  164 us
    reduce_scatter x1, waiting for transfers between devices, on_device(): lax.psum_scatter(gradients[14], 'seq', scatter_dimension=1, tiled=True)  164 us
    reduce_scatter x1, waiting for transfers between devices, on_device(): lax.psum_scatter(gradients[12], 'seq', scatter_dimension=1, tiled=True)  164 us
  transfers between devices with their start and end apart: 27, of which 21 were waited for; matrix products, arithmetic and copies ran while one was open for 8% of the time, Pallas kernels for 0%

commit v1 on v0

--- a/solution.py
+++ b/solution.py
@@ -591,6 +591,259 @@
     )
 
 
+def gather_rows(block):
+    return lax.all_gather(block, "seq", axis=0, tiled=True)
+
+
+def scatter_rows(partial):
+    return lax.psum_scatter(
+        partial.astype(jnp.bfloat16), "seq", scatter_dimension=0, tiled=True
+    ).astype(jnp.float32)
+
+
+def mm(left, right):
+    return jnp.dot(left, right, preferred_element_type=jnp.float32)
+
+
+def on_device_heads(
+    hidden,
+    latent_shape,
+    cond_r,
+    clip,
+    cotangent,
+    conv_weight,
+    conv_bias,
+    fc1_weight,
+    fc1_bias,
+    grn_gamma,
+    grn_beta,
+    fc2_weight,
+    fc2_bias,
+    time_weight,
+    time_bias,
+    map_weight,
+    map_bias,
+    query_weight,
+    query_bias,
+    key_weight,
+    value_weight,
+    value_bias,
+    out_weight,
+    out_bias,
+):
+    f32, bf16 = jnp.float32, jnp.bfloat16
+    shards = lax.axis_size("seq")
+    me = lax.axis_index("seq")
+    rows = hidden.shape[0]
+    total = rows * shards
+    cols = C // shards
+    local_heads = HEADS // shards
+    margin = WMAX + 1
+    shape_row = latent_shape[0]
+    positions = me * rows + jnp.arange(rows, dtype=jnp.int32)
+    segment, row_index, column, height, latent_width = latent_grid(positions, shape_row)
+    all_segment = latent_grid(jnp.arange(total, dtype=jnp.int32), shape_row)[0]
+    latents = jnp.arange(NLAT, dtype=jnp.int32)
+    picked = (segment[:, None] == latents[None, :]).astype(f32)
+    all_picked = (all_segment[:, None] == latents[None, :]).astype(f32)
+
+    mod_cols = jnp.dot(
+        cond_r, time_weight.astype(f32), precision=HIGHEST_PRECISION
+    ) + time_bias.astype(f32)
+    pack = jnp.concatenate(
+        [
+            conv_weight.astype(f32),
+            conv_bias.astype(f32)[None],
+            fc2_bias.astype(f32)[None],
+            mod_cols.reshape(NLAT * 2, cols),
+        ],
+        axis=0,
+    )
+    packed = lax.all_gather(pack, "seq", axis=0)
+    kernel_full = packed[:, :9].transpose(1, 0, 2).reshape(9, C)
+    kernel_bias = packed[:, 9].reshape(C)
+    shrink_bias = packed[:, 10].reshape(C)
+    modulation = (
+        packed[:, 11:].reshape(shards, NLAT, 2 * cols).transpose(1, 0, 2).reshape(NLAT, 2 * C)
+    )
+    mod_rows = jnp.dot(picked, modulation, precision=HIGHEST_PRECISION)
+    scale_rows = 1.0 + mod_rows[:, :C]
+
+    shrink_rows = lax.all_to_all(fc2_weight, "seq", 0, 1, tiled=True)
+    output_rows = lax.all_to_all(out_weight, "seq", 0, 1, tiled=True)
+    cot_full = gather_rows(cotangent)
+
+    padded = padded_2(hidden, (("seq", 0),), margin)
+    conv_out = jnp.broadcast_to(kernel_bias[None, :], (rows, C))
+    tap_list = []
+    for down_step in (-1, 0, 1):
+        for side_step in (-1, 0, 1):
+            tap_number = 3 * (down_step + 1) + (side_step + 1)
+            valid = valid_tap(row_index, column, height, latent_width, down_step, side_step)
+            offset = down_step * WMAX + side_step
+            nearby = padded[margin + offset : margin + offset + rows].astype(f32)
+            conv_out = conv_out + kernel_full[tap_number][None, :] * nearby * valid[:, None]
+            tap_list.append((tap_number, down_step, side_step, offset, valid))
+    normed_one, inverse_one = layer_stats(conv_out)
+    normed_full = gather_rows(normed_one.astype(bf16))
+
+    pre_act = mm(normed_full, fc1_weight) + fc1_bias.astype(f32)
+    phi = 0.5 * (1.0 + lax.erf(pre_act * math.sqrt(0.5)))
+    activated = pre_act * phi
+    energy = column_sum(all_picked, activated * activated)
+    root = jnp.sqrt(energy + 1.0)
+    denom = lax.psum(jnp.sum(root, axis=-1, keepdims=True), "seq") / FF + EPS_NORM
+    ratio = root / denom
+    ratio_rows = jnp.dot(all_picked, ratio, precision=HIGHEST_PRECISION)
+    gamma = grn_gamma.astype(f32)
+    response = gamma * (activated * ratio_rows) + grn_beta.astype(f32) + activated
+    response_low = response.astype(bf16)
+    branch = scatter_rows(mm(response_low, shrink_rows)) + shrink_bias
+    first_sum = hidden.astype(f32) + branch
+    second_sum = first_sum * scale_rows + mod_rows[:, C:]
+    normed_two, inverse_two = layer_stats(second_sum)
+    attn_full = gather_rows(normed_two.astype(bf16))
+
+    context_in = jax.nn.silu(clip.reshape(NLAT * NCTX, CLIP).astype(f32)).astype(bf16)
+    context_cols = (mm(context_in, map_weight) + map_bias.astype(f32)).astype(bf16)
+    context = lax.all_gather(context_cols, "seq", axis=1, tiled=True)
+
+    heads = lambda values: values.reshape(values.shape[0], local_heads, HEAD_DIM)
+    value_shift = value_bias.astype(f32)
+    queries = (mm(attn_full, query_weight) + query_bias.astype(f32)).astype(bf16)
+    inputs = jnp.concatenate([attn_full, context], axis=0)
+    keys = mm(inputs, key_weight).astype(bf16)
+    values = (mm(inputs, value_weight) + value_shift).astype(bf16)
+    key_segment = jnp.concatenate(
+        [all_segment, jnp.arange(NLAT * NCTX, dtype=jnp.int32) // NCTX], axis=0
+    )
+    admitted = all_segment[:, None] == key_segment[None, :]
+    scores = (
+        jnp.einsum("qhd,khd->hqk", heads(queries), heads(keys), preferred_element_type=f32)
+        * SCORE_SCALE
+    )
+    scores = jnp.where(admitted[None], scores, MASKED)
+    top = jnp.max(scores, axis=-1, keepdims=True)
+    expo = jnp.exp(scores - top)
+    probs = expo / jnp.sum(expo, axis=-1, keepdims=True)
+    probs_low = probs.astype(bf16)
+    mixed = jnp.einsum("hqk,khd->qhd", probs_low, heads(values), preferred_element_type=f32)
+    mixed_low = mixed.reshape(total, cols).astype(bf16)
+    mixed_full = lax.all_gather(mixed_low, "seq", axis=1, tiled=True)
+    out_cols = (mm(mixed_full, out_weight) + out_bias.astype(f32)).astype(bf16)
+    activations = (
+        second_sum + lax.all_to_all(out_cols, "seq", 0, 1, tiled=True).astype(f32)
+    ).astype(bf16)
+
+    cot_cols = lax.dynamic_slice_in_dim(cot_full, me * cols, cols, 1)
+    grad_out_w = outer_sum(mixed_full, cot_cols)
+    grad_out_b = jnp.sum(cot_cols.astype(f32), axis=0)
+    d_mixed_low = against(cot_full, output_rows).astype(bf16)
+    d_mixed = heads(d_mixed_low)
+    delta = jnp.sum(d_mixed.astype(f32) * mixed, axis=-1).T
+    d_probs = jnp.einsum("qhd,khd->hqk", d_mixed, heads(values), preferred_element_type=f32)
+    d_scores = (probs * (d_probs - delta[..., None])).astype(bf16)
+    d_queries = (
+        jnp.einsum("hqk,khd->qhd", d_scores, heads(keys), preferred_element_type=f32) * SCORE_SCALE
+    ).reshape(total, cols)
+    d_keys = (
+        jnp.einsum("hqk,qhd->khd", d_scores, heads(queries), preferred_element_type=f32)
+        * SCORE_SCALE
+    ).reshape(-1, cols)
+    d_values = jnp.einsum("hqk,qhd->khd", probs_low, d_mixed, preferred_element_type=f32).reshape(
+        -1, cols
+    )
+    d_queries_low = d_queries.astype(bf16)
+    d_keys_low = d_keys.astype(bf16)
+    d_values_low = d_values.astype(bf16)
+    grad_query_w = outer_sum(attn_full, d_queries_low)
+    grad_query_b = jnp.sum(d_queries_low.astype(f32), axis=0)
+    grad_key_w = outer_sum(inputs, d_keys_low)
+    grad_value_w = outer_sum(inputs, d_values_low)
+    grad_value_b = jnp.sum(d_values_low.astype(f32), axis=0)
+    ctx_part = against(d_keys_low[total:], key_weight) + against(d_values_low[total:], value_weight)
+    d_context = lax.psum_scatter(ctx_part, "seq", scatter_dimension=1, tiled=True)
+    grad_map_w = outer_sum(context_in, d_context.astype(bf16))
+    grad_map_b = jnp.sum(d_context, axis=0)
+    d_attn = scatter_rows(
+        against(d_queries_low, query_weight)
+        + against(d_keys_low[:total], key_weight)
+        + against(d_values_low[:total], value_weight)
+    )
+    d_second = cotangent.astype(f32) + layer_back(d_attn, normed_two, inverse_two)
+    d_first = d_second * scale_rows
+    d_mod = column_sum(picked, jnp.concatenate([d_second * first_sum, d_second], axis=1))
+    d_branch_low = d_first.astype(bf16)
+    branch_full = gather_rows(d_branch_low)
+    grad_shrink_rows = outer_sum(response_low, branch_full).astype(bf16)
+    grad_shrink_w = lax.all_to_all(grad_shrink_rows, "seq", 1, 0, tiled=True)
+    grad_shrink_b = jnp.sum(
+        lax.dynamic_slice_in_dim(branch_full, me * cols, cols, 1).astype(f32), axis=0
+    )
+    d_response = against(branch_full, shrink_rows)
+    d_scaled = d_response * activated
+    grad_gamma = jnp.sum(d_scaled * ratio_rows, axis=0)
+    grad_beta = jnp.sum(d_response, axis=0)
+    d_ratio = column_sum(all_picked, d_scaled * gamma)
+    pulled = lax.psum(jnp.sum(d_ratio * root, axis=-1, keepdims=True), "seq")
+    d_root = d_ratio / denom - pulled / (FF * denom * denom)
+    d_act = d_response * (gamma * ratio_rows + 1.0) + activated * jnp.dot(
+        all_picked, d_root / root, precision=HIGHEST_PRECISION
+    )
+    density = jnp.exp(-0.5 * pre_act * pre_act) * (1.0 / math.sqrt(2.0 * math.pi))
+    d_pre_low = (d_act * (phi + pre_act * density)).astype(bf16)
+    grad_expand_w = outer_sum(normed_full, d_pre_low)
+    grad_expand_b = jnp.sum(d_pre_low.astype(f32), axis=0)
+    d_normed = scatter_rows(against(d_pre_low, fc1_weight))
+    d_conv_low = layer_back(d_normed, normed_one, inverse_one).astype(bf16)
+    d_conv = d_conv_low.astype(f32)
+    d_padded = padded_2(d_conv_low, (("seq", 0),), margin)
+    small_rows = []
+    input_grad = d_first
+    for tap_number, down_step, side_step, offset, valid in tap_list:
+        nearby = padded[margin + offset : margin + offset + rows].astype(f32)
+        small_rows.append(jnp.sum(d_conv * nearby * valid[:, None], axis=0))
+        src_grid = latent_grid(positions - offset, shape_row)
+        src_valid = valid_tap(*src_grid[1:], down_step, side_step)
+        behind = d_padded[margin - offset : margin - offset + rows].astype(f32)
+        input_grad = input_grad + kernel_full[tap_number][None, :] * behind * src_valid[:, None]
+    small_rows.append(jnp.sum(d_conv, axis=0))
+    small = jnp.concatenate([jnp.stack(small_rows), d_mod.reshape(NLAT * 2, C)], axis=0)
+    conv_small = lax.psum_scatter(small[:10], "seq", scatter_dimension=1, tiled=True)
+    d_modulation = lax.psum_scatter(d_mod, "seq", scatter_dimension=1, tiled=True)
+    grad_time_w = lax.dot_general(
+        cond_r,
+        d_modulation,
+        (((0,), (0,)), ((), ())),
+        precision=HIGHEST_PRECISION,
+        preferred_element_type=f32,
+    )
+    grad_time_b = jnp.sum(d_modulation, axis=0)
+    gradients = (
+        conv_small[:9],
+        conv_small[9],
+        grad_expand_w,
+        grad_expand_b,
+        grad_gamma,
+        grad_beta,
+        grad_shrink_w,
+        grad_shrink_b,
+        grad_time_w,
+        grad_time_b,
+        grad_map_w,
+        grad_map_b,
+        grad_query_w,
+        grad_query_b,
+        grad_key_w,
+        grad_value_w,
+        grad_value_b,
+        grad_out_w,
+        grad_out_b,
+    )
+    summed = tuple(lax.psum(item.astype(bf16), "grp").astype(f32) for item in gradients)
+    return (activations, input_grad) + summed
+
+
 def solution(mesh):
     in_specs = (
         P(("grp", "seq"), None),
@@ -641,6 +894,7 @@
         P(None, "seq"),
         P("seq"),
     )
+    by_heads = HEADS % mesh.shape["seq"] == 0 and FF % mesh.shape["seq"] == 0
     return jax.shard_map(
-        on_device, mesh=mesh, in_specs=in_specs, out_specs=out_specs, check_vma=False
-    )
+        on_device_heads if by_heads else on_device, mesh=mesh, in_specs=in_specs, out_specs=out_specs, check_vma=False
+    )

time: 3970 us -> 1170 us (0.29)
  waiting for transfers between devices: 3110 us -> 683 us
  blocking collectives: 384 us -> 133 us
  matrix products: 269 us -> 138 us
    reduce_scatter x8 -> x4, waiting for transfers between devices: 2020 us -> 237 us  [the longest x3 227 us: scatter_rows(): lax.psum_scatter(partial.astype(jnp.bfloat16), 'seq', scatter_dimension=0...]
    all_gather x11 -> x5, waiting for transfers between devices: 934 us -> 246 us  [the longest x4 213 us: gather_rows(): return lax.all_gather(block, 'seq', axis=0, tiled=True)]
    all_gather x8 -> x2, blocking collectives: 292 us -> 69.7 us  [the longest x1 47.9 us: on_device_heads(): context = lax.all_gather(context_cols, 'seq', axis=1, tiled=True)]
    dot_general x28 -> x17, matrix products: 156 us -> 66.7 us  [the longest x7 26.9 us: mm(): return jnp.dot(left, right, preferred_element_type=jnp.float32)]
    unnamed x2 -> x0, blocking collectives: 78.5 us -> none
    unnamed x24 -> x14, waiting for transfers between devices: 17.1 us -> 90 us
    psum x3 -> x1, waiting for transfers between devices: 136 us -> 110 us  [on_device_heads(): lax.psum(item.astype(bf16), 'grp').astype(f32)]
  transfers between devices with their start and end apart: 27 -> 19, of which waited for: 21 -> 12; matrix products, arithmetic and copies ran while one was open for 8% -> 18% of each run, Pallas kernels for 0% -> 0%
where the time goes in v1:
time: 1170 us; the launch traced here: 1150 us
  waiting for transfers between devices  683 us (58%)
  matrix products  138 us (12%)
  blocking collectives  133 us (11%)
  other arithmetic  97.3 us (8%)
  local copies, waits for them, and re-layouts  54 us (5%)
  starting transfers between devices  32.2 us (3%)
  between operations  16.2 us (1%)
    reduce_scatter x3, waiting for transfers between devices, scatter_rows(): lax.psum_scatter(partial.astype(jnp.bfloat16), 'seq', scatter_dimension=0...  227 us
    all_gather x4, waiting for transfers between devices, gather_rows(): return lax.all_gather(block, 'seq', axis=0, tiled=True)  213 us
    psum x1, waiting for transfers between devices, on_device_heads(): lax.psum(item.astype(bf16), 'grp').astype(f32)  110 us
    unnamed x14, waiting for transfers between devices  90 us
    all_gather x1, blocking collectives, on_device_heads(): context = lax.all_gather(context_cols, 'seq', axis=1, tiled=True)  47.9 us
    all_gather x1, waiting for transfers between devices, on_device_heads(): mixed_full = lax.all_gather(mixed_low, 'seq', axis=1, tiled=True)  33.6 us
    convert_element_type x19, other arithmetic, on_device_heads(): lax.psum(item.astype(bf16), 'grp').astype(f32)  28.1 us
    dot_general x7, matrix products, outer_sum(): lax.dot_general(left_low, right_low, (((0,), (0,)), ((), ())), preferred_...  28 us
  transfers between devices with their start and end apart: 19, of which 12 were waited for; matrix products, arithmetic and copies ran while one was open for 18% of the time, Pallas kernels for 0%

profile of v1, /device:TPU:9, one launch (start us, length us, event | category | flops | bytes accessed | tf_op | source)
XLA Modules:
  0.0 1153.9 jit_solution(10438105617541486020)
XLA Ops:
  23.0 21.8 %all-gather.1 = f32[8,17,192]{2,1,0:T(8,128)S(1)} all-gather(f32[1,17,192]{2,1,0:T(8,128)S(1)} %maximum_bitcast_fusion), channel_id=2, replica_groups=mesh['grp'=4,'seq'=8] {'seq'}, dimensions={0}, use_global_device_ids=true | all-gather | bytes 117504 | tf_op jit(solution)/shard_map/all_gather | solution.py:662
  71.2 8.1 all-to-all-start
  79.5 88.6 %all-gather.8.cloned.1.call-done = bf16[1024,1536]{1,0:T(8,128)(2,1)} async-done(((bf16[128,1536]{1,0:T(8,128)(2,1)}), bf16[1024,1536]{1,0:T(8,128)(2,1)}) %all-gather.8.cloned.1.call-update) | async-done | bytes 3145744 | tf_op jit(solution)/shard_map/all_gather | solution.py:595
  168.0 6.2 add_multiply_fusion.1
  177.4 16.1 %psum.147 = f32[3,1]{0,1:T(1,128)S(1)} all-reduce(f32[3,1]{0,1:T(1,128)S(1)} %bitcast.174), channel_id=1, replica_groups=mesh['grp'=4,'seq'=8] {'seq'}, use_global_device_ids=true, to_apply=%region_8.9 | all-reduce | flops 3 | bytes 24 | tf_op jit(solution)/shard_map/psum | solution.py:695
  193.5 5.8 add_convert_fusion.1
  199.3 6.4 convolution_convert_fusion.1
  210.2 72.6 %reduce-scatter.11.cloned.1.call-done = bf16[128,1536]{1,0:T(8,128)(2,1)} async-done(((bf16[1024,1536]{1,0:T(8,128)(2,1)}), bf16[128,1536]{1,0:T(8,128)(2,1)}) %reduce-scatter.11.cloned.1.call-update) | async-done | bytes 393232 | tf_op jit(solution)/shard_map/reduce_scatter | solution.py:599
  288.6 4.6 all-to-all-start.2
  299.3 47.9 %all_gather.28 = bf16[231,1536]{0,1:T(8,128)(2,1)} all-gather(bf16[231,192]{0,1:T(8,128)(2,1)S(1)} %fusion.29), channel_id=1, replica_groups=mesh['grp'=4,'seq'=8] {'seq'}, dimensions={1}, use_global_device_ids=true | all-gather | bytes 798336 | tf_op jit(solution)/shard_map/all_gather | solution.py:709
  356.2 12.4 %all-gather.14.cloned.1.call-done = bf16[1024,1536]{1,0:T(8,128)(2,1)} async-done(((bf16[128,1536]{1,0:T(8,128)(2,1)}), bf16[1024,1536]{1,0:T(8,128)(2,1)}) %all-gather.14.cloned.1.call-update) | async-done | bytes 3145744 | tf_op jit(solution)/shard_map/all_gather | solution.py:595
  372.6 58.3 %all-gather.10.cloned.1.call-done = bf16[1024,1536]{1,0:T(8,128)(2,1)} async-done(((bf16[128,1536]{1,0:T(8,128)(2,1)}), bf16[1024,1536]{1,0:T(8,128)(2,1)}) %all-gather.10.cloned.1.call-update) | async-done | bytes 3145744 | tf_op jit(solution)/shard_map/all_gather | solution.py:595
  437.2 12.8 %fusion.135 = (f32[3,1024]{1,0:T(4,128)S(1)}, f32[3,1024,1255]{1,2,0:T(8,128)}) fusion(pred[1024,1255]{0,1:T(8,128)(4,1)} %broadcast_compare_fusion, bf16[1024,3,64]{0,2,1:T(8,128)(2,1)} %bitcast.158, bf16[1255,3,64]{0,2,1:T(8,128)(2,1)} %bitcast.154), kind=kOutput, calls=%fused_computation.350 | convolution fusion | flops 508908768 | bytes 17593984 | tf_op jit(solution)/shard_map/sub | solution.py:727
  450.0 10.9 fusion.5
  468.4 8.0 multiply_convert_fusion
  479.7 6.3 fusion.138
  494.0 33.6 %all-gather.12.cloned.1.call-done = bf16[1024,1536]{0,1:T(8,128)(2,1)} async-done(((bf16[1024,192]{0,1:T(8,128)(2,1)}), bf16[1024,1536]{0,1:T(8,128)(2,1)}) %all-gather.12.cloned.1.call-update) | async-done | bytes 3145744 | tf_op jit(solution)/shard_map/all_gather | solution.py:732
  530.5 17.7 %all_to_all.70 = bf16[8,128,192]{1,2,0:T(8,128)(2,1)S(1)} all-to-all(bf16[8,128,192]{1,2,0:T(8,128)(2,1)S(1)} %bitcast.152), channel_id=1, replica_groups=mesh['grp'=4,'seq'=8] {'seq'}, dimensions={0} | all-to-all | bytes 786432 | tf_op jit(solution)/shard_map/all_to_all | solution.py:735
  551.5 59.0 %reduce-scatter.13.cloned.1.call-done = bf16[128,1536]{1,0:T(8,128)(2,1)} async-done(((bf16[1024,1536]{1,0:T(8,128)(2,1)}), bf16[128,1536]{1,0:T(8,128)(2,1)}) %reduce-scatter.13.cloned.1.call-update) | async-done | bytes 393232 | tf_op jit(solution)/shard_map/reduce_scatter | solution.py:599
  623.4 53.4 %all-gather.16.cloned.1.call-done = bf16[1024,1536]{1,0:T(8,128)(2,1)} async-done(((bf16[128,1536]{1,0:T(8,128)(2,1)}), bf16[1024,1536]{1,0:T(8,128)(2,1)}) %all-gather.16.cloned.1.call-update) | async-done | bytes 3145744 | tf_op jit(solution)/shard_map/all_gather | solution.py:595
  676.8 7.8 fusion.126
  686.3 14.5 %psum.148 = f32[3,1]{0,1:T(1,128)S(1)} all-reduce(f32[3,1]{0,1:T(1,128)S(1)} %bitcast.173), channel_id=1, replica_groups=mesh['grp'=4,'seq'=8] {'seq'}, use_global_device_ids=true, to_apply=%region_19.20 | all-reduce | flops 3 | bytes 24 | tf_op jit(solution)/shard_map/psum | solution.py:788
  700.8 7.1 fusion.136
  713.0 6.5 convolution_convert_fusion.2
  723.8 6.7 all-to-all-start.3
  739.5 10.0 reduce-scatter.17.cloned.1.call-done
  758.7 95.2 %reduce-scatter.15.cloned.1.call-done = bf16[128,1536]{1,0:T(8,128)(2,1)} async-done(((bf16[1024,1536]{1,0:T(8,128)(2,1)}), bf16[128,1536]{1,0:T(8,128)(2,1)}) %reduce-scatter.15.cloned.1.call-update) | async-done | bytes 393232 | tf_op jit(solution)/shard_map/reduce_scatter | solution.py:599
  861.6 6.4 convolution_convert_fusion.3
  885.5 35.3 %reduce-scatter.21.cloned.1.call-done = f32[384,3]{1,0:T(8,128)} async-done(((f32[3072,3]{1,0:T(8,128)}), f32[384,3]{1,0:T(8,128)}) %reduce-scatter.21.cloned.1.call-update) | async-done | bytes 4624
  932.5 53.9 %reduce-scatter.19.cloned.1.call-done = f32[192,10]{1,0:T(8,128)} async-done(((f32[1536,10]{1,0:T(8,128)}), f32[192,10]{1,0:T(8,128)}) %reduce-scatter.19.cloned.1.call-update) | async-done | bytes 7696
  989.2 14.9 %all-reduce = (bf16[9,192]{1,0:T(8,128)(2,1)}, bf16[192]{0:T(256)(128)(2,1)}, bf16[768]{0:T(1024)(128)(2,1)}, bf16[768]{0:T(1024)(128)(2,1)}, bf16[768]{0:T(1024...) all-reduce(bf16[9,192]{1,0:T(8,128)(2,1)} %bitcast.164, ...), channel_id=1, replica_groups=mesh['grp'=4,'seq'=8] {'grp'}, use_global_device_ids=true, to_apply=%region_58.59 | all-reduce | flops 30144 | bytes 120576 | tf_op jit(solution)/shard_map/psum | solution.py:843
  1023.3 110.3 %all-reduce.4.cloned.1.call-done = (bf16[1536,768]{1,0:T(8,128)(2,1)}, bf16[6144,192]{0,1:T(8,128)(2,1)}, bf16[1280,192]{0,1:T(8,128)(2,1)}, bf16[1536,192]{0,1:...) async-done(((bf16[1536,768]{1,0:T(8,128)(2,1)}, bf16[6144,192]{0,1:T(8,128)(2,1)}, bf16[1280,192]{0,1:T(8,128)(2,1)}, ...) | async-done | bytes 7569424 | tf_op jit(solution)/shard_map/psum | solution.py:843
  (378 shorter events, 218.6 us)
Async XLA Ops:
  7.2 160.9 %copy-start = (bf16[1536,768]{1,0:T(8,128)(2,1)S(1)}, bf16[1536,768]{1,0:T(8,128)(2,1)}, u32[]{:S(2)}) copy-start(bf16[1536,768]{1,0:T(8,128)(2,1)} %param.31) | copy-start | bytes 7077892
  7.2 160.8 %all-gather.8.cloned.1.call-start = ((), (), s32[]{:S(2)}) async-start(), calls=%async_computation.10 | async-start | bytes 3538944 | tf_op jit(solution)/shard_map/all_gather | solution.py:595
  9.3 53.6 %collective-permute-start = (bf16[65,1536]{1,0:T(8,128)(2,1)}, bf16[65,1536]{1,0:T(8,128)(2,1)}, u32[]{:S(2)}, u32[]{:S(2)}) collective-permute-start(bf16[65,1536]{1,0:T(8,128)(2,1)} %get-tuple-element.115), channel_id=1, source_target_pairs={{0,1},{1,2},{2,3},{3,4},{4,5},{5,6},{6,7},{8,9},{9,10},{10,11},{11... | collective-permute-start | bytes 599048 | tf_op jit(solution)/shard_map/ppermute | solution.py:29
  12.4 49.5 %collective-permute-start.1 = (bf16[65,1536]{1,0:T(8,128)(2,1)}, bf16[65,1536]{1,0:T(8,128)(2,1)}, u32[]{:S(2)}, u32[]{:S(2)}) collective-permute-start(bf16[65,1536]{1,0:T(8,128)(2,1)} %get-tuple-element.116), channel_id=1, source_target_pairs={{1,0},{2,1},{3,2},{4,3},{5,4},{6,5},{7,6},{9,8},{10,9},{11,10},{12... | collective-permute-start | bytes 599048 | tf_op jit(solution)/shard_map/ppermute | solution.py:32
  61.2 796.6 %copy-start.48 = (f32[128]{0:T(128)}, f32[128]{0:T(128)S(1)}, u32[]{:S(2)}) copy-start(f32[128]{0:T(128)S(1)} %get-tuple-element.119) | copy-start | bytes 1540
  71.2 128.1 %all-to-all-start = ((bf16[8,768,192]{1,2,0:T(8,128)(2,1)}), bf16[8,768,192]{1,2,0:T(8,128)(2,1)}, u32[]{:S(2)}, u32[]{:S(2)}) async-start(bf16[8,768,192]{1,2,0:T(8,128)(2,1)} %bitcast.133), calls=%async_computation | async-start | bytes 4718592 | tf_op jit(solution)/shard_map/all_to_all | solution.py:672
  79.3 203.5 %reduce-scatter.11.cloned.1.call-start = ((), (), s32[]{:S(2)}) async-start(), calls=%async_computation.11 | async-start | bytes 3538944 | tf_op jit(solution)/shard_map/reduce_scatter | solution.py:599
  79.4 94.9 %copy-start.71 = (f32[768]{0:T(1024)}, f32[768]{0:T(1024)S(1)}, u32[]{:S(2)}) copy-start(f32[768]{0:T(1024)S(1)} %convert_element_type.519) | copy-start | bytes 9220
  205.8 162.9 %all-gather.14.cloned.1.call-start = ((), (), s32[]{:S(2)}) async-start(), calls=%async_computation.14 | async-start | bytes 3538944 | tf_op jit(solution)/shard_map/all_gather | solution.py:595
  206.5 224.4 %all-gather.10.cloned.1.call-start = ((), (), s32[]{:S(2)}) async-start(), calls=%async_computation.12 | async-start | bytes 3538944 | tf_op jit(solution)/shard_map/all_gather | solution.py:595
  288.6 62.7 %all-to-all-start.2 = ((bf16[8,192,192]{2,1,0:T(8,128)(2,1)}), bf16[8,192,192]{2,1,0:T(8,128)(2,1)}, u32[]{:S(2)}, u32[]{:S(2)}) async-start(bf16[8,192,192]{2,1,0:T(8,128)(2,1)} %bitcast.139), calls=%async_computation.3 | async-start | bytes 1572864 | tf_op jit(solution)/shard_map/all_to_all | solution.py:673
  293.2 234.4 %all-gather.12.cloned.1.call-start = ((), (), s32[]{:S(2)}) async-start(), calls=%async_computation.13 | async-start | bytes 3538944 | tf_op jit(solution)/shard_map/all_gather | solution.py:732
  468.4 142.2 %reduce-scatter.13.cloned.1.call-start = ((), (), s32[]{:S(2)}) async-start(), calls=%async_computation.15 | async-start | bytes 3538944 | tf_op jit(solution)/shard_map/reduce_scatter | solution.py:599
  493.4 183.4 %all-gather.16.cloned.1.call-start = ((), (), s32[]{:S(2)}) async-start(), calls=%async_computation.16 | async-start | bytes 3538944 | tf_op jit(solution)/shard_map/all_gather | solution.py:595
  617.3 132.2 %reduce-scatter.17.cloned.1.call-start = ((), (), s32[]{:S(2)}) async-start(), calls=%async_computation.18 | async-start | bytes 1769472 | tf_op jit(solution)/shard_map/reduce_scatter | solution.py:765
  623.3 230.6 %reduce-scatter.15.cloned.1.call-start = ((), (), s32[]{:S(2)}) async-start(), calls=%async_computation.17 | async-start | bytes 3538944 | tf_op jit(solution)/shard_map/reduce_scatter | solution.py:599
  723.8 144.2 %all-to-all-start.3 = ((bf16[768,8,192]{0,2,1:T(8,128)(2,1)}), bf16[768,8,192]{0,2,1:T(8,128)(2,1)}, u32[]{:S(2)}, u32[]{:S(2)}) async-start(bf16[768,8,192]{0,2,1:T(8,128)(2,1)} %bitcast.132), calls=%async_computation.6 | async-start | bytes 4718592 | tf_op jit(solution)/shard_map/all_to_all | solution.py:779
  730.5 190.3 %reduce-scatter.21.cloned.1.call-start = ((), (), s32[]{:S(2)}) async-start(), calls=%async_computation.20 | async-start | bytes 1769472
  756.0 97.9 %copy-start.50 = (f32[128]{0:T(128)S(1)}, f32[128]{0:T(128)}, u32[]{:S(2)}) copy-start(f32[128]{0:T(128)} %copy-done.49) | copy-start | bytes 1540
  756.0 99.5 %copy-start.60 = (f32[128]{0:T(128)S(1)}, f32[128]{0:T(128)}, u32[]{:S(2)}) copy-start(f32[128]{0:T(128)} %copy-done.59) | copy-start | bytes 1540
  756.0 99.5 %copy-start.62 = (f32[128]{0:T(128)S(1)}, f32[128]{0:T(128)}, u32[]{:S(2)}) copy-start(f32[128]{0:T(128)} %copy-done.61) | copy-start | bytes 1540
  756.0 99.5 %copy-start.66 = (f32[128]{0:T(128)S(1)}, f32[128]{0:T(128)}, u32[]{:S(2)}) copy-start(f32[128]{0:T(128)} %copy-done.65) | copy-start | bytes 1540
  756.0 99.5 %copy-start.68 = (f32[128]{0:T(128)S(1)}, f32[128]{0:T(128)}, u32[]{:S(2)}) copy-start(f32[128]{0:T(128)} %copy-done.67) | copy-start | bytes 1540
  758.6 99.2 %copy-start.54 = (f32[128]{0:T(128)S(1)}, f32[128]{0:T(128)}, u32[]{:S(2)}) copy-start(f32[128]{0:T(128)} %copy-done.53) | copy-start | bytes 1540
  758.6 99.2 %copy-start.56 = (f32[128]{0:T(128)S(1)}, f32[128]{0:T(128)}, u32[]{:S(2)}) copy-start(f32[128]{0:T(128)} %copy-done.55) | copy-start | bytes 1540
  758.6 99.2 %copy-start.58 = (f32[128]{0:T(128)S(1)}, f32[128]{0:T(128)}, u32[]{:S(2)}) copy-start(f32[128]{0:T(128)} %copy-done.57) | copy-start | bytes 1540
  758.6 99.2 %copy-start.64 = (f32[128]{0:T(128)S(1)}, f32[128]{0:T(128)}, u32[]{:S(2)}) copy-start(f32[128]{0:T(128)} %copy-done.63) | copy-start | bytes 1540
  758.7 227.7 %reduce-scatter.19.cloned.1.call-start = ((), (), s32[]{:S(2)}) async-start(), calls=%async_computation.19 | async-start | bytes 884736
  861.5 272.1 %all-reduce.4.cloned.1.call-start = ((), (), s32[]{:S(2)}) async-start(), calls=%async_computation.21 | async-start | bytes 15138816 | tf_op jit(solution)/shard_map/psum | solution.py:843
  871.4 147.7 %copy-start.10 = (f32[128,1536]{1,0:T(8,128)S(1)}, f32[128,1536]{1,0:T(8,128)}, u32[]{:S(2)}) copy-start(f32[128,1536]{1,0:T(8,128)} %copy-done.8) | copy-start | bytes 2359300
  923.5 95.5 %collective-permute-start.2 = (bf16[65,1536]{1,0:T(8,128)(2,1)}, bf16[65,1536]{1,0:T(8,128)(2,1)}, u32[]{:S(2)}, u32[]{:S(2)}) collective-permute-start(bf16[65,1536]{1,0:T(8,128)(2,1)} %get-tuple-element.113), channel_id=1, source_target_pairs={{1,0},{2,1},{3,2},{4,3},{5,4},{6,5},{7,6},{9,8},{10,9},{11,10},{12... | collective-permute-start | bytes 599048 | tf_op jit(solution)/shard_map/ppermute | solution.py:32
  926.0 93.0 %collective-permute-start.3 = (bf16[65,1536]{1,0:T(8,128)(2,1)}, bf16[65,1536]{1,0:T(8,128)(2,1)}, u32[]{:S(2)}, u32[]{:S(2)}) collective-permute-start(bf16[65,1536]{1,0:T(8,128)(2,1)} %get-tuple-element.114), channel_id=1, source_target_pairs={{0,1},{1,2},{2,3},{3,4},{4,5},{5,6},{6,7},{8,9},{9,10},{10,11},{11... | collective-permute-start | bytes 599048 | tf_op jit(solution)/shard_map/ppermute | solution.py:29
  (72 other events, 554.7 us)
Sparse Core Ops, SparseCore 0:
  67.9 100.1 all-gather.7
  205.9 76.8 reduce-scatter.10
  285.0 83.6 all-gather.13
  371.3 59.5 all-gather.9
  468.5 59.0 all-gather.11
  531.0 79.4 reduce-scatter.12
  617.4 59.3 all-gather.15
  680.2 69.2 reduce-scatter.16
  754.1 99.7 reduce-scatter.14
  857.6 63.1 reduce-scatter.20
  924.6 61.7 reduce-scatter.18
  991.1 142.4 all-reduce.3

commit v2 on v0

--- a/solution.py
+++ b/solution.py
@@ -1,8 +1,11 @@
+import functools
 import math
 
 import jax
 import jax.numpy as jnp
 from jax import lax
+from jax.experimental import pallas as pl
+from jax.experimental.pallas import tpu as pltpu
 from jax.sharding import PartitionSpec as P
 
 C = 1536
@@ -591,6 +594,1911 @@
     )
 
 
+def mm(left, right):
+    return jnp.dot(left, right, preferred_element_type=jnp.float32)
+
+
+MESH_ID = pl.DeviceIdType.MESH
+
+
+def dot_nt(left, right):
+    return lax.dot_general(
+        left, right, (((1,), (1,)), ((), ())), preferred_element_type=jnp.float32
+    )
+
+
+def place():
+    me = lax.axis_index("seq")
+    z, y = me // 2, lax.rem(me, 2)
+    return me, z, y, me + 1 - 2 * y
+
+
+def seq_copy(src, dst, send, recv, target):
+    return pltpu.make_async_remote_copy(
+        src_ref=src,
+        dst_ref=dst,
+        send_sem=send,
+        recv_sem=recv,
+        device_id={"seq": target},
+        device_id_type=MESH_ID,
+    )
+
+
+def dot_tn(left, right):
+    return lax.dot_general(
+        left, right, (((0,), (0,)), ((), ())), preferred_element_type=jnp.float32
+    )
+
+
+def grp_copy(src, dst, send, recv, target):
+    return pltpu.make_async_remote_copy(
+        src_ref=src,
+        dst_ref=dst,
+        send_sem=send,
+        recv_sem=recv,
+        device_id={"grp": target},
+        device_id_type=MESH_ID,
+    )
+
+
+def group_place():
+    group = lax.axis_index("grp")
+    core = lax.rem(group, 2)
+    return group // 2, core, group + 1 - 2 * core, lax.rem(group + 2, 4)
+
+
+def meet_all(shards, groups=0):
+    me = lax.axis_index("seq")
+    barrier = pltpu.get_barrier_semaphore()
+    for step in range(1, groups):
+        pl.semaphore_signal(
+            barrier,
+            inc=1,
+            device_id={"grp": lax.rem(lax.axis_index("grp") + step, groups)},
+            device_id_type=MESH_ID,
+        )
+    for step in range(1, shards):
+        pl.semaphore_signal(
+            barrier,
+            inc=1,
+            device_id={"seq": lax.rem(me + step, shards)},
+            device_id_type=MESH_ID,
+        )
+    pl.semaphore_wait(barrier, shards - 1 + max(groups - 1, 0))
+
+
+def tile_loop(count, body):
+    def step(index, carry):
+        body(index)
+        return carry
+
+    lax.fori_loop(0, count, step, 0)
+
+
+def add_rows(target, target_row, left, left_row, right, count):
+    def tile(index):
+        low = index * 32
+        here = pl.ds(pl.multiple_of(target_row + low, 32), 32)
+        there = pl.ds(pl.multiple_of(left_row + low, 32), 32)
+        value = left[there, :].astype(jnp.float32) + right[
+            pl.ds(pl.multiple_of(low, 32), 32), :
+        ].astype(jnp.float32)
+        target[here, :] = value.astype(target.dtype)
+
+    tile_loop(count // 32, tile)
+
+
+class PairSum:
+    def __init__(self, own, got, other, out, sems):
+        x, core, self.core_peer, self.x_peer = group_place()
+        self.half = own.shape[0] // 2
+        self.own, self.got, self.other, self.out = own, got, other, out
+        self.low = pl.multiple_of(core * self.half, self.half)
+        mine = pl.ds(self.low, self.half)
+        theirs = pl.ds(pl.multiple_of((1 - core) * self.half, self.half), self.half)
+        pair = lambda k: (sems.at[0, k], sems.at[1, k])
+        self.copies = (
+            grp_copy(own.at[theirs], got, *pair(0), self.core_peer),
+            grp_copy(own.at[mine], other, *pair(1), self.x_peer),
+            grp_copy(out.at[mine], out.at[mine], *pair(2), self.core_peer),
+        )
+
+    def begin(self):
+        self.copies[0].start()
+
+    def across(self):
+        self.copies[0].wait_recv()
+        add_rows(self.own, self.low, self.own, self.low, self.got, self.half)
+        self.copies[1].start()
+
+    def share(self):
+        self.copies[1].wait_recv()
+        add_rows(self.out, self.low, self.own, self.low, self.other, self.half)
+        self.copies[2].start()
+
+    def finish(self):
+        self.copies[2].wait_recv()
+        for copy in self.copies:
+            copy.wait_send()
+
+
+class QuarterSum:
+    def __init__(self, shards, own, got, other, out, sems):
+        x, core, core_peer, x_peer = group_place()
+        me = lax.axis_index("seq")
+        units, width = own.shape[2], own.shape[3]
+        self.own, self.got, self.other, self.out = own, got, other, out
+        self.core, self.shards = core, shards
+        self.mine = x * 2 + core
+        pair = lambda k: (sems.at[0, k], sems.at[1, k])
+
+        def rows(quarter):
+            return pl.ds(pl.multiple_of(quarter * units, units), units)
+
+        self.block = (rows(self.mine), pl.ds(pl.multiple_of(me * width, 128), width))
+        self.me = me
+        self.first = [
+            grp_copy(own.at[:, side * 2 + 1 - core], got.at[side], *pair(side), core_peer)
+            for side in (0, 1)
+        ]
+        self.second = grp_copy(own.at[:, (1 - x) * 2 + core], other, *pair(2), x_peer)
+        self.third = []
+        for step in range(1, shards):
+            goal = lax.rem(me + step, shards)
+            self.third.append(
+                seq_copy(own.at[goal, self.mine], out.at[self.block], *pair(2 + step), goal)
+            )
+        base = 2 + shards
+        whole = out.at[rows(self.mine)]
+        self.fourth = grp_copy(whole, whole, *pair(base), x_peer)
+        self.fifth = []
+        for side in (0, 1):
+            whole = out.at[rows(side * 2 + core)]
+            self.fifth.append(grp_copy(whole, whole, *pair(base + 1 + side), core_peer))
+
+    def add(self, quarter, right):
+        def tile(index):
+            self.own[index, quarter] = (
+                self.own[index, quarter].astype(jnp.float32) + right(index).astype(jnp.float32)
+            ).astype(self.own.dtype)
+
+        tile_loop(self.shards, tile)
+
+    def begin(self):
+        for copy in self.first:
+            copy.start()
+
+    def across(self):
+        for copy in self.first:
+            copy.wait_recv()
+        for side in (0, 1):
+            self.add(side * 2 + self.core, lambda index, side=side: self.got[side, index])
+        self.second.start()
+
+    def spread(self):
+        self.second.wait_recv()
+        self.add(self.mine, lambda index: self.other[index])
+        for copy in self.third:
+            copy.start()
+        self.out[self.block] = self.own[self.me, self.mine]
+
+    def share(self):
+        for copy in self.third:
+            copy.wait_recv()
+        self.fourth.start()
+
+    def share_core(self):
+        self.fourth.wait_recv()
+        for copy in self.fifth:
+            copy.start()
+
+    def finish(self):
+        for copy in self.fifth:
+            copy.wait_recv()
+        for copy in (*self.first, self.second, *self.third, self.fourth, *self.fifth):
+            copy.wait_send()
+
+
+def in_line(direction, z, hops, depth):
+    return z >= hops if direction == 0 else z + hops < depth
+
+
+class Gather:
+    def __init__(self, full, sems, depth):
+        self.full, self.depth = full, depth
+        self.sems = [sems.at[k] for k in range(4)]
+        self.me, self.z, self.y, self.other = place()
+
+    def origin(self, direction, hops, far):
+        column = 1 - self.y if far else self.y
+        return (self.z - hops if direction == 0 else self.z + hops) * 2 + column
+
+    def z_copy(self, direction, hops):
+        block = self.full.at[self.origin(direction, hops, False)]
+        send, recv = self.sems[0], self.sems[1]
+        target = self.me + 2 if direction == 0 else self.me - 2
+        return seq_copy(
+            block, block, send.at[direction, hops], recv.at[direction, hops + 1], target
+        )
+
+    def z_arrival(self, direction, hops):
+        block = self.full.at[self.origin(direction, hops, False)]
+        send, recv = self.sems[0], self.sems[1]
+        return seq_copy(
+            block, block, send.at[direction, hops], recv.at[direction, hops], self.other
+        )
+
+    def y_copy(self, direction, hops, arrival=False):
+        block = self.full.at[self.origin(direction, hops, arrival)]
+        send, recv = self.sems[2], self.sems[3]
+        return seq_copy(
+            block, block, send.at[direction, hops], recv.at[direction, hops], self.other
+        )
+
+    def here(self, direction, hops):
+        return in_line(direction, self.z, hops, self.depth)
+
+    def onward(self, direction):
+        return self.z < self.depth - 1 if direction == 0 else self.z > 0
+
+    def start(self):
+        for direction in (0, 1):
+
+            @pl.when(self.onward(direction))
+            def _():
+                self.z_copy(direction, 0).start()
+
+        self.y_copy(0, 0).start()
+
+    def hop(self, hops):
+        for direction in (0, 1):
+
+            @pl.when((hops < self.depth) & self.here(direction, hops))
+            def _():
+                self.z_arrival(direction, hops).wait_recv()
+
+                @pl.when(self.onward(direction))
+                def _():
+                    self.z_copy(direction, hops).start()
+
+                self.y_copy(direction, hops).start()
+
+    def near(self, hops, visit):
+        for direction in (0, 1):
+
+            @pl.when((hops < self.depth) & self.here(direction, hops))
+            def _():
+                visit(self.origin(direction, hops, False))
+
+    def far(self, hops, visit):
+        for direction in (0, 1):
+            here = self.here(direction, hops)
+            if direction == 1:
+                here = here & (hops > 0)
+
+            @pl.when(here)
+            def _():
+                self.y_copy(direction, hops, True).wait_recv()
+                visit(self.origin(direction, hops, True))
+
+    def drain(self):
+        def step(hops, carry):
+            for direction in (0, 1):
+                here = self.here(direction, hops)
+
+                @pl.when(here & self.onward(direction))
+                def _():
+                    self.z_copy(direction, hops).wait_send()
+
+                if direction == 1:
+                    here = here & (hops > 0)
+
+                @pl.when(here)
+                def _():
+                    self.y_copy(direction, hops).wait_send()
+
+            return carry
+
+        lax.fori_loop(0, self.depth, step, 0)
+
+    def finish(self):
+        tile_loop(self.depth, lambda hops: self.far(hops, lambda block: None))
+        self.drain()
+
+    def run(self, visit, hook=None):
+        self.start()
+        visit(self.me)
+
+        def step(hops, carry):
+            self.hop(hops)
+            self.near(hops, visit)
+            self.far(hops - 1, visit)
+            if hook is not None:
+                hook(hops)
+            return carry
+
+        lax.fori_loop(1, self.depth + 1, step, 0)
+        self.drain()
+
+
+class Reshard:
+    def __init__(self, shards, part, out, local_sem, sems):
+        x, core, core_peer, x_peer = group_place()
+        me = lax.axis_index("seq")
+        mine = x * 2 + core
+        pair = lambda k: (sems.at[0, k], sems.at[1, k])
+        self.local = pltpu.make_async_copy(part(me, mine), out.at[me, mine], local_sem)
+        self.first = []
+        for step in range(1, shards):
+            goal = lax.rem(me + step, shards)
+            self.first.append(seq_copy(part(goal, mine), out.at[me, mine], *pair(step - 1), goal))
+        self.second = grp_copy(out.at[:, mine], out.at[:, mine], *pair(shards - 1), x_peer)
+        self.third = []
+        for side in (0, 1):
+            whole = out.at[:, side * 2 + core]
+            self.third.append(grp_copy(whole, whole, *pair(shards + side), core_peer))
+
+    def begin(self):
+        self.local.start()
+        for copy in self.first:
+            copy.start()
+
+    def share(self):
+        self.local.wait()
+        for copy in self.first:
+            copy.wait_recv()
+        self.second.start()
+
+    def share_core(self):
+        self.second.wait_recv()
+        for copy in self.third:
+            copy.start()
+
+    def finish(self):
+        for copy in self.third:
+            copy.wait_recv()
+        for copy in (*self.first, self.second, *self.third):
+            copy.wait_send()
+
+
+def side_by_side(target, row, parts, count):
+    for pair in range(count // 2):
+        value = jnp.concatenate([parts(2 * pair), parts(2 * pair + 1)], axis=1)
+        rows, cols = value.shape
+        target[row : row + rows, pair * cols : (pair + 1) * cols] = value
+
+
+def scatter_blocks(
+    partial, to_y, from_y, to_z, from_z, acc, y_sems, z_sems, depth, between=None, hook=None
+):
+    me, z, y, other = place()
+    low = to_y.dtype
+
+    def y_copy(goal):
+        return seq_copy(
+            to_y.at[goal], from_y.at[goal], y_sems.at[0, goal], y_sems.at[1, goal], other
+        )
+
+    def z_copy(direction, goal):
+        return seq_copy(
+            to_z.at[goal],
+            from_z.at[direction, goal],
+            z_sems.at[0, direction, goal],
+            z_sems.at[1, direction, goal],
+            me + 2 if direction == 0 else me - 2,
+        )
+
+    def z_arrival(direction, goal):
+        return seq_copy(
+            to_z.at[goal],
+            from_z.at[direction, goal],
+            z_sems.at[0, direction, goal],
+            z_sems.at[1, direction, goal],
+            other,
+        )
+
+    def ahead(direction, hops):
+        return in_line(1 - direction, z, hops, depth)
+
+    def goal_of(direction, hops):
+        return z + hops if direction == 0 else z - hops
+
+    def over_y(step, carry):
+        hops = depth - 1 - step
+        for direction in (0, 1):
+            here = ahead(direction, hops)
+            if direction == 1:
+                here = here & (hops > 0)
+
+            @pl.when(here)
+            def _():
+                goal = goal_of(direction, hops)
+                to_y[goal] = partial(goal * 2 + other - z * 2).astype(low)
+                y_copy(goal).start()
+
+        return carry
+
+    lax.fori_loop(0, depth, over_y, 0)
+    if between is not None:
+        between()
+
+    def along_z(step, carry):
+        hops = depth - 1 - step
+        for direction in (0, 1):
+
+            @pl.when(ahead(direction, hops))
+            def _():
+                goal = goal_of(direction, hops)
+                acc[...] = partial(goal * 2 + y)
+                y_copy(goal).wait_recv()
+                acc[...] += from_y[goal].astype(jnp.float32)
+
+                @pl.when(in_line(direction, z, 1, depth))
+                def _():
+                    z_arrival(direction, goal).wait_recv()
+                    acc[...] += from_z[direction, goal].astype(jnp.float32)
+
+                to_z[goal] = acc[...].astype(low)
+                z_copy(direction, goal).start()
+
+        if hook is not None:
+            hook(step)
+        return carry
+
+    lax.fori_loop(0, depth - 1, along_z, 0)
+    acc[...] = partial(me)
+    y_copy(z).wait_recv()
+    acc[...] += from_y[z].astype(jnp.float32)
+    for direction in (0, 1):
+
+        @pl.when(in_line(direction, z, 1, depth))
+        def _():
+            z_arrival(direction, z).wait_recv()
+            acc[...] += from_z[direction, z].astype(jnp.float32)
+
+    def drain(goal, carry):
+        y_copy(goal).wait_send()
+        for direction in (0, 1):
+            sent = goal > z if direction == 0 else goal < z
+
+            @pl.when(sent)
+            def _():
+                z_copy(direction, goal).wait_send()
+
+        return carry
+
+    lax.fori_loop(0, depth, drain, 0)
+
+
+def peer_total(mine, theirs, sems, shards, meanwhile=None):
+    me = lax.axis_index("seq")
+    copies = [
+        seq_copy(
+            mine,
+            theirs.at[step - 1],
+            sems.at[0, step - 1],
+            sems.at[1, step - 1],
+            lax.rem(me + step, shards),
+        )
+        for step in range(1, shards)
+    ]
+    for copy in copies:
+        copy.start()
+    if meanwhile is not None:
+        meanwhile()
+    for copy in copies:
+        copy.wait()
+    total = mine[...]
+    for step in range(1, shards):
+        total = total + theirs[step - 1]
+    return total
+
+
+EDGE = 80
+VMEM_BYTES = 56 * 1024 * 1024
+ROOT_HALF = math.sqrt(0.5)
+DENSITY = 1.0 / math.sqrt(2.0 * math.pi)
+
+
+def exchange_edges(held, sems, rows, shards):
+    me = lax.axis_index("seq")
+
+    def copy(kind):
+        if kind == 0:
+            source, target = pl.ds(EDGE + rows - WMAX, WMAX), pl.ds(EDGE - WMAX, WMAX)
+        else:
+            source, target = pl.ds(EDGE, WMAX), pl.ds(EDGE + rows, WMAX)
+        return seq_copy(
+            held.at[source],
+            held.at[target],
+            sems.at[0, kind],
+            sems.at[1, kind],
+            me + 1 if kind == 0 else me - 1,
+        )
+
+    first, last = me == 0, me == shards - 1
+    zeros = jnp.zeros((EDGE, held.shape[1]), held.dtype)
+
+    held[pl.ds(0, EDGE - WMAX), :] = zeros[: EDGE - WMAX]
+    held[pl.ds(EDGE + rows + WMAX, EDGE - WMAX), :] = zeros[: EDGE - WMAX]
+
+    @pl.when(first)
+    def _():
+        held[pl.ds(EDGE - WMAX, WMAX), :] = zeros[:WMAX]
+
+    @pl.when(last)
+    def _():
+        held[pl.ds(EDGE + rows, WMAX), :] = zeros[:WMAX]
+
+    @pl.when(jnp.logical_not(last))
+    def _():
+        copy(0).start()
+
+    @pl.when(jnp.logical_not(first))
+    def _():
+        copy(1).start()
+
+    def finish():
+        @pl.when(jnp.logical_not(last))
+        def _():
+            copy(0).wait_send()
+            copy(1).wait_recv()
+
+        @pl.when(jnp.logical_not(first))
+        def _():
+            copy(1).wait_send()
+            copy(0).wait_recv()
+
+    return finish
+
+
+VEC_STEP = 256
+VEC_TAIL = 8 * VEC_STEP
+
+
+def column_of(row):
+    return jnp.broadcast_to(row, (8, row.shape[1])).T[:, 0:1]
+
+
+def stats_of(values_in):
+    average = jnp.mean(values_in, axis=-1, keepdims=True)
+    centred = values_in - average
+    variance = jnp.mean(centred * centred, axis=-1, keepdims=True)
+    inverse = lax.rsqrt(variance + EPS_NORM)
+    return centred * inverse, inverse
+
+
+class Latents:
+    def __init__(self, shape, total):
+        self.ends = []
+        low = 0
+        for latent in range(NLAT - 1):
+            low = low + shape[latent, 0] * WMAX
+            self.ends.append(low)
+        self.total = total
+
+    def segment(self, positions):
+        out = jnp.zeros_like(positions)
+        for end in self.ends:
+            out = out + (positions >= end).astype(jnp.int32)
+        return out
+
+    def picks(self, start, count):
+        segment = self.segment(start + lax.broadcasted_iota(jnp.int32, (count, 1), 0))
+        return [(segment == latent).astype(jnp.float32) for latent in range(NLAT)]
+
+    def valid(self, positions, down_step, side_step):
+        segment = self.segment(positions)
+        low, high = jnp.zeros_like(positions), jnp.full_like(positions, self.total)
+        for latent, end in enumerate(self.ends):
+            low = jnp.where(segment > latent, end, low)
+            high = jnp.where(segment == latent, end, high)
+        moved = positions + down_step * WMAX
+        column = (positions & (WMAX - 1)) + side_step
+        good = (moved >= low) & (moved < high) & (column >= 0) & (column < WMAX)
+        return good.astype(jnp.float32)
+
+
+def rows_of(picks, table):
+    out = picks[0] * table[0:1]
+    for latent in range(1, NLAT):
+        out = out + picks[latent] * table[latent : latent + 1]
+    return out
+
+
+WIDE_SCALE, WIDE_SHIFT = 16, 24
+SMALL_FC1, SMALL_GAMMA, SMALL_BETA, SMALL_TIME = 64, 66, 68, 70
+SMALL_QUERY, SMALL_VALUE, SMALL_OUT, SMALL_MAP, SMALL_ROWS = 71, 72, 73, 74, 80
+
+
+def mixer_kernel(
+    shards,
+    shape,
+    hidden,
+    cond,
+    time_weight,
+    conv_weight,
+    vec,
+    fc1,
+    ctx_cols,
+    cot,
+    fc2,
+    out_weight,
+    full,
+    held,
+    wide,
+    normed,
+    inverse,
+    pre,
+    root_out,
+    ratio_out,
+    denom_out,
+    response,
+    ctx_full,
+    cot_full,
+    fc2_rows,
+    out_rows,
+    pack,
+    packed,
+    floats,
+    conv,
+    act,
+    energy,
+    mine,
+    theirs,
+    edge_sems,
+    pack_sems,
+    gather_sems,
+    total_sems,
+    ctx_sems,
+    cot_sems,
+    out_parts,
+    local_sems,
+    fc2_sems,
+    out_sems,
+):
+    f32 = jnp.float32
+    rows = hidden.shape[0]
+    depth = shards // 2
+    me = lax.axis_index("seq")
+    meet_all(shards, lax.axis_size("grp"))
+    units, width = fc2_rows.shape[2:]
+    out_units = out_parts.shape[2]
+
+    def fc2_part(goal, quarter):
+        here = pl.ds(pl.multiple_of(quarter * units, units), units)
+        return fc2.at[here, pl.ds(pl.multiple_of(goal * width, 128), width)]
+
+    def out_part(goal, quarter):
+        low = (goal * 4 + quarter) * out_units
+        return out_weight.at[pl.ds(pl.multiple_of(low, out_units), out_units)]
+
+    fc2_shard = Reshard(shards, fc2_part, fc2_rows, local_sems.at[0], fc2_sems)
+    out_shard = Reshard(shards, out_part, out_parts, local_sems.at[1], out_sems)
+    ctx_gather = Gather(ctx_full, ctx_sems, depth)
+    cot_gather = Gather(cot_full, cot_sems, depth)
+    ctx_full[me] = ctx_cols[...]
+    cot_full[me] = cot[...]
+    latents = Latents(shape, shards * rows)
+    cols = pack.shape[1]
+    width_one = fc1.shape[1]
+    fc1_bias, gamma, beta = (vec[:, n * width_one : (n + 1) * width_one] for n in range(3))
+    vec_at = lambda n: vec[:, 3 * width_one + n * VEC_STEP : 3 * width_one + n * VEC_STEP + cols]
+    time_bias = vec[:, 3 * width_one + 6 * VEC_STEP : 3 * width_one + 6 * VEC_STEP + 2 * cols]
+    mod = (
+        jnp.dot(
+            cond[...],
+            time_weight[...].astype(f32),
+            precision=HIGHEST_PRECISION,
+            preferred_element_type=f32,
+        )
+        + time_bias
+    )
+    pack[...] = jnp.zeros_like(pack)
+    pack[0:9, :] = conv_weight[...].astype(f32)
+    pack[9:10, :] = vec_at(0)
+    pack[10:11, :] = vec_at(1)
+    pack[11 : 11 + NLAT, :] = mod[:, :cols]
+    pack[11 + NLAT : 11 + 2 * NLAT, :] = mod[:, cols:]
+    packed[me] = pack[...]
+    pack_copies = [
+        seq_copy(
+            pack,
+            packed.at[me],
+            pack_sems.at[0, step - 1],
+            pack_sems.at[1, step - 1],
+            lax.rem(me + step, shards),
+        )
+        for step in range(1, shards)
+    ]
+    held[pl.ds(EDGE, rows), :] = hidden[...]
+    finish = exchange_edges(held, edge_sems, rows, shards)
+    for copy in pack_copies:
+        copy.start()
+    finish()
+    fc2_shard.begin()
+    out_shard.begin()
+    ctx_gather.start()
+    cot_gather.start()
+    tile_loop(
+        floats.shape[0] // 32,
+        lambda i: floats.__setitem__(
+            (pl.ds(i * 32, 32), slice(None)), held[pl.ds(i * 32, 32), :].astype(f32)
+        ),
+    )
+    for copy in pack_copies:
+        copy.wait()
+    wide[...] = jnp.zeros_like(wide)
+    wide[0:16, :] = jnp.concatenate([packed[j, 0:16, :] for j in range(shards)], axis=1)
+    for low, device in ((WIDE_SCALE, 0), (WIDE_SHIFT, shards // 2)):
+        parts = []
+        for j in range(device, device + shards // 2):
+            parts.append(packed[j, 11 : 11 + NLAT, :])
+            parts.append(packed[j, 11 + NLAT : 11 + 2 * NLAT, :])
+        wide[low : low + NLAT, :] = jnp.concatenate(parts, axis=1)
+    positions = me * rows + lax.broadcasted_iota(jnp.int32, (rows, 1), 0)
+    masks = [latents.valid(positions, tap // 3 - 1, tap % 3 - 1) for tap in range(9)]
+
+    def conv_tile(index):
+        cols = pl.ds(pl.multiple_of(index * 256, 256), 256)
+        total = jnp.broadcast_to(wide[9:10, cols], (rows, 256))
+        for tap in range(9):
+            offset = EDGE + (tap // 3 - 1) * WMAX + tap % 3 - 1
+            total = total + (
+                floats[offset : offset + rows, cols] * wide[tap : tap + 1, cols]
+            ) * masks[tap]
+        conv[:, cols] = total
+
+    tile_loop(C // 256, conv_tile)
+
+    def norm_tile(index):
+        here = pl.ds(pl.multiple_of(index * 16, 16), 16)
+        values, factor = stats_of(conv[here, :])
+        normed[here, :] = values
+        inverse[here, :] = factor
+        full[me, here, :] = values.astype(full.dtype)
+
+    tile_loop(rows // 16, norm_tile)
+    energy[...] = jnp.zeros_like(energy)
+
+    def visit(block):
+        pre[block] = (
+            jnp.dot(full[block], fc1[...], preferred_element_type=f32) + fc1_bias
+        )
+
+        def tile(index):
+            here = pl.ds(pl.multiple_of(index * 32, 32), 32)
+            value = pre[block, here, :]
+            value = value * (0.5 * (1.0 + lax.erf(value * ROOT_HALF)))
+            act[block, here, :] = value
+            square = value * value
+            pick = latents.picks(block * rows + index * 32, 32)
+            for latent in range(NLAT):
+                energy[latent : latent + 1, :] += jnp.sum(
+                    square * pick[latent], axis=0, keepdims=True
+                )
+
+        tile_loop(rows // 32, tile)
+
+    def hook(hops):
+        @pl.when(hops == 1)
+        def _():
+            ctx_gather.hop(1)
+
+        @pl.when(hops == 2)
+        def _():
+            fc2_shard.share()
+            out_shard.share()
+            ctx_gather.hop(2)
+            cot_gather.hop(1)
+
+        @pl.when(hops == 3)
+        def _():
+            ctx_gather.hop(3)
+
+    Gather(full, gather_sems, depth).run(visit, hook)
+    cot_gather.hop(2)
+    fc2_shard.share_core()
+    out_shard.share_core()
+    root = jnp.sqrt(energy[...] + 1.0)
+    mine[...] = jnp.broadcast_to(jnp.sum(root, axis=1, keepdims=True), mine.shape)
+    denom = peer_total(mine, theirs, total_sems, shards) / FF + EPS_NORM
+    ratio = root / denom[:, 0:1]
+    cot_gather.hop(3)
+    root_out[...] = root
+    denom_out[...] = denom
+    ratio_out[...] = ratio
+    scaled = ratio * gamma + 1.0
+
+    def respond(index):
+        block = index // (rows // 32)
+        here = pl.ds(pl.multiple_of(lax.rem(index, rows // 32) * 32, 32), 32)
+        response[block, here, :] = (
+            act[block, here, :] * rows_of(latents.picks(index * 32, 32), scaled) + beta
+        ).astype(response.dtype)
+
+    tile_loop(shards * rows // 32, respond)
+    ctx_gather.finish()
+    fc2_shard.finish()
+    out_shard.finish()
+    for quarter in range(4):
+        side_by_side(
+            out_rows, quarter * out_units, lambda j, quarter=quarter: out_parts[j, quarter], shards
+        )
+    cot_gather.finish()
+
+
+def mixed_in_kernel(
+    shards,
+    shape,
+    response,
+    fc2,
+    hidden,
+    wide,
+    w_qkv,
+    vec,
+    context,
+    full,
+    first,
+    second,
+    normed,
+    inverse,
+    queries,
+    keys,
+    values,
+    acc,
+    to_y,
+    from_y,
+    to_z,
+    from_z,
+    y_sems,
+    z_sems,
+    gather_sems,
+):
+    f32 = jnp.float32
+    rows = hidden.shape[0]
+    depth = shards // 2
+    me = lax.axis_index("seq")
+    meet_all(shards)
+    latents = Latents(shape, shards * rows)
+    cols = keys.shape[0]
+    base = vec.shape[1] - VEC_TAIL
+    q_bias = vec[:, base + 2 * VEC_STEP : base + 2 * VEC_STEP + cols]
+    v_bias = column_of(vec[:, base + 3 * VEC_STEP : base + 4 * VEC_STEP])[:cols]
+    bias = wide[10:11, :]
+    scale, shift = wide[WIDE_SCALE : WIDE_SCALE + 8, :], wide[WIDE_SHIFT : WIDE_SHIFT + 8, :]
+
+    def partial(block):
+        return dot_nt(response[block], fc2[...])
+
+    scatter_blocks(partial, to_y, from_y, to_z, from_z, acc, y_sems, z_sems, depth)
+
+    def norm_tile(index):
+        here = pl.ds(pl.multiple_of(index * 16, 16), 16)
+        one = hidden[here, :].astype(f32) + acc[here, :] + bias
+        pick = latents.picks(me * rows + index * 16, 16)
+        two = one * (1.0 + rows_of(pick, scale)) + rows_of(pick, shift)
+        first[here, :] = one
+        second[here, :] = two
+        value, factor = stats_of(two)
+        normed[here, :] = value
+        inverse[here, :] = factor
+        full[me, here, :] = value.astype(full.dtype)
+
+    tile_loop(rows // 16, norm_tile)
+
+    side = jnp.dot(w_qkv[cols:, :], context[...], preferred_element_type=f32)
+    keys[:, shards * rows :] = side[:cols].astype(keys.dtype)
+    values[:, shards * rows :] = (side[cols:] + v_bias).astype(values.dtype)
+
+    def visit(block):
+        value = full[block]
+        query = dot_nt(value, w_qkv[:cols, :]) + q_bias
+        queries[block] = query.astype(queries.dtype)
+        here = pl.ds(pl.multiple_of(block * rows, 128), rows)
+        side = dot_nt(w_qkv[cols:, :], value)
+        keys[:, here] = side[:cols].astype(keys.dtype)
+        values[:, here] = (side[cols:] + v_bias).astype(values.dtype)
+
+    Gather(full, gather_sems, depth).run(visit)
+
+
+def attend_kernel(
+    shards,
+    shape,
+    queries,
+    keys,
+    values,
+    cot,
+    out_rows,
+    d_qkv,
+    mixed,
+    cot_cols,
+    dk_sum,
+    dv_sum,
+    probs_at,
+    sems,
+):
+    f32, bf16 = jnp.float32, jnp.bfloat16
+    cols = keys.shape[0]
+    heads = cols // HEAD_DIM
+    tiles, tile_rows = mixed.shape[0], mixed.shape[3]
+    span = tile_rows // queries.shape[1]
+    depth = shards // 2
+    me = lax.axis_index("seq")
+    meet_all(shards)
+    latents = Latents(shape, tiles * tile_rows)
+    place_at = lax.broadcasted_iota(jnp.int32, (1, keys.shape[1]), 1)
+    token = place_at - tiles * tile_rows
+    of_token = jnp.full_like(token, -1)
+    for latent in range(NLAT):
+        inside = (token >= latent * NCTX) & (token < (latent + 1) * NCTX)
+        of_token = jnp.where(inside, latent, of_token)
+    k_segment = jnp.where(token < 0, latents.segment(place_at), of_token)
+    dk_sum[...] = jnp.zeros_like(dk_sum)
+    dv_sum[...] = jnp.zeros_like(dv_sum)
+
+    def gather_of(tile):
+        return Gather(mixed.at[tile], sems.at[tile], depth)
+
+    def step(tile, carry):
+        blocks = pl.ds(tile * span, span)
+        here = pl.ds(pl.multiple_of(tile * tile_rows, 128), tile_rows)
+        query = queries[blocks].reshape(tile_rows, cols) * SCORE_SCALE
+        cot_tile = cot[blocks].reshape(tile_rows, C)
+        for j in range(shards):
+
+            @pl.when(me == j)
+            def _():
+                cot_cols[:, here] = cot_tile[:, j * cols : (j + 1) * cols].T
+
+        d_mixed = dot_nt(cot_tile, out_rows[...]).astype(bf16)
+        q_segment = latents.segment(
+            tile * tile_rows + lax.broadcasted_iota(jnp.int32, (tile_rows, 1), 0)
+        )
+        bias = jnp.where(q_segment == k_segment, 0.0, MASKED)
+        mixed_parts, d_query_parts = [], []
+        for head in range(heads):
+            own = slice(head * HEAD_DIM, (head + 1) * HEAD_DIM)
+            scores = jnp.dot(query[:, own], keys[own, :], preferred_element_type=f32) + bias
+            expo = jnp.exp(scores - jnp.max(scores, axis=-1, keepdims=True))
+            probs_at[head] = expo * (1.0 / jnp.sum(expo, axis=-1, keepdims=True))
+            mixed_parts.append(dot_nt(probs_at[head].astype(bf16), values[own, :]))
+        mixed[tile, me] = jnp.concatenate(mixed_parts, axis=1).T.astype(bf16)
+        gather_of(tile).start()
+        for hops in range(1, depth):
+
+            @pl.when(tile >= hops)
+            def _():
+                gather_of(tile - hops).hop(hops)
+
+        for head in range(heads):
+            own = slice(head * HEAD_DIM, (head + 1) * HEAD_DIM)
+            dm_head = d_mixed[:, own]
+            delta = jnp.sum(dm_head.astype(f32) * mixed_parts[head], axis=-1, keepdims=True)
+            d_probs = jnp.dot(dm_head, values[own, :], preferred_element_type=f32)
+            d_scores = (probs_at[head] * (d_probs - delta)).astype(bf16)
+            d_query_parts.append(dot_nt(d_scores, keys[own, :]) * SCORE_SCALE)
+            dk_sum[own, :] += dot_tn(query[:, own], d_scores)
+            dv_sum[own, :] += dot_tn(dm_head, probs_at[head].astype(bf16))
+        d_qkv[:cols, here] = jnp.concatenate(d_query_parts, axis=1).T.astype(bf16)
+        return carry
+
+    lax.fori_loop(0, tiles, step, 0)
+    for late in range(1, depth):
+        for hops in range(late, depth):
+            gather_of(tiles - 1 + late - hops).hop(hops)
+    d_qkv[:cols, tiles * tile_rows :] = jnp.zeros(
+        (cols, d_qkv.shape[1] - tiles * tile_rows), bf16
+    )
+    d_qkv[cols : 2 * cols, :] = dk_sum[...].astype(bf16)
+    d_qkv[2 * cols :, :] = dv_sum[...].astype(bf16)
+
+    def close(tile, carry):
+        gather_of(tile).finish()
+        return carry
+
+    lax.fori_loop(0, tiles, close, 0)
+
+
+def norm_back(gradient, normed, inverse):
+    mean_grad = jnp.mean(gradient, axis=-1, keepdims=True)
+    mean_mixed = jnp.mean(gradient * normed, axis=-1, keepdims=True)
+    return inverse * (gradient - mean_grad - normed * mean_mixed)
+
+
+def attn_back_kernel(
+    shards,
+    shape,
+    cond,
+    d_qkv,
+    w_qkv,
+    attn,
+    context,
+    mixed,
+    cot_cols,
+    out_weight,
+    vec,
+    second,
+    cot,
+    normed,
+    inverse,
+    first,
+    wide,
+    context_in,
+    fc2,
+    pre,
+    root,
+    ratio,
+    denom,
+    full,
+    d_first,
+    d_pre,
+    small,
+    map_grad,
+    weight_grads,
+    activations,
+    d_mod,
+    acc,
+    d_resp,
+    act,
+    slope,
+    sums,
+    mine,
+    theirs,
+    to_y,
+    from_y,
+    to_z,
+    from_z,
+    y_sems,
+    z_sems,
+    gather_sems,
+    total_sems,
+    g_own,
+    g_got,
+    g_other,
+    g_sems,
+    ctx_out,
+    ctx_in,
+    ctx_sems,
+    mod_in,
+    mod_sems,
+    act_out,
+    act_in,
+    act_sems,
+):
+    f32 = jnp.float32
+    rows = cot.shape[0]
+    depth = shards // 2
+    me = lax.axis_index("seq")
+    meet_all(shards, lax.axis_size("grp"))
+    cols = ctx_out.shape[1]
+    total = shards * rows
+    latents = Latents(shape, total)
+    base = vec.shape[1] - VEC_TAIL
+    width_one = base // 3
+    gamma = vec[:, width_one : 2 * width_one]
+    out_bias = column_of(vec[:, base + 4 * VEC_STEP : base + 5 * VEC_STEP])[:cols]
+    scale = wide[WIDE_SCALE : WIDE_SCALE + 8, :]
+    weight_sum = PairSum(g_own, g_got, g_other, weight_grads, g_sems)
+    peers = [lax.rem(me + step, shards) for step in range(1, shards)]
+    ctx_copies = [
+        seq_copy(ctx_out.at[peer], ctx_in.at[me], ctx_sems.at[0, k], ctx_sems.at[1, k], peer)
+        for k, peer in enumerate(peers)
+    ]
+
+    act_copies = [
+        seq_copy(
+            act_out.at[:, pl.ds(pl.multiple_of(peer * rows, 128), rows)],
+            act_in.at[me],
+            act_sems.at[0, k],
+            act_sems.at[1, k],
+            peer,
+        )
+        for k, peer in enumerate(peers)
+    ]
+
+    def partial(block):
+        here = pl.ds(pl.multiple_of(block * rows, 128), rows)
+        return dot_tn(d_qkv[:, here], w_qkv[...])
+
+    def between():
+        low_type = ctx_out.dtype
+        for device in range(shards):
+            ctx_out[device] = dot_tn(
+                w_qkv[:, device * cols : (device + 1) * cols], d_qkv[:, total:]
+            ).astype(low_type)
+        ctx_in[me] = ctx_out[me]
+        g_own[: 3 * cols, :] = (
+            jnp.dot(d_qkv[:, :total], attn[...].reshape(total, C), preferred_element_type=f32)
+            + dot_nt(d_qkv[:, total:], context[...])
+        ).astype(low_type)
+        grad = None
+        for tile in range(mixed.shape[0]):
+            here = slice(tile * mixed.shape[3], (tile + 1) * mixed.shape[3])
+            block = mixed[tile].reshape(C, mixed.shape[3])
+            act_out[:, here] = (
+                jnp.dot(out_weight[...], block, preferred_element_type=f32) + out_bias
+            ).astype(low_type)
+            part = dot_nt(cot_cols[:, here], block)
+            grad = part if grad is None else grad + part
+        g_own[3 * cols :, :] = grad.astype(low_type)
+        weight_sum.begin()
+        act_in[me] = act_out[:, pl.ds(pl.multiple_of(me * rows, 128), rows)]
+
+    def scatter_hook(step):
+        @pl.when(step == 1)
+        def _():
+            weight_sum.across()
+
+    scatter_blocks(
+        partial, to_y, from_y, to_z, from_z, acc, y_sems, z_sems, depth, between, scatter_hook
+    )
+    d_mod[...] = jnp.zeros_like(d_mod)
+
+    def norm_tile(index):
+        here = pl.ds(pl.multiple_of(index * 16, 16), 16)
+        d_second = cot[here, :].astype(f32) + norm_back(
+            acc[here, :], normed[here, :], inverse[here, :]
+        )
+        pick = latents.picks(me * rows + index * 16, 16)
+        value = d_second * (1.0 + rows_of(pick, scale))
+        d_first[here, :] = value
+        full[me, here, :] = value.astype(full.dtype)
+        scaled = d_second * first[here, :]
+        for latent in range(NLAT):
+            chosen = pick[latent]
+            d_mod[2 * latent : 2 * latent + 1, :] += jnp.sum(scaled * chosen, axis=0, keepdims=True)
+            d_mod[2 * latent + 1 : 2 * latent + 2, :] += jnp.sum(
+                d_second * chosen, axis=0, keepdims=True
+            )
+
+    tile_loop(rows // 16, norm_tile)
+    sums[...] = jnp.zeros_like(sums)
+    wide_mod = 2 * cols
+    half = shards // 2
+
+    def mod_part(device):
+        low = pl.multiple_of(lax.rem(device, half) * wide_mod, 128)
+        return d_mod.at[:, pl.ds(low, wide_mod)]
+
+    mod_in[me] = mod_part(me)[...]
+    mod_copies = [
+        seq_copy(mod_part(peer), mod_in.at[me], mod_sems.at[0, k], mod_sems.at[1, k], peer)
+        for k, peer in enumerate(peers)
+    ]
+    for copy in mod_copies:
+        copy.start()
+
+    def gather_hook(hops):
+        @pl.when(hops == 2)
+        def _():
+            weight_sum.share()
+
+    def visit(block):
+        d_resp[block] = jnp.dot(full[block], fc2[...], preferred_element_type=f32)
+
+        def tile(index):
+            here = pl.ds(pl.multiple_of(index * 32, 32), 32)
+            value = pre[block, here, :]
+            phi = 0.5 * (1.0 + lax.erf(value * ROOT_HALF))
+            slope[block, here, :] = phi + value * (DENSITY * jnp.exp(-0.5 * value * value))
+            value = value * phi
+            act[block, here, :] = value
+            pull = d_resp[block, here, :]
+            sums[NLAT : NLAT + 1, :] += jnp.sum(pull, axis=0, keepdims=True)
+            pull = pull * value
+            pick = latents.picks(block * rows + index * 32, 32)
+            for latent in range(NLAT):
+                sums[latent : latent + 1, :] += jnp.sum(
+                    pull * pick[latent], axis=0, keepdims=True
+                )
+
+        tile_loop(rows // 32, tile)
+
+    Gather(full, gather_sems, depth).run(visit, gather_hook)
+    small[...] = jnp.zeros_like(small)
+    wide_row = 2 * cols
+
+    def keep(row, value):
+        for part in range(value.shape[1] // wide_row):
+            small[row + part : row + part + 1, :] = value[
+                :, part * wide_row : (part + 1) * wide_row
+            ]
+
+    keep(SMALL_BETA, sums[NLAT : NLAT + 1, :])
+    pulls = sums[...]
+    keep(SMALL_GAMMA, jnp.sum(pulls[:NLAT] * ratio[:NLAT, :], axis=0, keepdims=True))
+    d_ratio = pulls * gamma
+    mine[...] = jnp.broadcast_to(jnp.sum(d_ratio * root[...], axis=1, keepdims=True), mine.shape)
+
+    def meanwhile():
+        for copy in (*ctx_copies, *act_copies):
+            copy.start()
+
+    pulled = peer_total(mine, theirs, total_sems, shards, meanwhile)[:, 0:1]
+    below = denom[:, 0:1]
+    d_root = d_ratio / below - pulled / (FF * below * below)
+    back = d_root / root[...]
+    scaled = ratio[...] * gamma + 1.0
+    sums[0:1, :] = jnp.zeros((1, width_one), f32)
+
+    def respond(index):
+        block = index // (rows // 32)
+        here = pl.ds(pl.multiple_of(lax.rem(index, rows // 32) * 32, 32), 32)
+        pick = latents.picks(index * 32, 32)
+        d_act = d_resp[block, here, :] * rows_of(pick, scaled) + act[block, here, :] * rows_of(
+            pick, back
+        )
+        value = (d_act * slope[block, here, :]).astype(d_pre.dtype)
+        d_pre[block, here, :] = value
+        sums[0:1, :] += jnp.sum(value.astype(f32), axis=0, keepdims=True)
+
+    tile_loop(shards * rows // 32, respond)
+    for copy in (*ctx_copies, *mod_copies, *act_copies):
+        copy.wait()
+    activations[...] = (second[...] + act_in[...].reshape(C, rows).astype(f32).T).astype(
+        activations.dtype
+    )
+    context_sum = ctx_in[0].astype(f32)
+    mod_sum = mod_in[0]
+    for device in range(1, shards):
+        context_sum = context_sum + ctx_in[device].astype(f32)
+        mod_sum = mod_sum + mod_in[device]
+    keep(SMALL_FC1, sums[0:1, :])
+    at = lax.broadcasted_iota(jnp.int32, (1, context.shape[1]), 1)
+    context_sum = jnp.where(at < NLAT * NCTX, context_sum, 0.0)
+    map_grad[...] = jnp.dot(
+        context_sum.astype(map_grad.dtype), context_in[...], preferred_element_type=f32
+    ).astype(map_grad.dtype)
+    chosen = [
+        jnp.where(me < half, mod_sum[2 * n : 2 * n + 1], mod_sum[2 * n + 1 : 2 * n + 2])
+        for n in range(NLAT)
+    ]
+    chosen = jnp.concatenate(chosen, axis=0)
+    small[0:SMALL_FC1, :] = lax.dot_general(
+        cond[...],
+        chosen,
+        (((0,), (0,)), ((), ())),
+        precision=HIGHEST_PRECISION,
+        preferred_element_type=f32,
+    )
+    keep(SMALL_TIME, jnp.sum(chosen, axis=0, keepdims=True))
+    ones = lambda values: jnp.ones((8, values.shape[1]), values.dtype)
+    for row, value in (
+        (SMALL_QUERY, d_qkv[:cols, :]),
+        (SMALL_VALUE, d_qkv[2 * cols :, :]),
+        (SMALL_OUT, cot_cols[...]),
+    ):
+        small[row : row + 1, :cols] = dot_nt(ones(value), value)[0:1]
+    small[SMALL_MAP : SMALL_MAP + 1, :cols] = lax.dot_general(
+        ones(context_sum),
+        context_sum,
+        (((1,), (1,)), ((), ())),
+        precision=HIGHEST_PRECISION,
+        preferred_element_type=f32,
+    )[0:1]
+    weight_sum.finish()
+
+
+def conv_back_kernel(
+    shards,
+    shape,
+    d_pre,
+    fc1,
+    normed,
+    inverse,
+    d_first,
+    hidden,
+    wide,
+    normed_full,
+    response,
+    branch,
+    map_grad,
+    small,
+    input_grad,
+    fc1_sum,
+    fc2_sum,
+    map_sum,
+    small_sum,
+    conv_sum,
+    held,
+    floats,
+    acc,
+    to_y,
+    from_y,
+    to_z,
+    from_z,
+    y_sems,
+    z_sems,
+    edge_sems,
+    d_conv_params,
+    fc1_own,
+    fc1_got,
+    fc1_other,
+    fc2_own,
+    fc2_got,
+    fc2_other,
+    map_own,
+    map_got,
+    map_other,
+    pair_sems,
+    fc2_sems,
+    small_in,
+    small_sems,
+    conv_out,
+    conv_in,
+    conv_part,
+    conv_group,
+    conv_sems,
+):
+    f32 = jnp.float32
+    rows = normed.shape[0]
+    depth = shards // 2
+    groups = lax.axis_size("grp")
+    me = lax.axis_index("seq")
+    meet_all(shards, groups)
+    cols = conv_part.shape[1]
+    units, width = fc2_own.shape[2:]
+    total = shards * rows
+    latents = Latents(shape, total)
+    positions = me * rows + lax.broadcasted_iota(jnp.int32, (rows, 1), 0)
+    fc1_pair = PairSum(fc1_own, fc1_got, fc1_other, fc1_sum, pair_sems.at[0])
+    map_pair = PairSum(map_own, map_got, map_other, map_sum, pair_sems.at[1])
+    fc2_quarter = QuarterSum(shards, fc2_own, fc2_got, fc2_other, fc2_sum, fc2_sems)
+    group = lax.axis_index("grp")
+    small_copies = [
+        grp_copy(
+            small,
+            small_in.at[step - 1],
+            small_sems.at[0, step - 1],
+            small_sems.at[1, step - 1],
+            lax.rem(group + step, groups),
+        )
+        for step in range(1, groups)
+    ]
+
+    def partial(block):
+        return dot_nt(d_pre[block], fc1[...])
+
+    def between():
+        map_own[...] = map_grad[...]
+        map_pair.begin()
+        for copy in small_copies:
+            copy.start()
+        right = response[...].reshape(total, width)
+        for goal in range(0, shards, 4):
+            here = slice(goal * 4 * units, (goal + 4) * 4 * units)
+            part = dot_tn(branch[:, :, here].reshape(total, 16 * units), right)
+            fc2_own[goal : goal + 4] = part.reshape(4, 4, units, width).astype(fc2_own.dtype)
+        fc2_quarter.begin()
+
+        def tile(index):
+            here = pl.ds(pl.multiple_of(index * 256, 256), 256)
+            fc1_own[here, :] = dot_tn(
+                normed_full[:, :, here].reshape(total, 256),
+                d_pre[...].reshape(total, width),
+            ).astype(fc1_own.dtype)
+
+        tile_loop(C // 256, tile)
+        fc1_pair.begin()
+
+    def scatter_hook(step):
+        @pl.when(step == 0)
+        def _():
+            fc2_quarter.across()
+            fc1_pair.across()
+
+        @pl.when(step == 2)
+        def _():
+            fc2_quarter.spread()
+            map_pair.across()
+
+    scatter_blocks(
+        partial, to_y, from_y, to_z, from_z, acc, y_sems, z_sems, depth, between, scatter_hook
+    )
+
+    def norm_tile(index):
+        start = pl.multiple_of(index * 16, 16)
+        here = pl.ds(start, 16)
+        held[pl.ds(EDGE + start, 16), :] = norm_back(
+            acc[here, :], normed[here, :], inverse[here, :]
+        ).astype(held.dtype)
+
+    tile_loop(rows // 16, norm_tile)
+    finish = exchange_edges(held, edge_sems, rows, shards)
+    tile_loop(
+        floats.shape[0] // 32,
+        lambda i: floats.__setitem__(
+            (pl.ds(i * 32, 32), slice(None)), hidden[pl.ds(i * 32, 32), :].astype(f32)
+        ),
+    )
+    d_conv_params[...] = jnp.zeros_like(d_conv_params)
+    masks = [latents.valid(positions, tap // 3 - 1, tap % 3 - 1) for tap in range(9)]
+
+    def grad_tile(index):
+        cols = pl.ds(pl.multiple_of(index * 256, 256), 256)
+        d_conv = held[pl.ds(EDGE, rows), cols].astype(f32)
+        d_conv_params[9:10, cols] = jnp.sum(d_conv, axis=0, keepdims=True)
+        d_conv_params[10:11, cols] = jnp.sum(branch[me, :, cols].astype(f32), axis=0, keepdims=True)
+        for tap in range(9):
+            offset = EDGE + (tap // 3 - 1) * WMAX + tap % 3 - 1
+            d_conv_params[tap : tap + 1, cols] = jnp.sum(
+                d_conv * floats[offset : offset + rows, cols] * masks[tap],
+                axis=0,
+                keepdims=True,
+            )
+
+    tile_loop(C // 256, grad_tile)
+    for goal in range(shards):
+        conv_out[goal] = d_conv_params[:, goal * cols : (goal + 1) * cols]
+    conv_in[me] = conv_out[me]
+    conv_copies = []
+    for step in range(1, shards):
+        goal = lax.rem(me + step, shards)
+        conv_copies.append(
+            seq_copy(
+                conv_out.at[goal],
+                conv_in.at[me],
+                conv_sems.at[0, step - 1],
+                conv_sems.at[1, step - 1],
+                goal,
+            )
+        )
+        conv_copies[-1].start()
+    finish()
+    fc2_quarter.share()
+    tile_loop(
+        floats.shape[0] // 32,
+        lambda i: floats.__setitem__(
+            (pl.ds(i * 32, 32), slice(None)), held[pl.ds(i * 32, 32), :].astype(f32)
+        ),
+    )
+
+    back_masks = []
+    for tap in range(9):
+        down_step, side_step = tap // 3 - 1, tap % 3 - 1
+        back_masks.append(
+            latents.valid(positions - down_step * WMAX - side_step, down_step, side_step)
+        )
+
+    def input_tile(index):
+        cols = pl.ds(pl.multiple_of(index * 256, 256), 256)
+        total = d_first[:, cols]
+        for tap in range(9):
+            offset = EDGE - (tap // 3 - 1) * WMAX - tap % 3 + 1
+            total = total + (
+                floats[offset : offset + rows, cols] * wide[tap : tap + 1, cols]
+            ) * back_masks[tap]
+        input_grad[:, cols] = total
+
+    for copy in conv_copies:
+        copy.wait()
+    conv_total = conv_in[0]
+    for device in range(1, shards):
+        conv_total = conv_total + conv_in[device]
+    conv_part[...] = conv_total
+    group_copies = []
+    for step in range(1, groups):
+        k = shards - 2 + step
+        group_copies.append(
+            grp_copy(
+                conv_part,
+                conv_group.at[step - 1],
+                conv_sems.at[0, k],
+                conv_sems.at[1, k],
+                lax.rem(group + step, groups),
+            )
+        )
+        group_copies[-1].start()
+    tile_loop(C // 256, input_tile)
+    fc1_pair.share()
+    map_pair.share()
+    fc2_quarter.share_core()
+    for copy in (*small_copies, *group_copies):
+        copy.wait()
+    small_sum[...] = small[...] + small_in[0] + small_in[1] + small_in[2]
+    conv_sum[...] = conv_part[...] + conv_group[0] + conv_group[1] + conv_group[2]
+    fc1_pair.finish()
+    map_pair.finish()
+    fc2_quarter.finish()
+
+
+def kernel_call(body, name, number, outs, scratch, operands, flops=0, far=(), scalars=()):
+    vmem, anywhere, smem = (
+        pl.BlockSpec(memory_space=space) for space in (pltpu.VMEM, pl.ANY, pltpu.SMEM)
+    )
+    space_of = lambda k: anywhere if k in far else smem if k in scalars else vmem
+    shapes = [jax.ShapeDtypeStruct(shape, dtype) for shape, dtype in outs]
+    moved = sum(math.prod(s.shape) * s.dtype.itemsize for s in shapes) + sum(
+        x.size * x.dtype.itemsize for x in operands
+    )
+    return pl.pallas_call(
+        body,
+        out_shape=shapes,
+        in_specs=[space_of(k) for k in range(len(operands))],
+        out_specs=[vmem] * len(shapes),
+        scratch_shapes=scratch,
+        name=name,
+        cost_estimate=pl.CostEstimate(flops=flops, bytes_accessed=moved, transcendentals=0),
+        compiler_params=pltpu.CompilerParams(
+            collective_id=number, has_side_effects=True, vmem_limit_bytes=VMEM_BYTES
+        ),
+    )(*operands)
+
+
+def scatter_scratch(rows, depth):
+    bf16 = jnp.bfloat16
+    return [
+        pltpu.VMEM((depth, rows, C), bf16),
+        pltpu.VMEM((depth, rows, C), bf16),
+        pltpu.VMEM((depth, rows, C), bf16),
+        pltpu.VMEM((2, depth, rows, C), bf16),
+        pltpu.SemaphoreType.DMA((2, depth)),
+        pltpu.SemaphoreType.DMA((2, 2, depth)),
+    ]
+
+
+def gather_scratch(depth):
+    return pltpu.SemaphoreType.DMA((4, 2, depth + 1))
+
+
+def total_scratch(shards):
+    return [
+        pltpu.VMEM((8, 128), jnp.float32),
+        pltpu.VMEM((shards - 1, 8, 128), jnp.float32),
+    ], pltpu.SemaphoreType.DMA((2, shards - 1))
+
+
+def on_device_heads(
+    hidden,
+    latent_shape,
+    cond_r,
+    clip,
+    cotangent,
+    conv_weight,
+    conv_bias,
+    fc1_weight,
+    fc1_bias,
+    grn_gamma,
+    grn_beta,
+    fc2_weight,
+    fc2_bias,
+    time_weight,
+    time_bias,
+    map_weight,
+    map_bias,
+    query_weight,
+    query_bias,
+    key_weight,
+    value_weight,
+    value_bias,
+    out_weight,
+    out_bias,
+):
+    f32, bf16 = jnp.float32, jnp.bfloat16
+    shards = lax.axis_size("seq")
+    rows = hidden.shape[0]
+    total = rows * shards
+    cols = C // shards
+    depth = shards // 2
+    hidden_cols = FF // shards
+    shape = latent_shape[0]
+    slot = lambda item: jnp.pad(item, (0, VEC_STEP - item.shape[0]))
+    vec = jnp.concatenate(
+        [
+            fc1_bias,
+            grn_gamma,
+            grn_beta,
+            *(slot(item) for item in (conv_bias, fc2_bias, query_bias, value_bias, out_bias)),
+            slot(map_bias),
+            jnp.pad(time_bias, (0, 2 * VEC_STEP - time_bias.shape[0])),
+        ]
+    ).astype(f32)[None]
+    w_qkv = jnp.concatenate([query_weight.T, key_weight.T, value_weight.T], axis=0)
+    ctx_rows = 256
+    context_in = jax.nn.silu(clip.reshape(NLAT * NCTX, CLIP).astype(f32)).astype(bf16)
+    context_in = jnp.pad(context_in, ((0, ctx_rows - NLAT * NCTX), (0, 0)))
+    ctx_cols = (against(map_weight.T, context_in) + map_bias.astype(f32)[:, None]).astype(bf16)
+    units = cols // 4
+    vmem = pltpu.VMEM
+    total_vmem, total_sems = total_scratch(shards)
+    (
+        normed_full,
+        held,
+        wide,
+        normed_one,
+        inverse_one,
+        pre_act,
+        root,
+        ratio,
+        denom,
+        response,
+        context,
+        cot_full,
+        shrink_parts,
+        output_rows,
+    ) = kernel_call(
+        functools.partial(mixer_kernel, shards),
+        "mixer",
+        1,
+        [
+            ((shards, rows, C), bf16),
+            ((rows + 2 * EDGE, C), bf16),
+            ((32, C), f32),
+            ((rows, C), f32),
+            ((rows, 1), f32),
+            ((shards, rows, hidden_cols), f32),
+            ((8, hidden_cols), f32),
+            ((8, hidden_cols), f32),
+            ((8, 128), f32),
+            ((shards, rows, hidden_cols), bf16),
+            ((shards, cols, ctx_rows), bf16),
+            ((shards, rows, C), bf16),
+            ((shards, 4, units, hidden_cols), bf16),
+            ((cols, C), bf16),
+        ],
+        [
+            vmem((24, cols), f32),
+            vmem((shards, 24, cols), f32),
+            vmem((rows + 2 * EDGE, C), f32),
+            vmem((rows, C), f32),
+            vmem((shards, rows, hidden_cols), f32),
+            vmem((8, hidden_cols), f32),
+            *total_vmem,
+            pltpu.SemaphoreType.DMA((2, 2)),
+            pltpu.SemaphoreType.DMA((2, shards - 1)),
+            gather_scratch(depth),
+            total_sems,
+            gather_scratch(depth),
+            gather_scratch(depth),
+            vmem((shards, 4, units, cols), bf16),
+            pltpu.SemaphoreType.DMA((2,)),
+            pltpu.SemaphoreType.DMA((2, shards + 2)),
+            pltpu.SemaphoreType.DMA((2, shards + 2)),
+        ],
+        (
+            shape,
+            hidden,
+            cond_r,
+            time_weight,
+            conv_weight,
+            vec,
+            fc1_weight,
+            ctx_cols,
+            cotangent,
+            fc2_weight.T,
+            out_weight,
+        ),
+        flops=2 * total * C * hidden_cols,
+        far=(9, 10),
+        scalars=(0,),
+    )
+    context = context.reshape(C, ctx_rows)
+    shrink_rows = shrink_parts.reshape(C, hidden_cols)
+    keys_all = total + ctx_rows
+    (
+        attn_blocks,
+        first_sum,
+        second_sum,
+        normed_two,
+        inverse_two,
+        queries,
+        keys,
+        values,
+    ) = kernel_call(
+        functools.partial(mixed_in_kernel, shards),
+        "mixed_in",
+        2,
+        [
+            ((shards, rows, C), bf16),
+            ((rows, C), f32),
+            ((rows, C), f32),
+            ((rows, C), f32),
+            ((rows, 1), f32),
+            ((shards, rows, cols), bf16),
+            ((cols, keys_all), bf16),
+            ((cols, keys_all), bf16),
+        ],
+        [pltpu.VMEM((rows, C), f32), *scatter_scratch(rows, depth), gather_scratch(depth)],
+        (
+            shape,
+            response,
+            shrink_rows,
+            hidden,
+            wide,
+            w_qkv,
+            vec,
+            context,
+        ),
+        flops=2 * total * C * (hidden_cols + 3 * cols),
+        scalars=(0,),
+    )
+
+    tiles, tile_rows = 4, total // 4
+    d_qkv, mixed_full, cot_cols = kernel_call(
+        functools.partial(attend_kernel, shards),
+        "attend",
+        5,
+        [
+            ((3 * cols, keys_all), bf16),
+            ((tiles, shards, cols, tile_rows), bf16),
+            ((cols, total), bf16),
+        ],
+        [
+            vmem((cols, keys_all), f32),
+            vmem((cols, keys_all), f32),
+            vmem((cols // HEAD_DIM, tile_rows, keys_all), f32),
+            pltpu.SemaphoreType.DMA((tiles, 4, 2, depth + 1)),
+        ],
+        (
+            shape,
+            queries,
+            keys,
+            values,
+            cot_full,
+            output_rows,
+        ),
+        flops=12 * total * keys_all * 3 * 256,
+        scalars=(0,),
+    )
+    (
+        branch_blocks,
+        d_first,
+        d_pre,
+        small,
+        grad_map_w,
+        weight_sums,
+        activations,
+    ) = kernel_call(
+        functools.partial(attn_back_kernel, shards),
+        "attn_back",
+        3,
+        [
+            ((shards, rows, C), bf16),
+            ((rows, C), f32),
+            ((shards, rows, hidden_cols), bf16),
+            ((SMALL_ROWS, 2 * cols), f32),
+            ((cols, CLIP), bf16),
+            ((4 * cols, C), bf16),
+            ((rows, C), bf16),
+        ],
+        [
+            vmem((8, C), f32),
+            pltpu.VMEM((rows, C), f32),
+            pltpu.VMEM((shards, rows, hidden_cols), f32),
+            pltpu.VMEM((shards, rows, hidden_cols), f32),
+            pltpu.VMEM((shards, rows, hidden_cols), f32),
+            pltpu.VMEM((8, hidden_cols), f32),
+            *total_vmem,
+            *scatter_scratch(rows, depth),
+            gather_scratch(depth),
+            total_sems,
+            vmem((4 * cols, C), bf16),
+            vmem((2 * cols, C), bf16),
+            vmem((2 * cols, C), bf16),
+            pltpu.SemaphoreType.DMA((2, 3)),
+            vmem((shards, cols, ctx_rows), bf16),
+            vmem((shards, cols, ctx_rows), bf16),
+            pltpu.SemaphoreType.DMA((2, shards - 1)),
+            vmem((shards, 8, 2 * cols), f32),
+            pltpu.SemaphoreType.DMA((2, shards - 1)),
+            vmem((cols, total), bf16),
+            vmem((shards, cols, rows), bf16),
+            pltpu.SemaphoreType.DMA((2, shards - 1)),
+        ],
+        (
+            shape,
+            cond_r,
+            d_qkv,
+            w_qkv,
+            attn_blocks,
+            context,
+            mixed_full,
+            cot_cols,
+            out_weight.T,
+            vec,
+            second_sum,
+            cotangent,
+            normed_two,
+            inverse_two,
+            first_sum,
+            wide,
+            context_in,
+            shrink_rows,
+            pre_act,
+            root,
+            ratio,
+            denom,
+        ),
+        flops=2 * total * C * (hidden_cols + 6 * cols),
+        scalars=(0,),
+    )
+    groups = lax.axis_size("grp")
+    input_grad, fc1_sum, fc2_sum, map_sum, small, conv_small = kernel_call(
+        functools.partial(conv_back_kernel, shards),
+        "conv_back",
+        4,
+        [
+            ((rows, C), f32),
+            ((C, hidden_cols), bf16),
+            ((cols, FF), bf16),
+            ((cols, CLIP), bf16),
+            ((SMALL_ROWS, 2 * cols), f32),
+            ((16, cols), f32),
+        ],
+        [
+            vmem((rows + 2 * EDGE, C), bf16),
+            vmem((rows + 2 * EDGE, C), f32),
+            vmem((rows, C), f32),
+            *scatter_scratch(rows, depth),
+            pltpu.SemaphoreType.DMA((2, 2)),
+            vmem((16, C), f32),
+            vmem((C, hidden_cols), bf16),
+            vmem((C // 2, hidden_cols), bf16),
+            vmem((C // 2, hidden_cols), bf16),
+            vmem((shards, 4, units, hidden_cols), bf16),
+            vmem((2, shards, units, hidden_cols), bf16),
+            vmem((shards, units, hidden_cols), bf16),
+            vmem((cols, CLIP), bf16),
+            vmem((cols // 2, CLIP), bf16),
+            vmem((cols // 2, CLIP), bf16),
+            pltpu.SemaphoreType.DMA((2, 2, 3)),
+            pltpu.SemaphoreType.DMA((2, 5 + shards)),
+            vmem((groups - 1, SMALL_ROWS, 2 * cols), f32),
+            pltpu.SemaphoreType.DMA((2, groups - 1)),
+            vmem((shards, 16, cols), f32),
+            vmem((shards, 16, cols), f32),
+            vmem((16, cols), f32),
+            vmem((groups - 1, 16, cols), f32),
+            pltpu.SemaphoreType.DMA((2, shards + groups - 2)),
+        ],
+        (
+            shape,
+            d_pre,
+            fc1_weight,
+            normed_one,
+            inverse_one,
+            d_first,
+            held,
+            wide,
+            normed_full,
+            response,
+            branch_blocks,
+            grad_map_w,
+            small,
+        ),
+        flops=6 * total * C * hidden_cols,
+        scalars=(0,),
+    )
+    two = lambda row: small[row : row + 2].reshape(hidden_cols)
+    one = lambda row: small[row, :cols]
+    part = lambda k: weight_sums[k * cols : (k + 1) * cols].astype(f32).T
+    return (
+        activations,
+        input_grad,
+        conv_small[:9],
+        conv_small[9],
+        fc1_sum.astype(f32),
+        two(SMALL_FC1),
+        two(SMALL_GAMMA),
+        two(SMALL_BETA),
+        fc2_sum.astype(f32).T,
+        conv_small[10],
+        small[:SMALL_FC1],
+        small[SMALL_TIME],
+        map_sum.astype(f32).T,
+        one(SMALL_MAP),
+        part(0),
+        one(SMALL_QUERY),
+        part(1),
+        part(2),
+        one(SMALL_VALUE),
+        part(3),
+        one(SMALL_OUT),
+    )
+
+
 def solution(mesh):
     in_specs = (
         P(("grp", "seq"), None),
@@ -641,6 +2549,7 @@
         P(None, "seq"),
         P("seq"),
     )
+    by_heads = mesh.shape["seq"] == 8 and mesh.shape["grp"] == 4
     return jax.shard_map(
-        on_device, mesh=mesh, in_specs=in_specs, out_specs=out_specs, check_vma=False
-    )
+        on_device_heads if by_heads else on_device, mesh=mesh, in_specs=in_specs, out_specs=out_specs, check_vma=False
+    )

time: 3970 us -> 501 us (0.13)
  waiting for transfers between devices: 3110 us -> 0 us
  Pallas kernels: 0 us -> 456 us
  blocking collectives: 384 us -> 0 us
  matrix products: 269 us -> 1.01 us
  other arithmetic: 86.6 us -> 14.4 us
    reduce_scatter x8 -> x0, waiting for transfers between devices: 2020 us -> none  [the longest x1 606 us: on_device(): lax.psum_scatter(gradients[6], 'seq', scatter_dimension=1, tiled=True)]
    all_gather x11 -> x0, waiting for transfers between devices: 934 us -> none  [the longest x1 304 us: on_device(): lax.all_gather(fc2_weight, 'seq', axis=1, tiled=True)]
    pallas_call x0 -> x5, Pallas kernels: none -> 456 us  [kernel_call(): pl.pallas_call(body, out_shape=shapes, in_specs=[space_of(k) for k in ran...]
    all_gather x8 -> x0, blocking collectives: 292 us -> none  [the longest x1 69.1 us: on_device(): lax.all_gather(fc1_bias, 'seq', axis=0, tiled=True)]
    dot_general x40 -> x0, matrix products: 231 us -> none  [the longest x6 53.2 us: outer_sum(): lax.dot_general(left_low, right_low, (((0,), (0,)), ((), ())), preferred_...]
    psum x3 -> x0, waiting for transfers between devices: 136 us -> none  [the longest x1 125 us: on_device(): lax.psum(shares[2].astype(jnp.bfloat16), 'grp').astype(jnp.float32)]
    unnamed x2 -> x0, blocking collectives: 78.5 us -> none
    convert_element_type x46 -> x4, other arithmetic: 52.2 us -> 5.96 us  [the longest x1 4.36 us: on_device_heads(): fc1_sum.astype(f32)]
  transfers between devices with their start and end apart: 27 -> 0, of which waited for: 21 -> 0; matrix products, arithmetic and copies ran while one was open for 8% -> 0% of each run, Pallas kernels for 0% -> 0%
where the time goes in v2:
time: 501 us; the launch traced here: 493 us
  Pallas kernels  456 us (91%)
  local copies, waits for them, and re-layouts  20.6 us (4%)
  other arithmetic  14.4 us (3%)
    pallas_call x5, Pallas kernels, kernel_call(): pl.pallas_call(body, out_shape=shapes, in_specs=[space_of(k) for k in ran...  456 us

profile of v2, /device:TPU:9, one launch (start us, length us, event | category | flops | bytes accessed | tf_op | source)
XLA Modules:
  0.0 492.9 jit_solution(9866551978153129061)
XLA Ops:
  0.7 0.8 pad.27
  1.4 0.7 pad.28
  2.1 0.7 pad.29
  2.8 0.7 pad.30
  3.4 0.7 pad.31
  4.1 0.7 pad.32
  4.7 0.7 pad.33
  5.4 0.7 convert_element_type.51
  6.1 1.3 copy.49.shape
  7.4 0.7 constant_dynamic-update-slice_fusion.9
  8.1 0.7 constant_dynamic-update-slice_fusion.8
  8.8 0.7 constant_dynamic-update-slice_fusion.7
  9.6 0.6 convert_element_type.47.vec
  10.2 2.2 copy.46.out_weight
  12.9 1.0 fusion.1.ctx_cols
  13.9 0.9 pad.34.context_in
  14.8 1.3 pad_maximum_fusion.w_qkv
  16.1 118.2 %mixer.1 = (bf16[8,128,1536]{2,1,0:T(8,128)(2,1)}, bf16[288,1536]{1,0:T(8,128)(2,1)}, f32[32,1536]{1,0:T(8,128)}, f32[128,1536]{1,0:T(8,128)}, f32[128,1]{1,0:T(...) custom-call(s32[3,2]{1,0:T(4,128)} %copy.49.shape, ...), custom_call_target="tpu_custom_call" | custom-call | flops 2415919104 | bytes 22931096 | tf_op jit(solution)/shard_map/mixer/pallas_call | solution.py:2116
  134.3 76.7 %mixed_in.1 = (bf16[8,128,1536]{2,1,0:T(8,128)(2,1)}, f32[128,1536]{1,0:T(8,128)}, f32[128,1536]{1,0:T(8,128)}, f32[128,1536]{1,0:T(8,128)}, f32[128,1]{1,0:T(8,...) custom-call(s32[3,2]{1,0:T(4,128)} %copy.49.shape, ...), custom_call_target="tpu_custom_call" | custom-call | flops 4227858432 | bytes 13977112 | tf_op jit(solution)/shard_map/mixed_in/pallas_call | solution.py:2116
  211.1 53.4 %attend.1 = (bf16[576,1280]{1,0:T(8,128)(2,1)}, bf16[4,8,192,256]{3,2,1,0:T(8,128)(2,1)}, bf16[192,1024]{1,0:T(8,128)(2,1)}) custom-call(s32[3,2]{1,0:T(4,128)} %copy.49.shape, bf16[8,128,192]{2,1,0:T(8,128)(2,1)} %get-tuple-element.63.queries, bf16[192,1280]{1,0:T(8,128)(2,1)} %get-tuple-element.64.keys, bf16[192,1280]{1,0:T(8,128)(2,1)} %get-tuple-element.65.values, ...), custom_call_target="tpu_custom_call" | custom-call | flops 12079595520 | bytes 10125336 | tf_op jit(solution)/shard_map/attend/pallas_call | solution.py:2116
  264.5 118.3 %attn_back.1 = (bf16[8,128,1536]{2,1,0:T(8,128)(2,1)}, f32[128,1536]{1,0:T(8,128)}, bf16[8,128,768]{2,1,0:T(8,128)(2,1)}, f32[80,384]{1,0:T(8,128)}, bf16[192,12...) custom-call(s32[3,2]{1,0:T(4,128)} %copy.49.shape, f32[3,64]{1,0:T(4,128)} %cond.3, ...), custom_call_target="tpu_custom_call" | custom-call | flops 6039797760 | bytes 29358360 | tf_op jit(solution)/shard_map/attn_back/pallas_call | solution.py:2116
  382.8 89.1 %conv_back.1 = (f32[128,1536]{1,0:T(8,128)}, bf16[1536,768]{1,0:T(8,128)(2,1)}, bf16[192,6144]{1,0:T(8,128)(2,1)}, bf16[192,1280]{1,0:T(8,128)(2,1)}, f32[80,384]{1,0:T(8,128)}, /*index=5*/f32[16,192]{1,0:T(8,128)}) custom-call(s32[3,2]{1,0:T(4,128)} %copy.49.shape, bf16[8,128,768]{2,1,0:T(8,128)(2,1)} %get-tuple-element.81.d_pre, bf16[1536,768]{1,0:T(8,128)(2,1)} %fc1.3, ...), custom_call_target="tpu_custom_call" | custom-call | flops 7247757312 | bytes 21197336 | tf_op jit(solution)/shard_map/conv_back/pallas_call | solution.py:2116
  472.0 1.3 slice_reduce_fusion
  473.3 1.4 fusion.3
  474.7 0.8 fusion.4
  475.5 1.5 slice.54
  478.8 2.0 convert_bitcast_fusion.5
  480.9 4.4 convert_element_type.54
  485.2 2.7 convert_bitcast_fusion
  488.0 2.4 convert_bitcast_fusion.1
  490.4 0.7 copy.63
  491.1 0.9 copy.64
  (35 shorter events, 3.0 us)
Async XLA Ops:
  0.7 12.2 %copy-start = (bf16[1280,192]{0,1:T(8,128)(2,1)S(1)}, bf16[1280,192]{0,1:T(8,128)(2,1)}, u32[]{:S(2)}) copy-start(bf16[1280,192]{0,1:T(8,128)(2,1)} %param.39) | copy-start | bytes 1474564
  0.7 11.7 %copy-start.5 = (bf16[3,77,1280]{2,1,0:T(8,128)(2,1)S(1)}, bf16[3,77,1280]{2,1,0:T(8,128)(2,1)}, u32[]{:S(2)}) copy-start(bf16[3,77,1280]{2,1,0:T(8,128)(2,1)} %param.27) | copy-start | bytes 1774084
  12.5 2.3 copy-start.6
  12.5 2.3 copy-start.7
  12.6 2.2 copy-start.8
  480.9 4.4 copy-start.3
  485.2 2.7 copy-start.2
  487.9 2.4 copy-start.9
  487.9 3.2 copy-start.4
  487.9 4.6 copy-start.1
  490.4 1.6 copy-start.10

commit v3 on v2

--- a/solution.py
+++ b/solution.py
@@ -722,65 +722,82 @@
             copy.wait_send()
 
 
+class CoreHalf:
+    def __init__(self, own, got, half, sems):
+        _, core, core_peer, _ = group_place()
+        self.own, self.got, self.half, self.core = own, got, half, core
+        self.copies = [
+            grp_copy(
+                own.at[:, side * 2 + 1 - core],
+                got.at[side],
+                sems.at[0, side],
+                sems.at[1, side],
+                core_peer,
+            )
+            for side in (0, 1)
+        ]
+
+    def begin(self):
+        for copy in self.copies:
+            copy.start()
+
+    def finish(self):
+        for side, copy in enumerate(self.copies):
+            copy.wait_recv()
+
+            def tile(index, side=side):
+                self.half[index, side] = (
+                    self.own[index, side * 2 + self.core].astype(jnp.float32)
+                    + self.got[side, index].astype(jnp.float32)
+                ).astype(self.half.dtype)
+
+            tile_loop(self.own.shape[0], tile)
+        for copy in self.copies:
+            copy.wait_send()
+
+
 class QuarterSum:
-    def __init__(self, shards, own, got, other, out, sems):
+    def __init__(self, shards, half, other, part, out, sems):
         x, core, core_peer, x_peer = group_place()
         me = lax.axis_index("seq")
-        units, width = own.shape[2], own.shape[3]
-        self.own, self.got, self.other, self.out = own, got, other, out
-        self.core, self.shards = core, shards
-        self.mine = x * 2 + core
+        units, width = half.shape[2], half.shape[3]
+        self.half, self.other, self.part, self.out = half, other, part, out
+        self.x, self.me, self.shards = x, me, shards
+        mine = x * 2 + core
         pair = lambda k: (sems.at[0, k], sems.at[1, k])
 
         def rows(quarter):
             return pl.ds(pl.multiple_of(quarter * units, units), units)
 
-        self.block = (rows(self.mine), pl.ds(pl.multiple_of(me * width, 128), width))
-        self.me = me
-        self.first = [
-            grp_copy(own.at[:, side * 2 + 1 - core], got.at[side], *pair(side), core_peer)
-            for side in (0, 1)
-        ]
-        self.second = grp_copy(own.at[:, (1 - x) * 2 + core], other, *pair(2), x_peer)
+        self.block = (rows(mine), pl.ds(pl.multiple_of(me * width, 128), width))
+        self.second = grp_copy(half.at[:, 1 - x], other, *pair(0), x_peer)
         self.third = []
         for step in range(1, shards):
             goal = lax.rem(me + step, shards)
-            self.third.append(
-                seq_copy(own.at[goal, self.mine], out.at[self.block], *pair(2 + step), goal)
-            )
-        base = 2 + shards
-        whole = out.at[rows(self.mine)]
-        self.fourth = grp_copy(whole, whole, *pair(base), x_peer)
+            self.third.append(seq_copy(part.at[goal], out.at[self.block], *pair(step), goal))
+        whole = out.at[rows(mine)]
+        self.fourth = grp_copy(whole, whole, *pair(shards), x_peer)
         self.fifth = []
         for side in (0, 1):
             whole = out.at[rows(side * 2 + core)]
-            self.fifth.append(grp_copy(whole, whole, *pair(base + 1 + side), core_peer))
-
-    def add(self, quarter, right):
-        def tile(index):
-            self.own[index, quarter] = (
-                self.own[index, quarter].astype(jnp.float32) + right(index).astype(jnp.float32)
-            ).astype(self.own.dtype)
-
-        tile_loop(self.shards, tile)
+            self.fifth.append(grp_copy(whole, whole, *pair(shards + 1 + side), core_peer))
 
     def begin(self):
-        for copy in self.first:
-            copy.start()
-
-    def across(self):
-        for copy in self.first:
-            copy.wait_recv()
-        for side in (0, 1):
-            self.add(side * 2 + self.core, lambda index, side=side: self.got[side, index])
         self.second.start()
 
     def spread(self):
         self.second.wait_recv()
-        self.add(self.mine, lambda index: self.other[index])
+
+        def tile(index):
+            self.part[index] = (
+                self.half[index, self.x].astype(jnp.float32)
+                + self.other[index].astype(jnp.float32)
+            ).astype(self.part.dtype)
+
+        tile_loop(self.shards, tile)
         for copy in self.third:
             copy.start()
-        self.out[self.block] = self.own[self.me, self.mine]
+        self.out[self.block] = self.part[self.me]
 
     def share(self):
         for copy in self.third:
@@ -795,7 +812,7 @@
     def finish(self):
         for copy in self.fifth:
             copy.wait_recv()
-        for copy in (*self.first, self.second, *self.third, self.fourth, *self.fifth):
+        for copy in (self.second, *self.third, self.fourth, *self.fifth):
             copy.wait_send()
 
 
@@ -804,32 +821,48 @@
 
 
 class Gather:
-    def __init__(self, full, sems, depth):
-        self.full, self.depth = full, depth
-        self.sems = [sems.at[k] for k in range(4)]
+    def __init__(self, full, sems, depth, extra=0):
+        self.full, self.depth, self.extra = full, depth, extra
+        self.sems = [sems.at[k] for k in range(6)]
         self.me, self.z, self.y, self.other = place()
+        self.rows = full.shape[1]
 
     def origin(self, direction, hops, far):
         column = 1 - self.y if far else self.y
         return (self.z - hops if direction == 0 else self.z + hops) * 2 + column
 
-    def z_copy(self, direction, hops):
-        block = self.full.at[self.origin(direction, hops, False)]
-        send, recv = self.sems[0], self.sems[1]
+    def block(self, direction, hops, far=False):
+        origin = self.origin(direction, hops, far)
+        if not self.extra:
+            return self.full.at[origin]
+        return self.full.at[origin, pl.ds(0, self.rows - self.extra)]
+
+    def pair(self, direction, hops):
+        low = self.origin(direction, hops, False) - self.y
+        return self.full.at[pl.ds(low, 2), pl.ds(self.rows - self.extra, self.extra)]
+
+    def z_move(self, block, kind, direction, hops, arrival):
+        send, recv = self.sems[kind], self.sems[kind + 1]
         target = self.me + 2 if direction == 0 else self.me - 2
         return seq_copy(
-            block, block, send.at[direction, hops], recv.at[direction, hops + 1], target
-        )
-
-    def z_arrival(self, direction, hops):
-        block = self.full.at[self.origin(direction, hops, False)]
-        send, recv = self.sems[0], self.sems[1]
-        return seq_copy(
-            block, block, send.at[direction, hops], recv.at[direction, hops], self.other
-        )
-
-    def y_copy(self, direction, hops, arrival=False):
-        block = self.full.at[self.origin(direction, hops, arrival)]
+            block,
+            block,
+            send.at[direction, hops],
+            recv.at[direction, hops if arrival else hops + 1],
+            self.other if arrival else target,
+        )
+
+    def z_copy(self, direction, hops, arrival=False):
+        return self.z_move(self.block(direction, hops), 0, direction, hops, arrival)
+
+    def pair_copy(self, direction, hops, arrival=False):
+        return self.z_move(self.pair(direction, hops), 4, direction, hops, arrival)
+
+    def y_copy(self, direction, hops, arrival=False, own=False):
+        if own:
+            block = self.full.at[self.origin(direction, hops, arrival)]
+        else:
+            block = self.block(direction, hops, arrival)
         send, recv = self.sems[2], self.sems[3]
         return seq_copy(
             block, block, send.at[direction, hops], recv.at[direction, hops], self.other
@@ -848,14 +881,23 @@
             def _():
                 self.z_copy(direction, 0).start()
 
-        self.y_copy(0, 0).start()
+        self.y_copy(0, 0, own=True).start()
+
+    def cross(self):
+        self.y_copy(0, 0, True, own=True).wait_recv()
+        if self.extra:
+            for direction in (0, 1):
+
+                @pl.when(self.onward(direction))
+                def _():
+                    self.pair_copy(direction, 0).start()
 
     def hop(self, hops):
         for direction in (0, 1):
 
-            @pl.when((hops < self.depth) & self.here(direction, hops))
+            @pl.when(self.here(direction, hops))
             def _():
-                self.z_arrival(direction, hops).wait_recv()
+                self.z_copy(direction, hops, True).wait_recv()
 
                 @pl.when(self.onward(direction))
                 def _():
@@ -863,25 +905,36 @@
 
                 self.y_copy(direction, hops).start()
 
+        if self.extra:
+            for direction in (0, 1):
+
+                @pl.when(self.here(direction, hops))
+                def _():
+                    self.pair_copy(direction, hops, True).wait_recv()
+
+                    @pl.when(self.onward(direction))
+                    def _():
+                        self.pair_copy(direction, hops).start()
+
     def near(self, hops, visit):
         for direction in (0, 1):
 
-            @pl.when((hops < self.depth) & self.here(direction, hops))
+            @pl.when(self.here(direction, hops))
             def _():
                 visit(self.origin(direction, hops, False))
 
-    def far(self, hops, visit):
+    def far(self, hops, visit=None):
         for direction in (0, 1):
-            here = self.here(direction, hops)
-            if direction == 1:
-                here = here & (hops > 0)
-
-            @pl.when(here)
+
+            @pl.when(self.here(direction, hops))
             def _():
                 self.y_copy(direction, hops, True).wait_recv()
-                visit(self.origin(direction, hops, True))
+                if visit is not None:
+                    visit(self.origin(direction, hops, True))
 
     def drain(self):
+        self.y_copy(0, 0, own=True).wait_send()
+
         def step(hops, carry):
             for direction in (0, 1):
                 here = self.here(direction, hops)
@@ -889,11 +942,10 @@
                 @pl.when(here & self.onward(direction))
                 def _():
                     self.z_copy(direction, hops).wait_send()
-
-                if direction == 1:
-                    here = here & (hops > 0)
-
-                @pl.when(here)
+                    if self.extra:
+                        self.pair_copy(direction, hops).wait_send()
+
+                @pl.when(here & (hops > 0))
                 def _():
                     self.y_copy(direction, hops).wait_send()
 
@@ -902,17 +954,29 @@
         lax.fori_loop(0, self.depth, step, 0)
 
     def finish(self):
-        tile_loop(self.depth, lambda hops: self.far(hops, lambda block: None))
+        def step(hops, carry):
+            self.far(hops)
+            return carry
+
+        lax.fori_loop(1, self.depth, step, 0)
         self.drain()
 
     def run(self, visit, hook=None):
         self.start()
         visit(self.me)
+        self.cross()
+        visit(self.other)
 
         def step(hops, carry):
-            self.hop(hops)
-            self.near(hops, visit)
-            self.far(hops - 1, visit)
+            @pl.when(hops < self.depth)
+            def _():
+                self.hop(hops)
+                self.near(hops, visit)
+
+            @pl.when(hops > 1)
+            def _():
+                self.far(hops - 1, visit)
+
             if hook is not None:
                 hook(hops)
             return carry
@@ -969,7 +1033,7 @@
 
 
 def scatter_blocks(
-    partial, to_y, from_y, to_z, from_z, acc, y_sems, z_sems, depth, between=None, hook=None
+    partial, to_y, from_y, to_z, from_z, acc, y_sems, z_sems, depth, between=None, hook=None, early=None
 ):
     me, z, y, other = place()
     low = to_y.dtype
@@ -979,10 +1043,13 @@
             to_y.at[goal], from_y.at[goal], y_sems.at[0, goal], y_sems.at[1, goal], other
         )
 
+    def slot(direction, goal, at):
+        return goal if direction == 0 else jnp.where(goal == at, depth, goal)
+
     def z_copy(direction, goal):
         return seq_copy(
             to_z.at[goal],
-            from_z.at[direction, goal],
+            from_z.at[slot(direction, goal, z - 1)],
             z_sems.at[0, direction, goal],
             z_sems.at[1, direction, goal],
             me + 2 if direction == 0 else me - 2,
@@ -991,7 +1058,7 @@
     def z_arrival(direction, goal):
         return seq_copy(
             to_z.at[goal],
-            from_z.at[direction, goal],
+            from_z.at[slot(direction, goal, z)],
             z_sems.at[0, direction, goal],
             z_sems.at[1, direction, goal],
             other,
@@ -1016,6 +1083,8 @@
                 to_y[goal] = partial(goal * 2 + other - z * 2).astype(low)
                 y_copy(goal).start()
 
+        if early is not None:
+            early(step)
         return carry
 
     lax.fori_loop(0, depth, over_y, 0)
@@ -1036,7 +1105,7 @@
                 @pl.when(in_line(direction, z, 1, depth))
                 def _():
                     z_arrival(direction, goal).wait_recv()
-                    acc[...] += from_z[direction, goal].astype(jnp.float32)
+                    acc[...] += from_z[slot(direction, goal, z)].astype(jnp.float32)
 
                 to_z[goal] = acc[...].astype(low)
                 z_copy(direction, goal).start()
@@ -1054,7 +1123,7 @@
         @pl.when(in_line(direction, z, 1, depth))
         def _():
             z_arrival(direction, z).wait_recv()
-            acc[...] += from_z[direction, z].astype(jnp.float32)
+            acc[...] += from_z[slot(direction, z, z)].astype(jnp.float32)
 
     def drain(goal, carry):
         y_copy(goal).wait_send()
@@ -1095,7 +1164,7 @@
 
 
 EDGE = 80
-VMEM_BYTES = 56 * 1024 * 1024
+VMEM_BYTES = 58 * 1024 * 1024
 ROOT_HALF = math.sqrt(0.5)
 DENSITY = 1.0 / math.sqrt(2.0 * math.pi)
 
@@ -1213,6 +1282,7 @@
 
 def mixer_kernel(
     shards,
+    emit,
     shape,
     hidden,
     cond,
@@ -1276,12 +1346,11 @@
     fc2_shard = Reshard(shards, fc2_part, fc2_rows, local_sems.at[0], fc2_sems)
     out_shard = Reshard(shards, out_part, out_parts, local_sems.at[1], out_sems)
     ctx_gather = Gather(ctx_full, ctx_sems, depth)
-    cot_gather = Gather(cot_full, cot_sems, depth)
+    cot_gather = Gather(cot_full, cot_sems, depth, rows // 8)
     ctx_full[me] = ctx_cols[...]
-    cot_full[me] = cot[...]
     latents = Latents(shape, shards * rows)
     cols = pack.shape[1]
-    width_one = fc1.shape[1]
+    width_one = response.shape[2]
     fc1_bias, gamma, beta = (vec[:, n * width_one : (n + 1) * width_one] for n in range(3))
     vec_at = lambda n: vec[:, 3 * width_one + n * VEC_STEP : 3 * width_one + n * VEC_STEP + cols]
     time_bias = vec[:, 3 * width_one + 6 * VEC_STEP : 3 * width_one + 6 * VEC_STEP + 2 * cols]
@@ -1319,7 +1388,9 @@
     fc2_shard.begin()
     out_shard.begin()
     ctx_gather.start()
+    cot_full[me] = cot.wait()[...]
     cot_gather.start()
+    emit(held)
     tile_loop(
         floats.shape[0] // 32,
         lambda i: floats.__setitem__(
@@ -1360,6 +1431,8 @@
 
     tile_loop(rows // 16, norm_tile)
     energy[...] = jnp.zeros_like(energy)
+    fc1 = fc1.wait()
+    emit(wide, normed)
 
     def visit(block):
         pre[block] = (
@@ -1383,6 +1456,7 @@
     def hook(hops):
         @pl.when(hops == 1)
         def _():
+            ctx_gather.cross()
             ctx_gather.hop(1)
 
         @pl.when(hops == 2)
@@ -1390,13 +1464,15 @@
             fc2_shard.share()
             out_shard.share()
             ctx_gather.hop(2)
+            cot_gather.cross()
             cot_gather.hop(1)
 
         @pl.when(hops == 3)
         def _():
             ctx_gather.hop(3)
 
-    Gather(full, gather_sems, depth).run(visit, hook)
+    Gather(full, gather_sems, depth, rows // 8).run(visit, hook)
+    emit(full, pre)
     cot_gather.hop(2)
     fc2_shard.share_core()
     out_shard.share_core()
@@ -1418,8 +1494,11 @@
         ).astype(response.dtype)
 
     tile_loop(shards * rows // 32, respond)
+    emit(response)
     ctx_gather.finish()
+    emit(ctx_full)
     fc2_shard.finish()
+    emit(fc2_rows)
     out_shard.finish()
     for quarter in range(4):
         side_by_side(
@@ -1430,6 +1509,7 @@
 
 def mixed_in_kernel(
     shards,
+    emit,
     shape,
     response,
     fc2,
@@ -1456,7 +1536,7 @@
     gather_sems,
 ):
     f32 = jnp.float32
-    rows = hidden.shape[0]
+    rows = acc.shape[0]
     depth = shards // 2
     me = lax.axis_index("seq")
     meet_all(shards)
@@ -1472,6 +1552,8 @@
         return dot_nt(response[block], fc2[...])
 
     scatter_blocks(partial, to_y, from_y, to_z, from_z, acc, y_sems, z_sems, depth)
+
+    hidden = hidden.wait()
 
     def norm_tile(index):
         here = pl.ds(pl.multiple_of(index * 16, 16), 16)
@@ -1486,6 +1568,8 @@
         full[me, here, :] = value.astype(full.dtype)
 
     tile_loop(rows // 16, norm_tile)
+    emit(first, second, normed)
+    w_qkv, context = w_qkv.wait(), context.wait()
 
     side = jnp.dot(w_qkv[cols:, :], context[...], preferred_element_type=f32)
     keys[:, shards * rows :] = side[:cols].astype(keys.dtype)
@@ -1500,11 +1584,12 @@
         keys[:, here] = side[:cols].astype(keys.dtype)
         values[:, here] = (side[cols:] + v_bias).astype(values.dtype)
 
-    Gather(full, gather_sems, depth).run(visit)
+    Gather(full, gather_sems, depth, rows // 8).run(visit)
 
 
 def attend_kernel(
     shards,
+    emit,
     shape,
     queries,
     keys,
@@ -1570,6 +1655,8 @@
 
             @pl.when(tile >= hops)
             def _():
+                if hops == 1:
+                    gather_of(tile - 1).cross()
                 gather_of(tile - hops).hop(hops)
 
         for head in range(heads):
@@ -1587,6 +1674,8 @@
     lax.fori_loop(0, tiles, step, 0)
     for late in range(1, depth):
         for hops in range(late, depth):
+            if hops == 1:
+                gather_of(tiles - 1).cross()
             gather_of(tiles - 1 + late - hops).hop(hops)
     d_qkv[:cols, tiles * tile_rows :] = jnp.zeros(
         (cols, d_qkv.shape[1] - tiles * tile_rows), bf16
@@ -1609,6 +1698,7 @@
 
 def attn_back_kernel(
     shards,
+    emit,
     shape,
     cond,
     d_qkv,
@@ -1619,30 +1709,31 @@
     cot_cols,
     out_weight,
     vec,
-    second,
     cot,
     normed,
     inverse,
     first,
     wide,
-    context_in,
     fc2,
     pre,
     root,
     ratio,
     denom,
+    response,
+    context_in,
     full,
     d_first,
     d_pre,
+    small_out,
+    weight_grads,
+    map_grad,
+    act_out,
+    fc2_half,
+    d_mod,
     small,
-    map_grad,
-    weight_grads,
-    activations,
-    d_mod,
     acc,
     d_resp,
     act,
-    slope,
     sums,
     mine,
     theirs,
@@ -1658,17 +1749,17 @@
     g_got,
     g_other,
     g_sems,
+    mod_in,
+    mod_sems,
+    fc2_own,
+    fc2_got,
+    fc2_sems,
     ctx_out,
     ctx_in,
     ctx_sems,
-    mod_in,
-    mod_sems,
-    act_out,
-    act_in,
-    act_sems,
 ):
     f32 = jnp.float32
-    rows = cot.shape[0]
+    rows = acc.shape[0]
     depth = shards // 2
     me = lax.axis_index("seq")
     meet_all(shards, lax.axis_size("grp"))
@@ -1680,23 +1771,14 @@
     gamma = vec[:, width_one : 2 * width_one]
     out_bias = column_of(vec[:, base + 4 * VEC_STEP : base + 5 * VEC_STEP])[:cols]
     scale = wide[WIDE_SCALE : WIDE_SCALE + 8, :]
+    later = (attn, context, mixed, cot_cols, out_weight)
     weight_sum = PairSum(g_own, g_got, g_other, weight_grads, g_sems)
     peers = [lax.rem(me + step, shards) for step in range(1, shards)]
     ctx_copies = [
-        seq_copy(ctx_out.at[peer], ctx_in.at[me], ctx_sems.at[0, k], ctx_sems.at[1, k], peer)
-        for k, peer in enumerate(peers)
+        seq_copy(ctx_out.at[peer], ctx_in.at[me], ctx_sems.at[0, n], ctx_sems.at[1, n], peer)
+        for n, peer in enumerate(peers)
     ]
-
-    act_copies = [
-        seq_copy(
-            act_out.at[:, pl.ds(pl.multiple_of(peer * rows, 128), rows)],
-            act_in.at[me],
-            act_sems.at[0, k],
-            act_sems.at[1, k],
-            peer,
-        )
-        for k, peer in enumerate(peers)
-    ]
+    fc2_sum = CoreHalf(fc2_own, fc2_got, fc2_half, fc2_sems)
 
     def partial(block):
         here = pl.ds(pl.multiple_of(block * rows, 128), rows)
@@ -1704,11 +1786,11 @@
 
     def between():
         low_type = ctx_out.dtype
+        attn, context, mixed, cot_cols, out_weight = (item.wait() for item in later)
         for device in range(shards):
             ctx_out[device] = dot_tn(
                 w_qkv[:, device * cols : (device + 1) * cols], d_qkv[:, total:]
             ).astype(low_type)
-        ctx_in[me] = ctx_out[me]
         g_own[: 3 * cols, :] = (
             jnp.dot(d_qkv[:, :total], attn[...].reshape(total, C), preferred_element_type=f32)
             + dot_nt(d_qkv[:, total:], context[...])
@@ -1724,7 +1806,6 @@
             grad = part if grad is None else grad + part
         g_own[3 * cols :, :] = grad.astype(low_type)
         weight_sum.begin()
-        act_in[me] = act_out[:, pl.ds(pl.multiple_of(me * rows, 128), rows)]
 
     def scatter_hook(step):
         @pl.when(step == 1)
@@ -1735,6 +1816,7 @@
         partial, to_y, from_y, to_z, from_z, acc, y_sems, z_sems, depth, between, scatter_hook
     )
     d_mod[...] = jnp.zeros_like(d_mod)
+    cot, normed, first = cot.wait(), normed.wait(), first.wait()
 
     def norm_tile(index):
         here = pl.ds(pl.multiple_of(index * 16, 16), 16)
@@ -1755,6 +1837,8 @@
 
     tile_loop(rows // 16, norm_tile)
     sums[...] = jnp.zeros_like(sums)
+    emit(d_first)
+    fc2, pre = fc2.wait(), pre.wait()
     wide_mod = 2 * cols
     half = shards // 2
 
@@ -1782,9 +1866,9 @@
             here = pl.ds(pl.multiple_of(index * 32, 32), 32)
             value = pre[block, here, :]
             phi = 0.5 * (1.0 + lax.erf(value * ROOT_HALF))
-            slope[block, here, :] = phi + value * (DENSITY * jnp.exp(-0.5 * value * value))
+            pre[block, here, :] = phi + value * (DENSITY * jnp.exp(-0.5 * value * value))
             value = value * phi
-            act[block, here, :] = value
+            act[block, here, :] = value.astype(act.dtype)
             pull = d_resp[block, here, :]
             sums[NLAT : NLAT + 1, :] += jnp.sum(pull, axis=0, keepdims=True)
             pull = pull * value
@@ -1796,7 +1880,8 @@
 
         tile_loop(rows // 32, tile)
 
-    Gather(full, gather_sems, depth).run(visit, gather_hook)
+    Gather(full, gather_sems, depth, rows // 8).run(visit, gather_hook)
+    emit(full)
     small[...] = jnp.zeros_like(small)
     wide_row = 2 * cols
 
@@ -1813,8 +1898,16 @@
     mine[...] = jnp.broadcast_to(jnp.sum(d_ratio * root[...], axis=1, keepdims=True), mine.shape)
 
     def meanwhile():
-        for copy in (*ctx_copies, *act_copies):
+        for copy in ctx_copies:
             copy.start()
+        ctx_in[me] = ctx_out[me]
+        right = response.wait()[...].reshape(total, width_one)
+        units = fc2_own.shape[2]
+        for goal in range(0, shards, 4):
+            here = slice(goal * 4 * units, (goal + 4) * 4 * units)
+            part = dot_tn(full[:, :, here].reshape(total, 16 * units), right)
+            fc2_own[goal : goal + 4] = part.reshape(4, 4, units, width_one).astype(fc2_own.dtype)
+        fc2_sum.begin()
 
     pulled = peer_total(mine, theirs, total_sems, shards, meanwhile)[:, 0:1]
     below = denom[:, 0:1]
@@ -1827,30 +1920,23 @@
         block = index // (rows // 32)
         here = pl.ds(pl.multiple_of(lax.rem(index, rows // 32) * 32, 32), 32)
         pick = latents.picks(index * 32, 32)
-        d_act = d_resp[block, here, :] * rows_of(pick, scaled) + act[block, here, :] * rows_of(
+        d_act = d_resp[block, here, :] * rows_of(pick, scaled) + act[block, here, :].astype(f32) * rows_of(
             pick, back
         )
-        value = (d_act * slope[block, here, :]).astype(d_pre.dtype)
+        value = (d_act * pre[block, here, :]).astype(d_pre.dtype)
         d_pre[block, here, :] = value
         sums[0:1, :] += jnp.sum(value.astype(f32), axis=0, keepdims=True)
 
     tile_loop(shards * rows // 32, respond)
-    for copy in (*ctx_copies, *mod_copies, *act_copies):
+    emit(d_pre)
+    for copy in mod_copies:
         copy.wait()
-    activations[...] = (second[...] + act_in[...].reshape(C, rows).astype(f32).T).astype(
-        activations.dtype
-    )
-    context_sum = ctx_in[0].astype(f32)
     mod_sum = mod_in[0]
     for device in range(1, shards):
-        context_sum = context_sum + ctx_in[device].astype(f32)
         mod_sum = mod_sum + mod_in[device]
     keep(SMALL_FC1, sums[0:1, :])
-    at = lax.broadcasted_iota(jnp.int32, (1, context.shape[1]), 1)
-    context_sum = jnp.where(at < NLAT * NCTX, context_sum, 0.0)
-    map_grad[...] = jnp.dot(
-        context_sum.astype(map_grad.dtype), context_in[...], preferred_element_type=f32
-    ).astype(map_grad.dtype)
+    fc2_sum.finish()
+    emit(fc2_half)
     chosen = [
         jnp.where(me < half, mod_sum[2 * n : 2 * n + 1], mod_sum[2 * n + 1 : 2 * n + 2])
         for n in range(NLAT)
@@ -1868,9 +1954,19 @@
     for row, value in (
         (SMALL_QUERY, d_qkv[:cols, :]),
         (SMALL_VALUE, d_qkv[2 * cols :, :]),
-        (SMALL_OUT, cot_cols[...]),
+        (SMALL_OUT, later[3].buffer[...]),
     ):
         small[row : row + 1, :cols] = dot_nt(ones(value), value)[0:1]
+    for copy in ctx_copies:
+        copy.wait()
+    context_sum = ctx_in[0].astype(f32)
+    for device in range(1, shards):
+        context_sum = context_sum + ctx_in[device].astype(f32)
+    at = lax.broadcasted_iota(jnp.int32, (1, context_sum.shape[1]), 1)
+    context_sum = jnp.where(at < NLAT * NCTX, context_sum, 0.0)
+    map_grad[...] = jnp.dot(
+        context_sum.astype(map_grad.dtype), context_in.wait()[...], preferred_element_type=f32
+    ).astype(map_grad.dtype)
     small[SMALL_MAP : SMALL_MAP + 1, :cols] = lax.dot_general(
         ones(context_sum),
         context_sum,
@@ -1878,11 +1974,13 @@
         precision=HIGHEST_PRECISION,
         preferred_element_type=f32,
     )[0:1]
+    small_out[...] = small[...].astype(small_out.dtype)
     weight_sum.finish()
 
 
 def conv_back_kernel(
     shards,
+    emit,
     shape,
     d_pre,
     fc1,
@@ -1892,9 +1990,11 @@
     hidden,
     wide,
     normed_full,
-    response,
     branch,
     map_grad,
+    act_out,
+    second,
+    fc2_half,
     small,
     input_grad,
     fc1_sum,
@@ -1902,6 +2002,7 @@
     map_sum,
     small_sum,
     conv_sum,
+    activations,
     held,
     floats,
     acc,
@@ -1916,9 +2017,8 @@
     fc1_own,
     fc1_got,
     fc1_other,
-    fc2_own,
-    fc2_got,
     fc2_other,
+    fc2_part,
     map_own,
     map_got,
     map_other,
@@ -1931,21 +2031,23 @@
     conv_part,
     conv_group,
     conv_sems,
+    act_in,
+    act_sems,
 ):
     f32 = jnp.float32
-    rows = normed.shape[0]
+    rows = acc.shape[0]
     depth = shards // 2
     groups = lax.axis_size("grp")
     me = lax.axis_index("seq")
     meet_all(shards, groups)
     cols = conv_part.shape[1]
-    units, width = fc2_own.shape[2:]
+    width = d_pre.shape[2]
     total = shards * rows
     latents = Latents(shape, total)
     positions = me * rows + lax.broadcasted_iota(jnp.int32, (rows, 1), 0)
     fc1_pair = PairSum(fc1_own, fc1_got, fc1_other, fc1_sum, pair_sems.at[0])
     map_pair = PairSum(map_own, map_got, map_other, map_sum, pair_sems.at[1])
-    fc2_quarter = QuarterSum(shards, fc2_own, fc2_got, fc2_other, fc2_sum, fc2_sems)
+    fc2_quarter = QuarterSum(shards, fc2_half, fc2_other, fc2_part, fc2_sum, fc2_sems)
     group = lax.axis_index("grp")
     small_copies = [
         grp_copy(
@@ -1961,42 +2063,59 @@
     def partial(block):
         return dot_nt(d_pre[block], fc1[...])
 
-    def between():
-        map_own[...] = map_grad[...]
-        map_pair.begin()
-        for copy in small_copies:
-            copy.start()
-        right = response[...].reshape(total, width)
-        for goal in range(0, shards, 4):
-            here = slice(goal * 4 * units, (goal + 4) * 4 * units)
-            part = dot_tn(branch[:, :, here].reshape(total, 16 * units), right)
-            fc2_own[goal : goal + 4] = part.reshape(4, 4, units, width).astype(fc2_own.dtype)
-        fc2_quarter.begin()
+    peers = [lax.rem(me + step, shards) for step in range(1, shards)]
+    act_copies = []
+    for n, peer in enumerate(peers):
+        there = pl.ds(pl.multiple_of(peer * rows, 128), rows)
+        act_copies.append(
+            seq_copy(act_out.at[:, there], act_in.at[me], act_sems.at[0, n], act_sems.at[1, n], peer)
+        )
+
+    def fc1_grad():
+        full = normed_full.wait()
 
         def tile(index):
             here = pl.ds(pl.multiple_of(index * 256, 256), 256)
             fc1_own[here, :] = dot_tn(
-                normed_full[:, :, here].reshape(total, 256),
-                d_pre[...].reshape(total, width),
+                full[:, :, here].reshape(total, 256), d_pre[...].reshape(total, width)
             ).astype(fc1_own.dtype)
 
         tile_loop(C // 256, tile)
         fc1_pair.begin()
 
+    fc2_quarter.begin()
+    map_own[...] = map_grad[...]
+    map_pair.begin()
+
+    def early(step):
+        @pl.when(step == 1)
+        def _():
+            for copy in act_copies:
+                copy.start()
+            fc1_grad()
+
     def scatter_hook(step):
-        @pl.when(step == 0)
-        def _():
-            fc2_quarter.across()
-            fc1_pair.across()
-
-        @pl.when(step == 2)
+        @pl.when(step == 1)
         def _():
             fc2_quarter.spread()
+            fc1_pair.across()
             map_pair.across()
 
     scatter_blocks(
-        partial, to_y, from_y, to_z, from_z, acc, y_sems, z_sems, depth, between, scatter_hook
-    )
+        partial,
+        to_y,
+        from_y,
+        to_z,
+        from_z,
+        acc,
+        y_sems,
+        z_sems,
+        depth,
+        None,
+        scatter_hook,
+        early,
+    )
+    normed, d_first, hidden = normed.wait(), d_first.wait(), hidden.wait()
 
     def norm_tile(index):
         start = pl.multiple_of(index * 16, 16)
@@ -2007,6 +2126,9 @@
 
     tile_loop(rows // 16, norm_tile)
     finish = exchange_edges(held, edge_sems, rows, shards)
+    for copy in small_copies:
+        copy.start()
+    fc2_quarter.share()
     tile_loop(
         floats.shape[0] // 32,
         lambda i: floats.__setitem__(
@@ -2020,7 +2142,7 @@
         cols = pl.ds(pl.multiple_of(index * 256, 256), 256)
         d_conv = held[pl.ds(EDGE, rows), cols].astype(f32)
         d_conv_params[9:10, cols] = jnp.sum(d_conv, axis=0, keepdims=True)
-        d_conv_params[10:11, cols] = jnp.sum(branch[me, :, cols].astype(f32), axis=0, keepdims=True)
+        d_conv_params[10:11, cols] = jnp.sum(branch[:, cols].astype(f32), axis=0, keepdims=True)
         for tap in range(9):
             offset = EDGE + (tap // 3 - 1) * WMAX + tap % 3 - 1
             d_conv_params[tap : tap + 1, cols] = jnp.sum(
@@ -2047,7 +2169,7 @@
         )
         conv_copies[-1].start()
     finish()
-    fc2_quarter.share()
+    act_in[me] = act_out[:, pl.ds(pl.multiple_of(me * rows, 128), rows)]
     tile_loop(
         floats.shape[0] // 32,
         lambda i: floats.__setitem__(
@@ -2077,6 +2199,8 @@
     conv_total = conv_in[0]
     for device in range(1, shards):
         conv_total = conv_total + conv_in[device]
+    tile_loop(C // 256, input_tile)
+    fc1_pair.share()
     conv_part[...] = conv_total
     group_copies = []
     for step in range(1, groups):
@@ -2091,34 +2215,91 @@
             )
         )
         group_copies[-1].start()
-    tile_loop(C // 256, input_tile)
-    fc1_pair.share()
+    fc2_quarter.share_core()
+    for copy in act_copies:
+        copy.wait()
+    activations[...] = (second.wait()[...] + act_in[...].reshape(C, rows).astype(f32).T).astype(
+        activations.dtype
+    )
     map_pair.share()
-    fc2_quarter.share_core()
     for copy in (*small_copies, *group_copies):
         copy.wait()
-    small_sum[...] = small[...] + small_in[0] + small_in[1] + small_in[2]
+    small_total = small[...].astype(f32)
+    for step in range(groups - 1):
+        small_total = small_total + small_in[step].astype(f32)
+    small_sum[...] = small_total
     conv_sum[...] = conv_part[...] + conv_group[0] + conv_group[1] + conv_group[2]
+    fc2_quarter.finish()
+    emit(fc2_sum)
+    map_pair.finish()
     fc1_pair.finish()
-    map_pair.finish()
-    fc2_quarter.finish()
-
-
-def kernel_call(body, name, number, outs, scratch, operands, flops=0, far=(), scalars=()):
+
+
+class Late:
+    def __init__(self, buffer, copy):
+        self.buffer, self.copy = buffer, copy
+
+    def wait(self):
+        self.copy.wait()
+        return self.buffer
+
+
+def staged_body(body, n_in, n_out, late, staged):
+    def run(*refs):
+        ins, outs = list(refs[:n_in]), list(refs[n_in : n_in + n_out])
+        rest = refs[n_in + n_out :]
+        count = len(late) + len(staged)
+        if not count:
+            body(lambda *buffers: None, *refs)
+            return
+        kept, buffers, sems = rest[: -count - 1], rest[-count - 1 : -1], rest[-1]
+        for n, k in enumerate(late):
+            copy = pltpu.make_async_copy(ins[k], buffers[n], sems.at[n])
+            copy.start()
+            ins[k] = Late(buffers[n], copy)
+        waiting = []
+        for n, k in enumerate(staged, len(late)):
+            waiting.append([buffers[n], pltpu.make_async_copy(buffers[n], outs[k], sems.at[n]), 0])
+            outs[k] = buffers[n]
+
+        def emit(*which):
+            for entry in waiting:
+                if not entry[2] and any(entry[0] is ref for ref in which):
+                    entry[1].start()
+                    entry[2] = 1
+
+        body(emit, *ins, *outs, *kept)
+        emit(*(entry[0] for entry in waiting))
+        for entry in waiting:
+            entry[1].wait()
+
+    return run
+
+
+def kernel_call(
+    body, name, number, outs, scratch, operands, flops=0, far=(), scalars=(), late=(), staged=()
+):
     vmem, anywhere, smem = (
         pl.BlockSpec(memory_space=space) for space in (pltpu.VMEM, pl.ANY, pltpu.SMEM)
     )
-    space_of = lambda k: anywhere if k in far else smem if k in scalars else vmem
+    in_specs = [
+        anywhere if k in far or k in late else smem if k in scalars else vmem
+        for k in range(len(operands))
+    ]
     shapes = [jax.ShapeDtypeStruct(shape, dtype) for shape, dtype in outs]
     moved = sum(math.prod(s.shape) * s.dtype.itemsize for s in shapes) + sum(
         x.size * x.dtype.itemsize for x in operands
     )
+    extra = [pltpu.VMEM(operands[k].shape, operands[k].dtype) for k in late]
+    extra += [pltpu.VMEM(shapes[k].shape, shapes[k].dtype) for k in staged]
+    if extra:
+        extra.append(pltpu.SemaphoreType.DMA((len(extra),)))
     return pl.pallas_call(
-        body,
+        staged_body(body, len(operands), len(outs), late, staged),
         out_shape=shapes,
-        in_specs=[space_of(k) for k in range(len(operands))],
-        out_specs=[vmem] * len(shapes),
-        scratch_shapes=scratch,
+        in_specs=in_specs,
+        out_specs=[anywhere if k in staged else vmem for k in range(len(shapes))],
+        scratch_shapes=[*scratch, *extra],
         name=name,
         cost_estimate=pl.CostEstimate(flops=flops, bytes_accessed=moved, transcendentals=0),
         compiler_params=pltpu.CompilerParams(
@@ -2133,14 +2314,14 @@
         pltpu.VMEM((depth, rows, C), bf16),
         pltpu.VMEM((depth, rows, C), bf16),
         pltpu.VMEM((depth, rows, C), bf16),
-        pltpu.VMEM((2, depth, rows, C), bf16),
+        pltpu.VMEM((depth + 1, rows, C), bf16),
         pltpu.SemaphoreType.DMA((2, depth)),
         pltpu.SemaphoreType.DMA((2, 2, depth)),
     ]
 
 
 def gather_scratch(depth):
-    return pltpu.SemaphoreType.DMA((4, 2, depth + 1))
+    return pltpu.SemaphoreType.DMA((6, 2, depth + 1))
 
 
 def total_scratch(shards):
@@ -2183,6 +2364,7 @@
     cols = C // shards
     depth = shards // 2
     hidden_cols = FF // shards
+    me = lax.axis_index("seq")
     shape = latent_shape[0]
     slot = lambda item: jnp.pad(item, (0, VEC_STEP - item.shape[0]))
     vec = jnp.concatenate(
@@ -2273,6 +2455,8 @@
         flops=2 * total * C * hidden_cols,
         far=(9, 10),
         scalars=(0,),
+        late=(6, 8),
+        staged=(0, 1, 2, 3, 5, 9, 10, 11, 12),
     )
     context = context.reshape(C, ctx_rows)
     shrink_rows = shrink_parts.reshape(C, hidden_cols)
@@ -2313,6 +2497,8 @@
         ),
         flops=2 * total * C * (hidden_cols + 3 * cols),
         scalars=(0,),
+        late=(3, 5, 7),
+        staged=(0, 1, 2, 3, 5, 6, 7),
     )
 
     tiles, tile_rows = 4, total // 4
@@ -2329,7 +2515,7 @@
             vmem((cols, keys_all), f32),
             vmem((cols, keys_all), f32),
             vmem((cols // HEAD_DIM, tile_rows, keys_all), f32),
-            pltpu.SemaphoreType.DMA((tiles, 4, 2, depth + 1)),
+            pltpu.SemaphoreType.DMA((tiles, 6, 2, depth + 1)),
         ],
         (
             shape,
@@ -2347,9 +2533,10 @@
         d_first,
         d_pre,
         small,
+        weight_sums,
         grad_map_w,
-        weight_sums,
-        activations,
+        act_cols,
+        fc2_half,
     ) = kernel_call(
         functools.partial(attn_back_kernel, shards),
         "attn_back",
@@ -2358,17 +2545,18 @@
             ((shards, rows, C), bf16),
             ((rows, C), f32),
             ((shards, rows, hidden_cols), bf16),
-            ((SMALL_ROWS, 2 * cols), f32),
+            ((SMALL_ROWS, 2 * cols), bf16),
+            ((4 * cols, C), bf16),
             ((cols, CLIP), bf16),
-            ((4 * cols, C), bf16),
-            ((rows, C), bf16),
+            ((cols, total), bf16),
+            ((shards, 2, units, hidden_cols), bf16),
         ],
         [
             vmem((8, C), f32),
+            vmem((SMALL_ROWS, 2 * cols), f32),
             pltpu.VMEM((rows, C), f32),
             pltpu.VMEM((shards, rows, hidden_cols), f32),
-            pltpu.VMEM((shards, rows, hidden_cols), f32),
-            pltpu.VMEM((shards, rows, hidden_cols), f32),
+            pltpu.VMEM((shards, rows, hidden_cols), bf16),
             pltpu.VMEM((8, hidden_cols), f32),
             *total_vmem,
             *scatter_scratch(rows, depth),
@@ -2378,13 +2566,13 @@
             vmem((2 * cols, C), bf16),
             vmem((2 * cols, C), bf16),
             pltpu.SemaphoreType.DMA((2, 3)),
+            vmem((shards, 8, 2 * cols), f32),
+            pltpu.SemaphoreType.DMA((2, shards - 1)),
+            vmem((shards, 4, units, hidden_cols), bf16),
+            vmem((2, shards, units, hidden_cols), bf16),
+            pltpu.SemaphoreType.DMA((2, 2)),
             vmem((shards, cols, ctx_rows), bf16),
             vmem((shards, cols, ctx_rows), bf16),
-            pltpu.SemaphoreType.DMA((2, shards - 1)),
-            vmem((shards, 8, 2 * cols), f32),
-            pltpu.SemaphoreType.DMA((2, shards - 1)),
-            vmem((cols, total), bf16),
-            vmem((shards, cols, rows), bf16),
             pltpu.SemaphoreType.DMA((2, shards - 1)),
         ],
         (
@@ -2398,24 +2586,27 @@
             cot_cols,
             out_weight.T,
             vec,
-            second_sum,
             cotangent,
             normed_two,
             inverse_two,
             first_sum,
             wide,
-            context_in,
             shrink_rows,
             pre_act,
             root,
             ratio,
             denom,
+            response,
+            context_in,
         ),
         flops=2 * total * C * (hidden_cols + 6 * cols),
         scalars=(0,),
+        late=(4, 5, 6, 7, 8, 10, 11, 13, 15, 16, 20, 21),
+        staged=(0, 1, 2, 4, 6, 7),
     )
     groups = lax.axis_size("grp")
-    input_grad, fc1_sum, fc2_sum, map_sum, small, conv_small = kernel_call(
+    branch_own = lax.dynamic_index_in_dim(branch_blocks, me, 0, keepdims=False)
+    input_grad, fc1_sum, fc2_sum, map_sum, small, conv_small, activations = kernel_call(
         functools.partial(conv_back_kernel, shards),
         "conv_back",
         4,
@@ -2426,6 +2617,7 @@
             ((cols, CLIP), bf16),
             ((SMALL_ROWS, 2 * cols), f32),
             ((16, cols), f32),
+            ((rows, C), bf16),
         ],
         [
             vmem((rows + 2 * EDGE, C), bf16),
@@ -2437,21 +2629,22 @@
             vmem((C, hidden_cols), bf16),
             vmem((C // 2, hidden_cols), bf16),
             vmem((C // 2, hidden_cols), bf16),
-            vmem((shards, 4, units, hidden_cols), bf16),
-            vmem((2, shards, units, hidden_cols), bf16),
+            vmem((shards, units, hidden_cols), bf16),
             vmem((shards, units, hidden_cols), bf16),
             vmem((cols, CLIP), bf16),
             vmem((cols // 2, CLIP), bf16),
             vmem((cols // 2, CLIP), bf16),
             pltpu.SemaphoreType.DMA((2, 2, 3)),
-            pltpu.SemaphoreType.DMA((2, 5 + shards)),
-            vmem((groups - 1, SMALL_ROWS, 2 * cols), f32),
+            pltpu.SemaphoreType.DMA((2, 3 + shards)),
+            vmem((groups - 1, SMALL_ROWS, 2 * cols), bf16),
             pltpu.SemaphoreType.DMA((2, groups - 1)),
             vmem((shards, 16, cols), f32),
             vmem((shards, 16, cols), f32),
             vmem((16, cols), f32),
             vmem((groups - 1, 16, cols), f32),
             pltpu.SemaphoreType.DMA((2, shards + groups - 2)),
+            vmem((shards, cols, rows), bf16),
+            pltpu.SemaphoreType.DMA((2, shards - 1)),
         ],
         (
             shape,
@@ -2463,13 +2656,17 @@
             held,
             wide,
             normed_full,
-            response,
-            branch_blocks,
+            branch_own,
             grad_map_w,
+            act_cols,
+            second_sum,
+            fc2_half,
             small,
         ),
         flops=6 * total * C * hidden_cols,
         scalars=(0,),
+        late=(3, 5, 6, 8, 12),
+        staged=(1, 2),
     )
     two = lambda row: small[row : row + 2].reshape(hidden_cols)
     one = lambda row: small[row, :cols]

time: 501 us -> 477 us (0.952)
  Pallas kernels: 456 us -> 436 us
    pallas_call x5, Pallas kernels: 456 us -> 436 us  [kernel_call(): pl.pallas_call(staged_body(body, len(operands), len(outs), late, staged),...]
where the time goes in v3:
time: 477 us; the launch traced here: 470 us
  Pallas kernels  436 us (91%)
  local copies, waits for them, and re-layouts  19.1 us (4%)
  other arithmetic  12.8 us (3%)
    pallas_call x5, Pallas kernels, kernel_call(): pl.pallas_call(staged_body(body, len(operands), len(outs), late, staged),...  436 us

profile of v3, /device:TPU:9, one launch (start us, length us, event | category | flops | bytes accessed | tf_op | source)
XLA Modules:
  0.0 470.4 jit_solution(16729048687411679403)
XLA Ops:
  0.7 1.4 copy.50.refs_0_
  2.1 0.7 constant_dynamic-update-slice_fusion.9
  2.8 0.7 constant_dynamic-update-slice_fusion.8
  3.4 0.7 constant_dynamic-update-slice_fusion.7
  4.1 0.7 pad.27
  4.8 0.7 pad.28
  5.5 0.7 pad.29
  6.2 0.7 pad.30
  6.8 0.7 pad.31
  7.5 0.7 pad.32
  8.2 0.7 pad.33
  8.9 0.6 convert_element_type.47.refs_5_.refs_6_.refs_9_
  9.5 1.2 reshape.199
  11.1 1.0 fusion.1.refs_7_
  12.1 1.2 copy.46.refs_10_
  13.3 106.5 %mixer.1 = (bf16[8,128,1536]{2,1,0:T(8,128)(2,1)}, bf16[288,1536]{1,0:T(8,128)(2,1)}, f32[32,1536]{1,0:T(8,128)}, f32[128,1536]{1,0:T(8,128)}, f32[128,1]{1,0:T(...) custom-call(s32[3,2]{1,0:T(4,128)} %copy.50.refs_0_, ...), custom_call_target="tpu_custom_call" | custom-call | flops 2415919104 | bytes 22931096 | tf_op jit(solution)/shard_map/mixer/pallas_call | solution.py:2297
  119.8 1.3 pad_maximum_fusion.refs_5_.refs_3_
  121.1 73.7 %mixed_in.1 = (bf16[8,128,1536]{2,1,0:T(8,128)(2,1)}, f32[128,1536]{1,0:T(8,128)}, f32[128,1536]{1,0:T(8,128)}, f32[128,1536]{1,0:T(8,128)}, f32[128,1]{1,0:T(8,...) custom-call(s32[3,2]{1,0:T(4,128)} %copy.50.refs_0_, ...), custom_call_target="tpu_custom_call" | custom-call | flops 4227858432 | bytes 13977112 | tf_op jit(solution)/shard_map/mixed_in/pallas_call | solution.py:2297
  194.8 50.3 %attend.1 = (bf16[576,1280]{1,0:T(8,128)(2,1)}, bf16[4,8,192,256]{3,2,1,0:T(8,128)(2,1)}, bf16[192,1024]{1,0:T(8,128)(2,1)}) custom-call(s32[3,2]{1,0:T(4,128)} %copy.50.refs_0_, bf16[8,128,192]{2,1,0:T(8,128)(2,1)} %get-tuple-element.65.refs_1_, bf16[192,1280]{1,0:T(8,128)(2,1)} %get-tuple-element.66.refs_2_, bf16[192,1280]{1,0:T(8,128)(2,1)} %get-tuple-element.67.refs_3_, ...), custom_call_target="tpu_custom_call" | custom-call | flops 12079595520 | bytes 10125336 | tf_op jit(solution)/shard_map/attend/pallas_call | solution.py:2297
  245.1 0.9 pad.34.refs_21_
  246.0 111.9 %attn_back.1 = (bf16[8,128,1536]{2,1,0:T(8,128)(2,1)}, f32[128,1536]{1,0:T(8,128)}, bf16[8,128,768]{2,1,0:T(8,128)(2,1)}, bf16[80,384]{1,0:T(8,128)(2,1)}, bf16[...) custom-call(s32[3,2]{1,0:T(4,128)} %copy.50.refs_0_, ...), custom_call_target="tpu_custom_call" | custom-call | flops 6039797760 | bytes 31263000 | tf_op jit(solution)/shard_map/attn_back/pallas_call | solution.py:2297
  358.0 1.8 dynamic-slice_bitcast_fusion.refs_9_
  359.7 93.9 %conv_back.1 = (f32[128,1536]{1,0:T(8,128)}, bf16[1536,768]{1,0:T(8,128)(2,1)}, bf16[192,6144]{1,0:T(8,128)(2,1)}, bf16[192,1280]{1,0:T(8,128)(2,1)}, f32[80,384...) custom-call(s32[3,2]{1,0:T(4,128)} %copy.50.refs_0_, bf16[8,128,768]{2,1,0:T(8,128)(2,1)} %get-tuple-element.81.refs_1_, ...), custom_call_target="tpu_custom_call" | custom-call | flops 7247757312 | bytes 19563032 | tf_op jit(solution)/shard_map/conv_back/pallas_call | solution.py:2297
  453.7 4.5 convert_bitcast_fusion
  458.3 2.6 convert_element_type.54
  461.4 1.0 convert_bitcast_fusion.5
  462.4 0.6 slice.54
  463.1 0.6 reshape.196
  465.5 2.4 convert_bitcast_fusion.1
  467.9 0.7 copy.63
  468.7 0.9 copy.64
  469.5 0.6 copy.65
  (42 shorter events, 2.9 us)
Async XLA Ops:
  0.7 10.4 %copy-start = (bf16[1280,192]{0,1:T(8,128)(2,1)S(1)}, bf16[1280,192]{0,1:T(8,128)(2,1)}, u32[]{:S(2)}) copy-start(bf16[1280,192]{0,1:T(8,128)(2,1)} %param.39) | copy-start | bytes 1474564
  9.5 1.6 copy-start.13
  10.7 1.4 copy-start.8
  13.3 106.5 %copy-start.5 = (bf16[1536,192]{0,1:T(8,128)(2,1)S(1)}, bf16[1536,192]{0,1:T(8,128)(2,1)}, u32[]{:S(2)}) copy-start(bf16[1536,192]{0,1:T(8,128)(2,1)} %param.44) | copy-start | bytes 1769476
  13.3 106.5 %copy-start.6 = (bf16[1536,192]{0,1:T(8,128)(2,1)S(1)}, bf16[1536,192]{0,1:T(8,128)(2,1)}, u32[]{:S(2)}) copy-start(bf16[1536,192]{0,1:T(8,128)(2,1)} %param.43) | copy-start | bytes 1769476
  13.3 106.5 %copy-start.7 = (bf16[1536,192]{0,1:T(8,128)(2,1)S(1)}, bf16[1536,192]{0,1:T(8,128)(2,1)}, u32[]{:S(2)}) copy-start(bf16[1536,192]{0,1:T(8,128)(2,1)} %param.41) | copy-start | bytes 1769476
  453.7 4.6 copy-start.3
  458.2 2.6 copy-start.11
  458.2 2.6 copy-start.12
  458.2 3.2 copy-start.9
  458.3 7.3 %copy-start.2 = (bf16[768,1536]{1,0:T(8,128)(2,1)S(1)}, bf16[768,1536]{1,0:T(8,128)(2,1)}, u32[]{:S(2)}) copy-start(bf16[768,1536]{1,0:T(8,128)(2,1)} %get-tuple-element.100) | copy-start | bytes 7077892
  465.5 2.4 copy-start.10
  465.5 3.2 copy-start.4
  465.5 4.6 copy-start.1

commit v4 on v3

--- a/solution.py
+++ b/solution.py
@@ -985,6 +985,44 @@
         self.drain()
 
 
+class LineGather:
+    def __init__(self, full, sems, depth):
+        self.full, self.sems, self.depth = full, sems, depth
+        self.me, self.z, _, self.other = place()
+
+    def copy(self, direction, hops, arrival=False):
+        block = self.full.at[self.z - hops if direction == 0 else self.z + hops]
+        target = self.me + 2 if direction == 0 else self.me - 2
+        return seq_copy(
+            block,
+            block,
+            self.sems.at[0, direction, hops],
+            self.sems.at[1, direction, hops if arrival else hops + 1],
+            self.other if arrival else target,
+        )
+
+    def hop(self, hops):
+        for direction in (0, 1):
+
+            @pl.when(in_line(direction, self.z, hops, self.depth))
+            def _():
+                if hops:
+                    self.copy(direction, hops, True).wait_recv()
+
+                @pl.when(in_line(1 - direction, self.z, 1, self.depth))
+                def _():
+                    self.copy(direction, hops).start()
+
+    def drain(self):
+        for hops in range(self.depth):
+            for direction in (0, 1):
+                here = in_line(direction, self.z, hops, self.depth)
+
+                @pl.when(here & in_line(1 - direction, self.z, 1, self.depth))
+                def _():
+                    self.copy(direction, hops).wait_send()
+
+
 class Reshard:
     def __init__(self, shards, part, out, local_sem, sems):
         x, core, core_peer, x_peer = group_place()
@@ -1002,9 +1040,13 @@
             whole = out.at[:, side * 2 + core]
             self.third.append(grp_copy(whole, whole, *pair(shards + side), core_peer))
 
-    def begin(self):
+    def begin_near(self):
         self.local.start()
-        for copy in self.first:
+        for copy in self.first[1::2]:
+            copy.start()
+
+    def begin_far(self):
+        for copy in self.first[0::2]:
             copy.start()
 
     def share(self):
@@ -1221,12 +1263,15 @@
     return finish
 
 
-VEC_STEP = 256
-VEC_TAIL = 8 * VEC_STEP
-
-
-def column_of(row):
-    return jnp.broadcast_to(row, (8, row.shape[1])).T[:, 0:1]
+def row_of(vector):
+    return vector[...].astype(jnp.float32).reshape(1, vector.shape[0])
+
+
+def column_of(vector):
+    row = row_of(vector)
+    fill = -row.shape[1] % 128
+    row = jnp.concatenate([row, jnp.zeros((1, fill), jnp.float32)], axis=1)
+    return jnp.broadcast_to(row, (8, row.shape[1])).T[: vector.shape[0], 0:1]
 
 
 def stats_of(values_in):
@@ -1288,7 +1333,12 @@
     cond,
     time_weight,
     conv_weight,
-    vec,
+    conv_bias,
+    fc1_bias,
+    gamma,
+    beta,
+    fc2_bias,
+    time_bias,
     fc1,
     ctx_cols,
     cot,
@@ -1305,9 +1355,9 @@
     denom_out,
     response,
     ctx_full,
-    cot_full,
+    d_mixed,
+    cot_cols,
     fc2_rows,
-    out_rows,
     pack,
     packed,
     floats,
@@ -1323,6 +1373,10 @@
     ctx_sems,
     cot_sems,
     out_parts,
+    out_rows,
+    cot_line,
+    to_other,
+    other_sems,
     local_sems,
     fc2_sems,
     out_sems,
@@ -1333,27 +1387,24 @@
     me = lax.axis_index("seq")
     meet_all(shards, lax.axis_size("grp"))
     units, width = fc2_rows.shape[2:]
-    out_units = out_parts.shape[2]
+    out_units = out_parts.shape[3]
 
     def fc2_part(goal, quarter):
         here = pl.ds(pl.multiple_of(quarter * units, units), units)
         return fc2.at[here, pl.ds(pl.multiple_of(goal * width, 128), width)]
 
     def out_part(goal, quarter):
-        low = (goal * 4 + quarter) * out_units
-        return out_weight.at[pl.ds(pl.multiple_of(low, out_units), out_units)]
+        return out_weight.at[pl.ds(goal // 2 * 2, 2), quarter]
 
     fc2_shard = Reshard(shards, fc2_part, fc2_rows, local_sems.at[0], fc2_sems)
     out_shard = Reshard(shards, out_part, out_parts, local_sems.at[1], out_sems)
     ctx_gather = Gather(ctx_full, ctx_sems, depth)
-    cot_gather = Gather(cot_full, cot_sems, depth, rows // 8)
+    _, z, y, other = place()
+    cot_gather = LineGather(cot_line, cot_sems, depth)
     ctx_full[me] = ctx_cols[...]
     latents = Latents(shape, shards * rows)
     cols = pack.shape[1]
-    width_one = response.shape[2]
-    fc1_bias, gamma, beta = (vec[:, n * width_one : (n + 1) * width_one] for n in range(3))
-    vec_at = lambda n: vec[:, 3 * width_one + n * VEC_STEP : 3 * width_one + n * VEC_STEP + cols]
-    time_bias = vec[:, 3 * width_one + 6 * VEC_STEP : 3 * width_one + 6 * VEC_STEP + 2 * cols]
+    fc1_bias, gamma, beta, time_bias = map(row_of, (fc1_bias, gamma, beta, time_bias))
     mod = (
         jnp.dot(
             cond[...],
@@ -1365,8 +1416,8 @@
     )
     pack[...] = jnp.zeros_like(pack)
     pack[0:9, :] = conv_weight[...].astype(f32)
-    pack[9:10, :] = vec_at(0)
-    pack[10:11, :] = vec_at(1)
+    pack[9:10, :] = row_of(conv_bias)
+    pack[10:11, :] = row_of(fc2_bias)
     pack[11 : 11 + NLAT, :] = mod[:, :cols]
     pack[11 + NLAT : 11 + 2 * NLAT, :] = mod[:, cols:]
     packed[me] = pack[...]
@@ -1384,12 +1435,14 @@
     finish = exchange_edges(held, edge_sems, rows, shards)
     for copy in pack_copies:
         copy.start()
+    fc2_shard.begin_near()
+    out_shard.begin_near()
     finish()
-    fc2_shard.begin()
-    out_shard.begin()
+    fc2_shard.begin_far()
+    out_shard.begin_far()
     ctx_gather.start()
-    cot_full[me] = cot.wait()[...]
-    cot_gather.start()
+    cot_line[z] = cot.wait()[...]
+    cot_gather.hop(0)
     emit(held)
     tile_loop(
         floats.shape[0] // 32,
@@ -1464,23 +1517,66 @@
             fc2_shard.share()
             out_shard.share()
             ctx_gather.hop(2)
-            cot_gather.cross()
             cot_gather.hop(1)
 
         @pl.when(hops == 3)
         def _():
             ctx_gather.hop(3)
+            cot_gather.hop(2)
 
     Gather(full, gather_sems, depth, rows // 8).run(visit, hook)
     emit(full, pre)
-    cot_gather.hop(2)
+    out_shard.share_core()
     fc2_shard.share_core()
-    out_shard.share_core()
     root = jnp.sqrt(energy[...] + 1.0)
     mine[...] = jnp.broadcast_to(jnp.sum(root, axis=1, keepdims=True), mine.shape)
-    denom = peer_total(mine, theirs, total_sems, shards) / FF + EPS_NORM
+
+    other_copies = [
+        seq_copy(
+            to_other.at[n],
+            target.at[:, y],
+            other_sems.at[0, n],
+            other_sems.at[1, n],
+            other,
+        )
+        for n, target in enumerate((d_mixed, cot_cols))
+    ]
+    wide_cols = 2 * cols
+
+    def cot_part(block):
+        rows_here = cot_line[block]
+        pair = cot_line[block, :, pl.ds(pl.multiple_of(z * wide_cols, 128), wide_cols)]
+        for side in (0, 1):
+            taken = pair[:, side * cols : (side + 1) * cols]
+            product = dot_nt(rows_here, out_rows[side]).astype(d_mixed.dtype)
+
+            @pl.when(y == side)
+            def _():
+                d_mixed[block, side] = product
+                cot_cols[block, side] = taken
+
+            @pl.when(y != side)
+            def _():
+                to_other[0, block] = product
+                to_other[1, block] = taken
+
+    def meanwhile():
+        cot_gather.hop(3)
+        out_shard.finish()
+        for quarter in range(4):
+            for side in (0, 1):
+                side_by_side(
+                    out_rows.at[side],
+                    quarter * out_units,
+                    lambda j, quarter=quarter, side=side: out_parts[j, quarter, side],
+                    shards,
+                )
+        tile_loop(depth, cot_part)
+        for copy in other_copies:
+            copy.start()
+
+    denom = peer_total(mine, theirs, total_sems, shards, meanwhile) / FF + EPS_NORM
     ratio = root / denom[:, 0:1]
-    cot_gather.hop(3)
     root_out[...] = root
     denom_out[...] = denom
     ratio_out[...] = ratio
@@ -1499,12 +1595,9 @@
     emit(ctx_full)
     fc2_shard.finish()
     emit(fc2_rows)
-    out_shard.finish()
-    for quarter in range(4):
-        side_by_side(
-            out_rows, quarter * out_units, lambda j, quarter=quarter: out_parts[j, quarter], shards
-        )
-    cot_gather.finish()
+    cot_gather.drain()
+    for copy in other_copies:
+        copy.wait()
 
 
 def mixed_in_kernel(
@@ -1516,7 +1609,8 @@
     hidden,
     wide,
     w_qkv,
-    vec,
+    q_bias,
+    v_bias,
     context,
     full,
     first,
@@ -1542,9 +1636,7 @@
     meet_all(shards)
     latents = Latents(shape, shards * rows)
     cols = keys.shape[0]
-    base = vec.shape[1] - VEC_TAIL
-    q_bias = vec[:, base + 2 * VEC_STEP : base + 2 * VEC_STEP + cols]
-    v_bias = column_of(vec[:, base + 3 * VEC_STEP : base + 4 * VEC_STEP])[:cols]
+    q_bias, v_bias = row_of(q_bias), column_of(v_bias)
     bias = wide[10:11, :]
     scale, shift = wide[WIDE_SCALE : WIDE_SCALE + 8, :], wide[WIDE_SHIFT : WIDE_SHIFT + 8, :]
 
@@ -1594,8 +1686,8 @@
     queries,
     keys,
     values,
+    d_mixed_all,
     cot,
-    out_rows,
     d_qkv,
     mixed,
     cot_cols,
@@ -1630,14 +1722,8 @@
         blocks = pl.ds(tile * span, span)
         here = pl.ds(pl.multiple_of(tile * tile_rows, 128), tile_rows)
         query = queries[blocks].reshape(tile_rows, cols) * SCORE_SCALE
-        cot_tile = cot[blocks].reshape(tile_rows, C)
-        for j in range(shards):
-
-            @pl.when(me == j)
-            def _():
-                cot_cols[:, here] = cot_tile[:, j * cols : (j + 1) * cols].T
-
-        d_mixed = dot_nt(cot_tile, out_rows[...]).astype(bf16)
+        cot_cols[:, here] = cot[blocks].reshape(tile_rows, cols).T
+        d_mixed = d_mixed_all[blocks].reshape(tile_rows, cols)
         q_segment = latents.segment(
             tile * tile_rows + lax.broadcasted_iota(jnp.int32, (tile_rows, 1), 0)
         )
@@ -1708,7 +1794,8 @@
     mixed,
     cot_cols,
     out_weight,
-    vec,
+    gamma,
+    out_bias,
     cot,
     normed,
     inverse,
@@ -1721,7 +1808,6 @@
     denom,
     response,
     context_in,
-    full,
     d_first,
     d_pre,
     small_out,
@@ -1729,6 +1815,8 @@
     map_grad,
     act_out,
     fc2_half,
+    branch_sum,
+    full,
     d_mod,
     small,
     acc,
@@ -1766,10 +1854,8 @@
     cols = ctx_out.shape[1]
     total = shards * rows
     latents = Latents(shape, total)
-    base = vec.shape[1] - VEC_TAIL
-    width_one = base // 3
-    gamma = vec[:, width_one : 2 * width_one]
-    out_bias = column_of(vec[:, base + 4 * VEC_STEP : base + 5 * VEC_STEP])[:cols]
+    gamma, out_bias = row_of(gamma), column_of(out_bias)
+    width_one = gamma.shape[1]
     scale = wide[WIDE_SCALE : WIDE_SCALE + 8, :]
     later = (attn, context, mixed, cot_cols, out_weight)
     weight_sum = PairSum(g_own, g_got, g_other, weight_grads, g_sems)
@@ -1816,6 +1902,7 @@
         partial, to_y, from_y, to_z, from_z, acc, y_sems, z_sems, depth, between, scatter_hook
     )
     d_mod[...] = jnp.zeros_like(d_mod)
+    branch_sum[...] = jnp.zeros_like(branch_sum)
     cot, normed, first = cot.wait(), normed.wait(), first.wait()
 
     def norm_tile(index):
@@ -1826,7 +1913,9 @@
         pick = latents.picks(me * rows + index * 16, 16)
         value = d_second * (1.0 + rows_of(pick, scale))
         d_first[here, :] = value
-        full[me, here, :] = value.astype(full.dtype)
+        value = value.astype(full.dtype)
+        full[me, here, :] = value
+        branch_sum[0:1, :] += jnp.sum(value.astype(f32), axis=0, keepdims=True)
         scaled = d_second * first[here, :]
         for latent in range(NLAT):
             chosen = pick[latent]
@@ -1881,7 +1970,6 @@
         tile_loop(rows // 32, tile)
 
     Gather(full, gather_sems, depth, rows // 8).run(visit, gather_hook)
-    emit(full)
     small[...] = jnp.zeros_like(small)
     wide_row = 2 * cols
 
@@ -2142,7 +2230,7 @@
         cols = pl.ds(pl.multiple_of(index * 256, 256), 256)
         d_conv = held[pl.ds(EDGE, rows), cols].astype(f32)
         d_conv_params[9:10, cols] = jnp.sum(d_conv, axis=0, keepdims=True)
-        d_conv_params[10:11, cols] = jnp.sum(branch[:, cols].astype(f32), axis=0, keepdims=True)
+        d_conv_params[10:11, cols] = branch[0:1, cols]
         for tap in range(9):
             offset = EDGE + (tap // 3 - 1) * WMAX + tap % 3 - 1
             d_conv_params[tap : tap + 1, cols] = jnp.sum(
@@ -2364,19 +2452,7 @@
     cols = C // shards
     depth = shards // 2
     hidden_cols = FF // shards
-    me = lax.axis_index("seq")
     shape = latent_shape[0]
-    slot = lambda item: jnp.pad(item, (0, VEC_STEP - item.shape[0]))
-    vec = jnp.concatenate(
-        [
-            fc1_bias,
-            grn_gamma,
-            grn_beta,
-            *(slot(item) for item in (conv_bias, fc2_bias, query_bias, value_bias, out_bias)),
-            slot(map_bias),
-            jnp.pad(time_bias, (0, 2 * VEC_STEP - time_bias.shape[0])),
-        ]
-    ).astype(f32)[None]
     w_qkv = jnp.concatenate([query_weight.T, key_weight.T, value_weight.T], axis=0)
     ctx_rows = 256
     context_in = jax.nn.silu(clip.reshape(NLAT * NCTX, CLIP).astype(f32)).astype(bf16)
@@ -2397,9 +2473,9 @@
         denom,
         response,
         context,
-        cot_full,
+        d_mixed,
+        cot_blocks,
         shrink_parts,
-        output_rows,
     ) = kernel_call(
         functools.partial(mixer_kernel, shards),
         "mixer",
@@ -2416,9 +2492,9 @@
             ((8, 128), f32),
             ((shards, rows, hidden_cols), bf16),
             ((shards, cols, ctx_rows), bf16),
-            ((shards, rows, C), bf16),
+            ((depth, 2, rows, cols), bf16),
+            ((depth, 2, rows, cols), bf16),
             ((shards, 4, units, hidden_cols), bf16),
-            ((cols, C), bf16),
         ],
         [
             vmem((24, cols), f32),
@@ -2433,8 +2509,12 @@
             gather_scratch(depth),
             total_sems,
             gather_scratch(depth),
-            gather_scratch(depth),
-            vmem((shards, 4, units, cols), bf16),
+            pltpu.SemaphoreType.DMA((2, 2, depth + 1)),
+            vmem((shards, 4, 2, units, cols), bf16),
+            vmem((2, cols, C), bf16),
+            vmem((depth, rows, C), bf16),
+            vmem((2, depth, rows, cols), bf16),
+            pltpu.SemaphoreType.DMA((2, 2)),
             pltpu.SemaphoreType.DMA((2,)),
             pltpu.SemaphoreType.DMA((2, shards + 2)),
             pltpu.SemaphoreType.DMA((2, shards + 2)),
@@ -2445,18 +2525,23 @@
             cond_r,
             time_weight,
             conv_weight,
-            vec,
+            conv_bias,
+            fc1_bias,
+            grn_gamma,
+            grn_beta,
+            fc2_bias,
+            time_bias,
             fc1_weight,
             ctx_cols,
             cotangent,
             fc2_weight.T,
-            out_weight,
+            out_weight.reshape(shards, 4, units, cols),
         ),
         flops=2 * total * C * hidden_cols,
-        far=(9, 10),
+        far=(14, 15),
         scalars=(0,),
-        late=(6, 8),
-        staged=(0, 1, 2, 3, 5, 9, 10, 11, 12),
+        late=(11, 13),
+        staged=(0, 1, 2, 3, 5, 9, 10, 13),
     )
     context = context.reshape(C, ctx_rows)
     shrink_rows = shrink_parts.reshape(C, hidden_cols)
@@ -2492,12 +2577,13 @@
             hidden,
             wide,
             w_qkv,
-            vec,
+            query_bias,
+            value_bias,
             context,
         ),
         flops=2 * total * C * (hidden_cols + 3 * cols),
         scalars=(0,),
-        late=(3, 5, 7),
+        late=(3, 5, 8),
         staged=(0, 1, 2, 3, 5, 6, 7),
     )
 
@@ -2522,14 +2608,13 @@
             queries,
             keys,
             values,
-            cot_full,
-            output_rows,
+            d_mixed.reshape(shards, rows, cols),
+            cot_blocks.reshape(shards, rows, cols),
         ),
         flops=12 * total * keys_all * 3 * 256,
         scalars=(0,),
     )
     (
-        branch_blocks,
         d_first,
         d_pre,
         small,
@@ -2537,12 +2622,12 @@
         grad_map_w,
         act_cols,
         fc2_half,
+        branch_sum,
     ) = kernel_call(
         functools.partial(attn_back_kernel, shards),
         "attn_back",
         3,
         [
-            ((shards, rows, C), bf16),
             ((rows, C), f32),
             ((shards, rows, hidden_cols), bf16),
             ((SMALL_ROWS, 2 * cols), bf16),
@@ -2550,8 +2635,10 @@
             ((cols, CLIP), bf16),
             ((cols, total), bf16),
             ((shards, 2, units, hidden_cols), bf16),
+            ((8, C), f32),
         ],
         [
+            vmem((shards, rows, C), bf16),
             vmem((8, C), f32),
             vmem((SMALL_ROWS, 2 * cols), f32),
             pltpu.VMEM((rows, C), f32),
@@ -2585,7 +2672,8 @@
             mixed_full,
             cot_cols,
             out_weight.T,
-            vec,
+            grn_gamma,
+            out_bias,
             cotangent,
             normed_two,
             inverse_two,
@@ -2601,11 +2689,10 @@
         ),
         flops=2 * total * C * (hidden_cols + 6 * cols),
         scalars=(0,),
-        late=(4, 5, 6, 7, 8, 10, 11, 13, 15, 16, 20, 21),
-        staged=(0, 1, 2, 4, 6, 7),
+        late=(4, 5, 6, 7, 8, 11, 12, 14, 16, 17, 21, 22),
+        staged=(0, 1, 3, 5, 6),
     )
     groups = lax.axis_size("grp")
-    branch_own = lax.dynamic_index_in_dim(branch_blocks, me, 0, keepdims=False)
     input_grad, fc1_sum, fc2_sum, map_sum, small, conv_small, activations = kernel_call(
         functools.partial(conv_back_kernel, shards),
         "conv_back",
@@ -2656,7 +2743,7 @@
             held,
             wide,
             normed_full,
-            branch_own,
+            branch_sum,
             grad_map_w,
             act_cols,
             second_sum,

time: 477 us -> 470 us (0.985); the launches traced: 470 us -> 471 us
  local copies, waits for them, and re-layouts: 19.1 us -> 13.7 us
  Pallas kernels: 436 us -> 441 us
where the time goes in v4:
time: 470 us; the launch traced here: 471 us
  Pallas kernels  441 us (94%)
  other arithmetic  13.9 us (3%)
  local copies, waits for them, and re-layouts  13.7 us (3%)
    pallas_call x5, Pallas kernels, kernel_call(): pl.pallas_call(staged_body(body, len(operands), len(outs), late, staged),...  441 us

profile of v4, /device:TPU:9, one launch (start us, length us, event | category | flops | bytes accessed | tf_op | source)
XLA Modules:
  0.0 470.8 jit_solution(3240714581653168898)
XLA Ops:
  0.7 0.0 copy-start
  0.7 0.7 convert_element_type.31
  1.4 1.3 copy.50.refs_0_
  2.8 2.2 copy.45
  5.0 0.1 reshape.78
  5.1 0.0 copy-start.6
  5.1 0.0 copy-start.7
  5.1 0.0 copy-start.8
  5.2 0.3 multiply_convert_fusion
  5.5 1.0 fusion.1.refs_12_
  6.5 0.9 pad.4.refs_22_
  7.4 1.3 pad_maximum_fusion.refs_5_.refs_3_
  8.7 111.6 %mixer.1 = (bf16[8,128,1536]{2,1,0:T(8,128)(2,1)}, bf16[288,1536]{1,0:T(8,128)(2,1)}, f32[32,1536]{1,0:T(8,128)}, f32[128,1536]{1,0:T(8,128)}, f32[128,1]{1,0:T(...) custom-call(s32[3,2]{1,0:T(4,128)} %copy.50.refs_0_, ...), custom_call_target="tpu_custom_call" | custom-call | flops 2415919104 | bytes 19970712 | tf_op jit(solution)/shard_map/mixer/pallas_call | solution.py:2385
  120.3 89.2 %mixed_in.1 = (bf16[8,128,1536]{2,1,0:T(8,128)(2,1)}, f32[128,1536]{1,0:T(8,128)}, f32[128,1536]{1,0:T(8,128)}, f32[128,1536]{1,0:T(8,128)}, f32[128,1]{1,0:T(8,...) custom-call(s32[3,2]{1,0:T(4,128)} %copy.50.refs_0_, ...), custom_call_target="tpu_custom_call" | custom-call | flops 4227858432 | bytes 13960472 | tf_op jit(solution)/shard_map/mixed_in/pallas_call | solution.py:2385
  209.5 47.1 %attend.1 = (bf16[576,1280]{1,0:T(8,128)(2,1)}, bf16[4,8,192,256]{3,2,1,0:T(8,128)(2,1)}, bf16[192,1024]{1,0:T(8,128)(2,1)}) custom-call(s32[3,2]{1,0:T(4,128)} %copy.50.refs_0_, bf16[8,128,192]{2,1,0:T(8,128)(2,1)} %get-tuple-element.65.refs_1_, bf16[192,1280]{1,0:T(8,128)(2,1)} %get-tuple-element.66.refs_2_, bf16[192,1280]{1,0:T(8,128)(2,1)} %get-tuple-element.67.refs_3_, ...), custom_call_target="tpu_custom_call" | custom-call | flops 12079595520 | bytes 7176216 | tf_op jit(solution)/shard_map/attend/pallas_call | solution.py:2385
  256.6 97.3 %attn_back.1 = (f32[128,1536]{1,0:T(8,128)}, bf16[8,128,768]{2,1,0:T(8,128)(2,1)}, bf16[80,384]{1,0:T(8,128)(2,1)}, bf16[768,1536]{1,0:T(8,128)(2,1)}, bf16[192,...) custom-call(s32[3,2]{1,0:T(4,128)} %copy.50.refs_0_, ...), custom_call_target="tpu_custom_call" | custom-call | flops 6039797760 | bytes 28150936 | tf_op jit(solution)/shard_map/attn_back/pallas_call | solution.py:2385
  353.9 95.8 %conv_back.1 = (f32[128,1536]{1,0:T(8,128)}, bf16[1536,768]{1,0:T(8,128)(2,1)}, bf16[192,6144]{1,0:T(8,128)(2,1)}, bf16[192,1280]{1,0:T(8,128)(2,1)}, f32[80,384...) custom-call(s32[3,2]{1,0:T(4,128)} %copy.50.refs_0_, bf16[8,128,768]{2,1,0:T(8,128)(2,1)} %get-tuple-element.81.refs_1_, ...), custom_call_target="tpu_custom_call" | custom-call | flops 7247757312 | bytes 19218968 | tf_op jit(solution)/shard_map/conv_back/pallas_call | solution.py:2385
  449.7 1.3 slice_reduce_fusion
  451.0 1.4 fusion.3
  452.4 0.8 fusion.4
  453.2 1.5 slice.54
  454.7 0.6 reshape.77
  455.3 0.6 reshape.76
  455.9 0.6 reshape.75
  456.5 2.0 convert_bitcast_fusion.5
  458.6 4.4 convert_element_type.34
  462.9 0.0 copy-done.3
  462.9 2.7 convert_bitcast_fusion
  465.7 2.4 convert_bitcast_fusion.1
  468.1 0.7 copy.54
  468.8 0.9 copy.55
  469.7 0.6 copy.56
  (17 shorter events, 0.0 us)
Async XLA Ops:
  0.7 4.8 %copy-start = (bf16[1280,192]{0,1:T(8,128)(2,1)S(1)}, bf16[1280,192]{0,1:T(8,128)(2,1)}, u32[]{:S(2)}) copy-start(bf16[1280,192]{0,1:T(8,128)(2,1)} %param.39) | copy-start | bytes 1474564
  0.7 4.3 copy-start.5
  5.1 2.3 copy-start.6
  5.1 2.3 copy-start.7
  5.1 2.3 copy-start.8
  458.6 4.4 copy-start.3
  462.9 2.7 copy-start.2
  465.7 2.4 copy-start.9
  465.7 3.2 copy-start.4
  465.7 4.6 copy-start.1
  468.1 1.6 copy-start.10

commit v5 on v4

--- a/solution.py
+++ b/solution.py
@@ -1067,13 +1067,6 @@
             copy.wait_send()
 
 
-def side_by_side(target, row, parts, count):
-    for pair in range(count // 2):
-        value = jnp.concatenate([parts(2 * pair), parts(2 * pair + 1)], axis=1)
-        rows, cols = value.shape
-        target[row : row + rows, pair * cols : (pair + 1) * cols] = value
-
-
 def scatter_blocks(
     partial, to_y, from_y, to_z, from_z, acc, y_sems, z_sems, depth, between=None, hook=None, early=None
 ):
@@ -1373,7 +1366,6 @@
     ctx_sems,
     cot_sems,
     out_parts,
-    out_rows,
     cot_line,
     to_other,
     other_sems,
@@ -1387,14 +1379,15 @@
     me = lax.axis_index("seq")
     meet_all(shards, lax.axis_size("grp"))
     units, width = fc2_rows.shape[2:]
-    out_units = out_parts.shape[3]
+    out_units, wide_cols = out_parts.shape[2:]
 
     def fc2_part(goal, quarter):
         here = pl.ds(pl.multiple_of(quarter * units, units), units)
         return fc2.at[here, pl.ds(pl.multiple_of(goal * width, 128), width)]
 
     def out_part(goal, quarter):
-        return out_weight.at[pl.ds(goal // 2 * 2, 2), quarter]
+        here = pl.ds(pl.multiple_of(quarter * out_units, out_units), out_units)
+        return out_weight.at[here, pl.ds(pl.multiple_of(goal // 2 * wide_cols, 128), wide_cols)]
 
     fc2_shard = Reshard(shards, fc2_part, fc2_rows, local_sems.at[0], fc2_sems)
     out_shard = Reshard(shards, out_part, out_parts, local_sems.at[1], out_sems)
@@ -1541,14 +1534,15 @@
         )
         for n, target in enumerate((d_mixed, cot_cols))
     ]
-    wide_cols = 2 * cols
 
     def cot_part(block):
-        rows_here = cot_line[block]
+        products = jnp.dot(
+            cot_line[block], out_parts[...].reshape(C, wide_cols), preferred_element_type=f32
+        ).astype(d_mixed.dtype)
         pair = cot_line[block, :, pl.ds(pl.multiple_of(z * wide_cols, 128), wide_cols)]
         for side in (0, 1):
             taken = pair[:, side * cols : (side + 1) * cols]
-            product = dot_nt(rows_here, out_rows[side]).astype(d_mixed.dtype)
+            product = products[:, side * cols : (side + 1) * cols]
 
             @pl.when(y == side)
             def _():
@@ -1563,14 +1557,6 @@
     def meanwhile():
         cot_gather.hop(3)
         out_shard.finish()
-        for quarter in range(4):
-            for side in (0, 1):
-                side_by_side(
-                    out_rows.at[side],
-                    quarter * out_units,
-                    lambda j, quarter=quarter, side=side: out_parts[j, quarter, side],
-                    shards,
-                )
         tile_loop(depth, cot_part)
         for copy in other_copies:
             copy.start()
@@ -2510,8 +2496,7 @@
             total_sems,
             gather_scratch(depth),
             pltpu.SemaphoreType.DMA((2, 2, depth + 1)),
-            vmem((shards, 4, 2, units, cols), bf16),
-            vmem((2, cols, C), bf16),
+            vmem((shards, 4, units, 2 * cols), bf16),
             vmem((depth, rows, C), bf16),
             vmem((2, depth, rows, cols), bf16),
             pltpu.SemaphoreType.DMA((2, 2)),
@@ -2535,7 +2520,7 @@
             ctx_cols,
             cotangent,
             fc2_weight.T,
-            out_weight.reshape(shards, 4, units, cols),
+            out_weight.T,
         ),
         flops=2 * total * C * hidden_cols,
         far=(14, 15),

time: 470 us -> 465 us (0.989)
  Pallas kernels: 441 us -> 436 us
    pallas_call x5, Pallas kernels: 441 us -> 436 us  [kernel_call(): pl.pallas_call(staged_body(body, len(operands), len(outs), late, staged),...]
where the time goes in v5:
time: 465 us; the launch traced here: 464 us
  Pallas kernels  436 us (94%)
  other arithmetic  13.9 us (3%)
  local copies, waits for them, and re-layouts  12.6 us (3%)
    pallas_call x5, Pallas kernels, kernel_call(): pl.pallas_call(staged_body(body, len(operands), len(outs), late, staged),...  436 us

profile of v5, /device:TPU:9, one launch (start us, length us, event | category | flops | bytes accessed | tf_op | source)
XLA Modules:
  0.0 464.3 jit_solution(8270500238816128805)
XLA Ops:
  0.7 0.0 copy-start
  0.7 0.7 convert_element_type.31
  1.4 1.3 copy.49.refs_0_
  2.7 1.2 reshape.74
  3.9 0.0 copy-start.5
  3.9 0.0 copy-start.6
  3.9 0.0 copy-start.7
  4.0 0.3 multiply_convert_fusion
  4.3 1.0 fusion.1.refs_12_
  5.3 0.9 pad.4.refs_22_
  6.2 0.0 copy-done.5
  6.2 0.0 copy-done.7
  6.2 1.3 pad_maximum_fusion.refs_5_.refs_3_
  7.5 104.6 %mixer.1 = (bf16[8,128,1536]{2,1,0:T(8,128)(2,1)}, bf16[288,1536]{1,0:T(8,128)(2,1)}, f32[32,1536]{1,0:T(8,128)}, f32[128,1536]{1,0:T(8,128)}, f32[128,1]{1,0:T(...) custom-call(s32[3,2]{1,0:T(4,128)} %copy.49.refs_0_, ...), custom_call_target="tpu_custom_call" | custom-call | flops 2415919104 | bytes 19970712 | tf_op jit(solution)/shard_map/mixer/pallas_call | solution.py:2371
  112.1 86.6 %mixed_in.1 = (bf16[8,128,1536]{2,1,0:T(8,128)(2,1)}, f32[128,1536]{1,0:T(8,128)}, f32[128,1536]{1,0:T(8,128)}, f32[128,1536]{1,0:T(8,128)}, f32[128,1]{1,0:T(8,...) custom-call(s32[3,2]{1,0:T(4,128)} %copy.49.refs_0_, ...), custom_call_target="tpu_custom_call" | custom-call | flops 4227858432 | bytes 13960472 | tf_op jit(solution)/shard_map/mixed_in/pallas_call | solution.py:2371
  198.7 49.5 %attend.1 = (bf16[576,1280]{1,0:T(8,128)(2,1)}, bf16[4,8,192,256]{3,2,1,0:T(8,128)(2,1)}, bf16[192,1024]{1,0:T(8,128)(2,1)}) custom-call(s32[3,2]{1,0:T(4,128)} %copy.49.refs_0_, bf16[8,128,192]{2,1,0:T(8,128)(2,1)} %get-tuple-element.65.refs_1_, bf16[192,1280]{1,0:T(8,128)(2,1)} %get-tuple-element.66.refs_2_, bf16[192,1280]{1,0:T(8,128)(2,1)} %get-tuple-element.67.refs_3_, ...), custom_call_target="tpu_custom_call" | custom-call | flops 12079595520 | bytes 7176216 | tf_op jit(solution)/shard_map/attend/pallas_call | solution.py:2371
  248.2 98.7 %attn_back.1 = (f32[128,1536]{1,0:T(8,128)}, bf16[8,128,768]{2,1,0:T(8,128)(2,1)}, bf16[80,384]{1,0:T(8,128)(2,1)}, bf16[768,1536]{1,0:T(8,128)(2,1)}, bf16[192,...) custom-call(s32[3,2]{1,0:T(4,128)} %copy.49.refs_0_, ...), custom_call_target="tpu_custom_call" | custom-call | flops 6039797760 | bytes 28150936 | tf_op jit(solution)/shard_map/attn_back/pallas_call | solution.py:2371
  346.9 96.2 %conv_back.1 = (f32[128,1536]{1,0:T(8,128)}, bf16[1536,768]{1,0:T(8,128)(2,1)}, bf16[192,6144]{1,0:T(8,128)(2,1)}, bf16[192,1280]{1,0:T(8,128)(2,1)}, f32[80,384...) custom-call(s32[3,2]{1,0:T(4,128)} %copy.49.refs_0_, bf16[8,128,768]{2,1,0:T(8,128)(2,1)} %get-tuple-element.81.refs_1_, ...), custom_call_target="tpu_custom_call" | custom-call | flops 7247757312 | bytes 19218968 | tf_op jit(solution)/shard_map/conv_back/pallas_call | solution.py:2371
  443.2 1.3 slice_reduce_fusion
  444.5 1.4 fusion.3
  445.9 0.8 fusion.4
  446.7 1.5 slice.54
  448.3 0.6 reshape.73
  448.9 0.6 reshape.72
  449.5 0.6 reshape.71
  450.1 2.0 convert_bitcast_fusion.5
  452.1 4.4 convert_element_type.34
  456.5 2.7 convert_bitcast_fusion
  459.2 2.4 convert_bitcast_fusion.1
  461.6 0.7 copy.53
  462.3 0.9 copy.54
  463.2 0.6 copy.55
  (14 shorter events, 0.0 us)
Async XLA Ops:
  0.7 3.6 copy-start
  3.9 2.3 copy-start.5
  3.9 2.3 copy-start.6
  3.9 2.2 copy-start.7
  452.1 4.4 copy-start.3
  456.5 2.7 copy-start.2
  459.2 2.4 copy-start.8
  459.2 3.2 copy-start.4
  459.2 4.6 %copy-start.1 = (bf16[1280,192]{0,1:T(8,128)(2,1)S(1)}, bf16[1280,192]{0,1:T(8,128)(2,1)}, u32[]{:S(2)}) copy-start(bf16[1280,192]{0,1:T(8,128)(2,1)} %param.39) | copy-start | bytes 1474564
  461.6 1.6 copy-start.9

commit v6 on v5

--- a/solution.py
+++ b/solution.py
@@ -1280,7 +1280,7 @@
         self.ends = []
         low = 0
         for latent in range(NLAT - 1):
-            low = low + shape[latent, 0] * WMAX
+            low = low + shape[latent] * WMAX
             self.ends.append(low)
         self.total = total
 
@@ -2438,11 +2438,13 @@
     cols = C // shards
     depth = shards // 2
     hidden_cols = FF // shards
-    shape = latent_shape[0]
+    shape = latent_shape[0, :, 0]
     w_qkv = jnp.concatenate([query_weight.T, key_weight.T, value_weight.T], axis=0)
     ctx_rows = 256
-    context_in = jax.nn.silu(clip.reshape(NLAT * NCTX, CLIP).astype(f32)).astype(bf16)
-    context_in = jnp.pad(context_in, ((0, ctx_rows - NLAT * NCTX), (0, 0)))
+    context_in = jnp.pad(
+        clip.reshape(NLAT * NCTX, CLIP), ((0, ctx_rows - NLAT * NCTX), (0, 0))
+    )
+    context_in = jax.nn.silu(context_in.astype(f32)).astype(bf16)
     ctx_cols = (against(map_weight.T, context_in) + map_bias.astype(f32)[:, None]).astype(bf16)
     units = cols // 4
     vmem = pltpu.VMEM

time: 465 us -> 465 us (level)
  no operation moved by 1% of the time
where the time goes in v6:
time: 465 us; the launch traced here: 464 us
  Pallas kernels  436 us (94%)
  other arithmetic  13.8 us (3%)
  local copies, waits for them, and re-layouts  11.7 us (3%)
    pallas_call x5, Pallas kernels, kernel_call(): pl.pallas_call(staged_body(body, len(operands), len(outs), late, staged),...  436 us

profile of v6, /device:TPU:9, one launch (start us, length us, event | category | flops | bytes accessed | tf_op | source)
XLA Modules:
  0.0 463.5 jit_solution(6211182304398172023)
XLA Ops:
  0.7 0.0 copy-start
  0.7 1.2 slice_bitcast_fusion.refs_0_
  1.9 0.7 convert_element_type.27
  2.6 1.4 reshape.67
  3.9 0.3 fusion.3.refs_22_
  4.3 0.0 copy-done
  4.3 0.0 copy-start.2
  4.3 1.0 fusion.5.refs_12_
  5.3 0.0 copy-done.6
  5.4 0.0 copy-done.7
  5.4 0.0 copy-done.8
  5.4 1.3 pad_maximum_fusion.refs_5_.refs_3_
  6.7 104.6 %mixer.1 = (bf16[8,128,1536]{2,1,0:T(8,128)(2,1)}, bf16[288,1536]{1,0:T(8,128)(2,1)}, f32[32,1536]{1,0:T(8,128)}, f32[128,1536]{1,0:T(8,128)}, f32[128,1]{1,0:T(...) custom-call(s32[3]{0:T(128)} %slice_bitcast_fusion.refs_0_, ...), custom_call_target="tpu_custom_call" | custom-call | flops 2415919104 | bytes 19970700 | tf_op jit(solution)/shard_map/mixer/pallas_call | solution.py:2371
  111.3 86.6 %mixed_in.1 = (bf16[8,128,1536]{2,1,0:T(8,128)(2,1)}, f32[128,1536]{1,0:T(8,128)}, f32[128,1536]{1,0:T(8,128)}, f32[128,1536]{1,0:T(8,128)}, f32[128,1]{1,0:T(8,...) custom-call(s32[3]{0:T(128)} %slice_bitcast_fusion.refs_0_, ...), custom_call_target="tpu_custom_call" | custom-call | flops 4227858432 | bytes 13960460 | tf_op jit(solution)/shard_map/mixed_in/pallas_call | solution.py:2371
  198.0 49.4 %attend.1 = (bf16[576,1280]{1,0:T(8,128)(2,1)}, bf16[4,8,192,256]{3,2,1,0:T(8,128)(2,1)}, bf16[192,1024]{1,0:T(8,128)(2,1)}) custom-call(s32[3]{0:T(128)} %slice_bitcast_fusion.refs_0_, bf16[8,128,192]{2,1,0:T(8,128)(2,1)} %get-tuple-element.65.refs_1_, bf16[192,1280]{1,0:T(8,128)(2,1)} %get-tuple-element.66.refs_2_, ...), custom_call_target="tpu_custom_call" | custom-call | flops 12079595520 | bytes 7176204 | tf_op jit(solution)/shard_map/attend/pallas_call | solution.py:2371
  247.4 98.8 %attn_back.1 = (f32[128,1536]{1,0:T(8,128)}, bf16[8,128,768]{2,1,0:T(8,128)(2,1)}, bf16[80,384]{1,0:T(8,128)(2,1)}, bf16[768,1536]{1,0:T(8,128)(2,1)}, bf16[192,...) custom-call(s32[3]{0:T(128)} %slice_bitcast_fusion.refs_0_, ...), custom_call_target="tpu_custom_call" | custom-call | flops 6039797760 | bytes 28150924 | tf_op jit(solution)/shard_map/attn_back/pallas_call | solution.py:2371
  346.1 96.3 %conv_back.1 = (f32[128,1536]{1,0:T(8,128)}, bf16[1536,768]{1,0:T(8,128)(2,1)}, bf16[192,6144]{1,0:T(8,128)(2,1)}, bf16[192,1280]{1,0:T(8,128)(2,1)}, f32[80,384...) custom-call(s32[3]{0:T(128)} %slice_bitcast_fusion.refs_0_, ...), custom_call_target="tpu_custom_call" | custom-call | flops 7247757312 | bytes 19218956 | tf_op jit(solution)/shard_map/conv_back/pallas_call | solution.py:2371
  442.4 1.3 slice_reduce_fusion
  443.7 1.4 fusion.6
  445.1 0.8 fusion.7
  446.0 1.5 slice.58
  447.5 0.6 reshape.74
  448.1 0.6 reshape.73
  448.7 0.6 reshape.72
  449.3 2.0 convert_bitcast_fusion.5
  451.4 4.4 convert_element_type.30
  455.7 2.7 convert_bitcast_fusion
  458.4 2.4 convert_bitcast_fusion.1
  460.8 0.7 copy.48
  461.6 0.0 copy-done.5
  461.6 0.9 copy.49
  462.5 0.6 copy.50
  (15 shorter events, 0.0 us)
Async XLA Ops:
  0.7 3.6 copy-start
  2.6 2.8 copy-start.6
  2.6 2.8 copy-start.7
  2.6 2.8 copy-start.8
  4.3 2.4 copy-start.2
  451.3 4.4 copy-start.4
  455.7 2.7 copy-start.3
  458.4 2.4 copy-start.9
  458.4 3.2 copy-start.5
  458.4 4.6 %copy-start.1 = (bf16[1280,192]{0,1:T(8,128)(2,1)S(1)}, bf16[1280,192]{0,1:T(8,128)(2,1)}, u32[]{:S(2)}) copy-start(bf16[1280,192]{0,1:T(8,128)(2,1)} %param.39) | copy-start | bytes 1474564
  460.8 1.6 copy-start.10
